TPU v7x, 512 devices: a whole 4x8x8 slice. The times are simulated.
512 devices in a mesh: tile: 128 (over y, z, core), seg: 4 (over x).
Axes of the slice: x: 4, y: 8, z: 8, core: 2. Of those that a mesh axis runs over, the one named last changes fastest.
Arguments:
- coords: float32 [3, 524288], P(None, ('tile', 'seg')), may hold values from 8 to 16
- weights: float32 [524288], P(('tile', 'seg')), may hold values from 0.5 to 4
- mode_vectors: bfloat16 [256, 3, 524288], P(None, None, ('tile', 'seg')), may hold values from -0.375 to 0.375
- amplitudes: float32 [256], replicated, may hold values from -4 to 4
- density_map: bfloat16 [128, 32768], P('tile'), may hold values from 0 to 2
- block_tiles: int32 [16384, 4], P(('tile', 'seg')), may hold values from 0 to 127, all different within a row; in each aligned block of 32 rows (0 to 31, 32 to 63, ...) at most 2 rows name the same one
- block_offsets: int32 [16384, 4, 3], P(('tile', 'seg')), may hold values from 0 to 16
Outputs:
- forces: float32 [3, 524288], P(None, ('tile', 'seg'))
- mode_grad: float32 [256], replicated
- correlation: float32 [], replicated
Inputs may be any that keep to these rules, and one draw needn't show every extreme that they name: `block_tiles`: the 4 tiles of a row differ; among the 32 rows of one device no tile is named more than 2 times.
All inputs are finite; a program needn't handle non-finite values.
Results may differ from a plain program's by a relative error of at most 0.0044.
Values may be sent and summed in bfloat16 or wider, within the bound.
No kernel may reach another device: no remote copies, remote signals or barrier semaphores. Data moves between devices by JAX's collectives and lax.ppermute only.
A program may use at most 64 MiB of HBM per device.

v0:
```python
from functools import partial

import jax
import jax.numpy as jnp
from jax import lax
from jax.sharding import PartitionSpec as P

EDGE = 32
ATOM_BLOCK = 32


inverse_var = 1.0 / 2.25


def factors(frame_pos, edge_len):
    centers = jnp.arange(edge_len, dtype=jnp.float32) + 0.5
    distance = centers[None, :, None] - frame_pos[:, None, :]
    profile = jnp.exp(-0.5 * inverse_var * distance * distance)
    slopes = inverse_var * distance * profile
    return (profile, slopes)


def splat_tile(frame_pos, masses, edge_len):
    profile, slopes = factors(frame_pos, edge_len)
    rounded = profile.astype(jnp.bfloat16)
    along_y = (masses[None, :] * profile[1]).astype(jnp.bfloat16)
    plane_kr = (
        rounded[2].astype(jnp.float32)[:, None, :] * rounded[0].astype(jnp.float32)[None, :, :]
    ).astype(jnp.bfloat16)
    plane_kr = plane_kr.reshape(edge_len * edge_len, frame_pos.shape[1])
    return lax.dot_general(
        plane_kr, along_y, (((1,), (1,)), ((), ())), preferred_element_type=jnp.float32
    )


def backproject(frame_pos, masses, gradient, edge_len):
    profile, slopes = factors(frame_pos, edge_len)
    atom_count = frame_pos.shape[1]
    rounded = profile.astype(jnp.bfloat16)
    rounded_slopes = slopes.astype(jnp.bfloat16)
    y_factors = jnp.concatenate(
        [
            (masses[None, :] * profile[1]).astype(jnp.bfloat16),
            (masses[None, :] * slopes[1]).astype(jnp.bfloat16),
        ],
        axis=1,
    )
    contracted = jnp.dot(gradient, y_factors, preferred_element_type=jnp.float32).astype(
        jnp.bfloat16
    )
    contracted = (
        lax.optimization_barrier(contracted)
        .astype(jnp.float32)
        .reshape(edge_len, edge_len, 2 * atom_count)
    )
    plain_sum = contracted[:, :, :atom_count]
    sloped = contracted[:, :, atom_count:]
    along_x = rounded[0].astype(jnp.float32)
    along_z = rounded[2].astype(jnp.float32)
    slope_x = rounded_slopes[0].astype(jnp.float32)
    slope_z = rounded_slopes[2].astype(jnp.float32)
    force_x = jnp.sum(along_z * jnp.sum(plain_sum * slope_x[None], axis=1), axis=0)
    force_y = jnp.sum(along_z * jnp.sum(sloped * along_x[None], axis=1), axis=0)
    force_z = jnp.sum(slope_z * jnp.sum(plain_sum * along_x[None], axis=1), axis=0)
    return jnp.stack([force_x, force_y, force_z])


def gradient_of(density, target, totals, voxels):
    root = jnp.sqrt(totals[1] * totals[2])
    correlation = totals[0] / root
    return (voxels * (target / root - correlation * density / totals[1])).astype(jnp.bfloat16)


def ranks_of(tile_ids):
    entry_count = tile_ids.shape[0]
    ordinal = jnp.arange(entry_count, dtype=jnp.int32)
    before = (ordinal[None, :] < ordinal[:, None]) & (tile_ids[None, :] == tile_ids[:, None])
    return jnp.sum(before.astype(jnp.int32), axis=1)


def slot_sources(tile_ids, ranking, targets, most_slots):
    entry_count = tile_ids.shape[0]
    ordinal = jnp.arange(entry_count, dtype=jnp.int32) + 1
    levels = jnp.arange(most_slots, dtype=jnp.int32)
    matches = (tile_ids[None, None, :] == targets[:, None, None]) & (
        ranking[None, None, :] == levels[None, :, None]
    )
    return jnp.sum(jnp.where(matches, ordinal[None, None, :], 0), axis=2) - 1


def pack_slots(bundle, offsets_f, sources, atoms_per):
    block_count = bundle.shape[1] // atoms_per
    per_block = offsets_f.shape[0] // block_count
    filled = sources >= 0
    entry_ids = jnp.maximum(sources, 0)
    block_ids = entry_ids // per_block
    grouped_bundle = bundle.reshape(4, block_count, atoms_per)
    picked = jnp.take(grouped_bundle, block_ids, axis=1)
    offset_rows = jnp.take(offsets_f, entry_ids, axis=0)
    frame_part = picked[:3] + jnp.moveaxis(offset_rows, -1, 0)[..., None]
    mass_part = picked[3] * filled[..., None].astype(jnp.float32)
    joined = jnp.concatenate([frame_part, mass_part[None]], axis=0)
    return jnp.moveaxis(joined, 0, -2)


def on_device(coords, weights, mode_vectors, amplitudes, density_map, block_tiles, block_offsets):
    edge_len = EDGE
    atoms_per = ATOM_BLOCK
    a_dev = coords.shape[1]
    block_count = block_tiles.shape[0]
    per_block = block_tiles.shape[1]
    entry_count = block_count * per_block
    n_tile = lax.axis_size("tile")
    n_seg = lax.axis_size("seg")
    most_slots = max(2, 2 * entry_count // n_tile)
    my_tile = lax.axis_index("tile")
    modes_flat = mode_vectors.reshape(mode_vectors.shape[0], 3 * a_dev)
    displacement = jnp.dot(
        amplitudes.astype(jnp.bfloat16)[None, :], modes_flat, preferred_element_type=jnp.float32
    ).reshape(3, a_dev)
    bundle = jnp.concatenate([coords + displacement, weights[None, :]], axis=0)
    tile_ids = block_tiles.reshape(entry_count)
    offsets_f = block_offsets.reshape(entry_count, 3).astype(jnp.float32)
    entry_table = jnp.concatenate([tile_ids.astype(jnp.float32)[:, None], offsets_f], axis=1)
    every_bundle, every_table = (
        lax.all_gather(bundle, "tile", axis=1, tiled=True),
        lax.all_gather(entry_table, "tile", axis=0, tiled=True),
    )
    every_bundle = jnp.moveaxis(every_bundle.reshape(4, n_tile, a_dev), 1, 0)
    every_table = every_table.reshape(n_tile, entry_count, 4)
    every_tiles = every_table[:, :, 0].astype(jnp.int32)
    every_offsets = every_table[:, :, 1:]

    def sources_of(own_tiles):
        return slot_sources(own_tiles, ranks_of(own_tiles), my_tile[None], most_slots)[0]

    sources = jax.vmap(sources_of)(every_tiles)
    slot_rows = jax.vmap(partial(pack_slots, atoms_per=atoms_per))(
        every_bundle, every_offsets, sources
    )
    slot_count = n_tile * most_slots
    group_slots = min(slot_count, max(1, 1024 // atoms_per))
    groups = slot_count // group_slots
    grouped = jnp.transpose(
        slot_rows.reshape(groups, group_slots, 4, atoms_per), (0, 2, 1, 3)
    ).reshape(groups, 4, group_slots * atoms_per)

    def add_group(density, group_rows):
        return (density + splat_tile(group_rows[:3], group_rows[3], edge_len), None)

    partial_density, _ = lax.scan(
        add_group, jnp.zeros((edge_len * edge_len, edge_len), jnp.float32), grouped
    )
    target = density_map.reshape(edge_len * edge_len, edge_len).astype(jnp.float32)
    voxels = float(n_tile * edge_len**3)
    density = lax.psum(partial_density, "seg")
    totals = lax.psum(
        (jnp.sum(density * target), jnp.sum(density * density), jnp.sum(target * target)), "tile"
    )
    gradient = gradient_of(density, target, totals, voxels)
    correlation = totals[0] / jnp.sqrt(totals[1] * totals[2])

    def pull_group(group_rows):
        return backproject(group_rows[:3], group_rows[3], gradient, edge_len)

    pulled = lax.map(pull_group, grouped)
    pulled = jnp.transpose(pulled.reshape(groups, 3, group_slots, atoms_per), (0, 2, 1, 3)).reshape(
        n_tile, most_slots, 3, atoms_per
    )
    filled = sources >= 0
    block_ids = jnp.maximum(sources, 0) // per_block
    onehot = (
        (block_ids[:, :, None] == jnp.arange(block_count, dtype=jnp.int32)[None, None, :])
        & filled[:, :, None]
    ).astype(jnp.float32)
    owner_terms = jnp.einsum(
        "drb,drca->dcba", onehot, pulled, precision=lax.Precision.HIGHEST
    ).reshape(n_tile, 3, a_dev)
    forces = lax.psum_scatter(owner_terms, "tile", scatter_dimension=0, tiled=True).reshape(
        3, a_dev
    )
    partial_modes = jnp.dot(
        modes_flat,
        forces.astype(jnp.bfloat16).reshape(3 * a_dev),
        preferred_element_type=jnp.float32,
    )
    total_atoms = a_dev * n_tile * n_seg
    mode_grad = lax.psum(partial_modes, ("tile", "seg")) / jnp.sqrt(jnp.float32(total_atoms))
    return (forces, mode_grad, correlation)


def solution(mesh):
    return jax.shard_map(
        on_device,
        mesh=mesh,
        in_specs=(
            P(None, ("tile", "seg")),
            P(("tile", "seg")),
            P(None, None, ("tile", "seg")),
            P(),
            P("tile", None),
            P(("tile", "seg"), None),
            P(("tile", "seg"), None, None),
        ),
        out_specs=(P(None, ("tile", "seg")), P(), P()),
        check_vma=False,
    )
```

profile of v0, /device:TPU:1, one launch (start us, length us, event | category | flops | bytes accessed | tf_op | source)
XLA Modules:
  0.0 889.4 jit_solution(2226179243172119362)
XLA Ops:
  7.3 1.7 copy.66
  11.4 58.6 %all_gather.6 = f32[16384,4]{0,1:T(4,128)S(1)} all-gather(f32[128,4]{0,1:T(4,128)S(1)} %pad_maximum_fusion.1), channel_id=1, replica_groups=mesh['tile'=128,'seg'=4] {'tile'}, dimensions={0}, use_global_device_ids=true | all-gather | bytes 264192 | tf_op jit(solution)/shard_map/all_gather | solution.py:127
  70.0 5.1 copy.65
  75.0 9.1 %slice.87 = f32[128,128,3]{2,1,0:T(8,128)} slice(f32[128,128,4]{2,1,0:T(8,128)} %bitcast.178), slice={[0:128], [0:128], [1:4]} | slice | bytes 393216 | tf_op jit(solution)/shard_map/slice | solution.py:132
  84.1 2.2 fusion.26
  86.4 5.1 convert_reduce_fusion
  92.1 2.4 gather_fusion.1
  95.0 5.6 all-gather.2.cloned.1.call-done
  100.5 4.2 copy.99
  104.7 1.9 copy.67
  106.6 6.1 copy.69
  112.7 4.7 gather_fusion
  118.3 12.3 %while.22 = (s32[]{:T(128)}, f32[1024,32]{0,1:T(8,128)S(1)}, f32[8,4,1024]{2,1,0:T(4,128)S(1)}, s32[]{:T(128)}, s32[]{:T(128)}, /*index=5*/s32[]{}) while((s32[]{:T(128)}, f32[1024,32]{0,1:T(8,128)S(1)}, f32[8,4,1024]{2,1,0:T(4,128)S(1)}, s32[]{:T(128)}, s32[]{:T(128)}, /*index=5*/s32[]{}) %tuple.80), condition=%wide.region_3.4_spmd.clone, body=%wide.region_2.3_spmd.clone.sunk | while | flops 69795872 | bytes 5882215 | solution.py:151
  133.4 46.5 %all-reduce.5.cloned.1.call-done = f32[1024,32]{1,0:T(8,128)} async-done(((f32[1024,32]{1,0:T(8,128)}), f32[1024,32]{1,0:T(8,128)}) %all-reduce.5.cloned.1.call-update) | async-done | bytes 131088 | tf_op jit(solution)/shard_map/psum | solution.py:156
  179.8 1.8 multiply_reduce_fusion.2
  181.6 250.9 %all-reduce.1 = (f32[]{:T(128)}, f32[]{:T(128)}, f32[]{:T(128)}) all-reduce(f32[]{:T(128)} %get-tuple-element.94, f32[]{:T(128)} %get-tuple-element.93, f32[]{:T(128)} %get-tuple-element.95), channel_id=1, replica_groups=mesh['tile'=128,'seg'=4] {'tile'}, use_global_device_ids=true, to_apply=%region_6.7 | all-reduce | flops 3 | bytes 24 | tf_op jit(solution)/shard_map/psum | solution.py:157
  434.6 1.8 multiply_convert_fusion.1
  436.5 132.6 %while.21 = (s32[]{:T(128)}, f32[8,3,1024]{2,0,1:T(8,128)S(1)}, f32[8,4,1024]{2,1,0:T(4,128)S(1)}, bf16[1024,32]{1,0:T(8,128)(2,1)S(1)}, s32[]{:T(128)}, /*index=5*/s32[]{:T(128)}, s32[]{}) while((s32[]{:T(128)}, f32[8,3,1024]{2,0,1:T(8,128)S(1)}, f32[8,4,1024]{2,1,0:T(4,128)S(1)}, bf16[1024,32]{1,0:T(8,128)(2,1)S(1)}, s32[]{:T(128)}, ...), condition=%wide.region_18.19_spmd, body=%wide.region_11.0_spmd.sunk | while | flops 143920160 | bytes 28643688 | solution.py:166
  436.7 3.3 convert_bitcast_fusion.3
  440.0 7.1 copy.102
  447.2 5.5 fusion.63
  453.3 3.3 convert_bitcast_fusion.3
  456.6 7.1 copy.102
  463.8 5.5 fusion.63
  469.9 3.3 convert_bitcast_fusion.3
  473.2 7.1 copy.102
  480.3 5.5 fusion.63
  486.5 3.3 convert_bitcast_fusion.3
  489.7 7.1 copy.102
  496.9 5.5 fusion.63
  503.0 3.3 convert_bitcast_fusion.3
  506.3 7.1 copy.102
  513.5 5.5 fusion.63
  519.6 3.3 convert_bitcast_fusion.3
  522.9 7.1 copy.102
  530.1 5.5 fusion.63
  536.2 3.3 convert_bitcast_fusion.3
  539.5 7.1 copy.102
  546.6 5.5 fusion.63
  552.7 3.3 convert_bitcast_fusion.3
  556.0 7.1 copy.102
  563.2 5.5 fusion.63
  569.2 7.4 convolution_bitcast_fusion
  576.6 5.7 copy.82
  582.3 2.0 copy.83
  585.6 194.3 %all-reduce.7.cloned.1.call-done = f32[128,3,1024]{2,1,0:T(4,128)} async-done(((f32[128,3,1024]{2,1,0:T(4,128)}), f32[128,3,1024]{2,1,0:T(4,128)}) %all-reduce.7.cloned.1.call-update) | async-done | bytes 1572880
  780.0 2.0 convert_bitcast_fusion.1
  782.4 98.7 %psum.39 = f32[256]{0:T(256)S(1)} all-reduce(f32[256]{0:T(256)S(1)} %bitcast.196), channel_id=1, replica_groups=mesh['tile'=128,'seg'=4] {'tile','seg'}, use_global_device_ids=true, to_apply=%region_20.21 | all-reduce | flops 256 | bytes 2048 | tf_op jit(solution)/shard_map/psum | solution.py:188
  (211 shorter events, 25.4 us)
Async XLA Ops:
  7.2 3.0 copy-start.2
  7.2 3.0 copy-start.4
  7.2 3.7 copy-start.3
  7.2 4.0 copy-start.5
  7.2 93.3 %all-gather.2.cloned.1.call-start = ((), (), s32[]{:S(2)}) async-start(), calls=%async_computation | async-start | bytes 2113536 | tf_op jit(solution)/shard_map/all_gather | solution.py:126
  10.8 169.0 %all-reduce.5.cloned.1.call-start = ((), (), s32[]{:S(2)}) async-start(), calls=%async_computation.1 | async-start | bytes 1048576 | tf_op jit(solution)/shard_map/psum | solution.py:156
  75.0 9.1 %slice-start = ((s8[8388608]{0:T(1024)(128)(4,1)}), s8[4194304]{0:T(1024)(128)(4,1)S(1)}, s32[]{:S(2)}) async-start(s8[8388608]{0:T(1024)(128)(4,1)} %bitcast.179), calls=%async_computation.3 | async-start | bytes 8388608
  75.0 9.1 %slice-start.1 = ((s8[8388608]{0:T(1024)(128)(4,1)}), s8[4194304]{0:T(1024)(128)(4,1)S(1)}, s32[]{:S(2)}) async-start(s8[8388608]{0:T(1024)(128)(4,1)} %bitcast.179), calls=%async_computation.4 | async-start | bytes 8388608
  118.3 13.6 %copy-start.1 = (bf16[1,32768]{1,0:T(2,128)(2,1)S(1)}, bf16[1,32768]{1,0:T(2,128)(2,1)}, u32[]{:S(2)}) copy-start(bf16[1,32768]{1,0:T(2,128)(2,1)} %param.15) | copy-start | bytes 196612
  131.7 648.3 %all-reduce.7.cloned.1.call-start = ((), (), s32[]{:S(2)}) async-start(), calls=%async_computation.2 | async-start | bytes 4194304
  582.3 199.6 %copy-start = (bf16[256,3,1024]{2,0,1:T(8,128)(2,1)S(1)}, bf16[256,3,1024]{2,0,1:T(8,128)(2,1)}, u32[]{:S(2)}) copy-start(bf16[256,3,1024]{2,0,1:T(8,128)(2,1)} %param.13) | copy-start | bytes 4718596
Sparse Core Ops, SparseCore 0:
  11.7 88.7 all-gather.1
  131.8 48.0 all-reduce.4
  584.5 195.4 all-reduce.6
where the time goes:
time: 891 us; the launch traced here: 889 us
  blocking collectives  408 us (46%)
  waiting for transfers between devices  246 us (28%)
  local copies, waits for them, and re-layouts  106 us (12%)
  other arithmetic  69 us (8%)
  matrix products  40.6 us (5%)
  between operations  17.3 us (2%)
    psum x1, blocking collectives, on_device(): lax.psum((jnp.sum(density * target), jnp.sum(density * density), jnp.sum(...  251 us
    unnamed x4, waiting for transfers between devices  194 us
    psum x1, blocking collectives, on_device(): lax.psum(partial_modes, ('tile', 'seg'))  98.7 us
    all_gather x1, blocking collectives, on_device(): lax.all_gather(entry_table, 'tile', axis=0, tiled=True)  58.6 us
    reshape x8, local copies, waits for them, and re-layouts, backproject(): contracted = lax.optimization_barrier(contracted).astype(jnp.float32).res...  57.1 us
    psum x1, waiting for transfers between devices, on_device(): density = lax.psum(partial_density, 'seg')  46.5 us
    reduce_sum x8, other arithmetic, backproject(): force_y = jnp.sum(along_z * jnp.sum(sloped * along_x[None], axis=1), axis=0)  44.3 us
    dot_general x8, matrix products, backproject(): jnp.dot(gradient, y_factors, preferred_element_type=jnp.float32)  26.3 us
  transfers between devices with their start and end apart: 3, of which 3 were waited for; matrix products, arithmetic and copies ran while one was open for 3% of the time, Pallas kernels for 0%

commit v1 on v0

v1 whole, which is shorter than its diff:
```python
import jax
import jax.numpy as jnp
from jax import lax
from jax.sharding import PartitionSpec as P

EDGE = 32
ATOM_BLOCK = 32


inverse_var = 1.0 / 2.25


def factors(frame_pos, edge_len):
    centers = jnp.arange(edge_len, dtype=jnp.float32) + 0.5
    distance = centers[None, :, None] - frame_pos[:, None, :]
    profile = jnp.exp(-0.5 * inverse_var * distance * distance)
    slopes = inverse_var * distance * profile
    return (profile, slopes)


def splat_tile(frame_pos, masses, edge_len):
    profile, slopes = factors(frame_pos, edge_len)
    rounded = profile.astype(jnp.bfloat16)
    along_y = (masses[None, :] * profile[1]).astype(jnp.bfloat16)
    plane_kr = (
        rounded[2].astype(jnp.float32)[:, None, :] * rounded[0].astype(jnp.float32)[None, :, :]
    ).astype(jnp.bfloat16)
    plane_kr = plane_kr.reshape(edge_len * edge_len, frame_pos.shape[1])
    return lax.dot_general(
        plane_kr, along_y, (((1,), (1,)), ((), ())), preferred_element_type=jnp.float32
    )


def backproject(frame_pos, masses, gradient, edge_len):
    profile, slopes = factors(frame_pos, edge_len)
    atom_count = frame_pos.shape[1]
    rounded = profile.astype(jnp.bfloat16)
    rounded_slopes = slopes.astype(jnp.bfloat16)
    y_factors = jnp.concatenate(
        [
            (masses[None, :] * profile[1]).astype(jnp.bfloat16),
            (masses[None, :] * slopes[1]).astype(jnp.bfloat16),
        ],
        axis=1,
    )
    contracted = jnp.dot(gradient, y_factors, preferred_element_type=jnp.float32).astype(
        jnp.bfloat16
    )
    contracted = (
        lax.optimization_barrier(contracted)
        .astype(jnp.float32)
        .reshape(edge_len, edge_len, 2 * atom_count)
    )
    plain_sum = contracted[:, :, :atom_count]
    sloped = contracted[:, :, atom_count:]
    along_x = rounded[0].astype(jnp.float32)
    along_z = rounded[2].astype(jnp.float32)
    slope_x = rounded_slopes[0].astype(jnp.float32)
    slope_z = rounded_slopes[2].astype(jnp.float32)
    force_x = jnp.sum(along_z * jnp.sum(plain_sum * slope_x[None], axis=1), axis=0)
    force_y = jnp.sum(along_z * jnp.sum(sloped * along_x[None], axis=1), axis=0)
    force_z = jnp.sum(slope_z * jnp.sum(plain_sum * along_x[None], axis=1), axis=0)
    return jnp.stack([force_x, force_y, force_z])


def gradient_of(density, target, totals, voxels):
    root = jnp.sqrt(totals[1] * totals[2])
    correlation = totals[0] / root
    return (voxels * (target / root - correlation * density / totals[1])).astype(jnp.bfloat16)


def swap_over(values, axis, mask):
    size = lax.axis_size(axis)
    return lax.ppermute(values, axis, [(i, i ^ mask) for i in range(size)])


def small_sum(values, axis):
    mask = 1
    while mask < lax.axis_size(axis):
        values = values + swap_over(values, axis, mask)
        mask *= 2
    return values


def ring_sum(values, axis):
    size = lax.axis_size(axis)
    step = [lax.ppermute(values, axis, [(i, (i + k) % size) for i in range(size)]) for k in (1, 2, 3)]
    return (values + step[1]) + (step[0] + step[2])


def on_device(coords, weights, mode_vectors, amplitudes, density_map, block_tiles, block_offsets):
    edge_len = EDGE
    atoms_per = ATOM_BLOCK
    a_dev = coords.shape[1]
    block_count = block_tiles.shape[0]
    per_block = block_tiles.shape[1]
    entry_count = block_count * per_block
    n_tile = lax.axis_size("tile")
    n_seg = lax.axis_size("seg")
    modes_flat = mode_vectors.reshape(mode_vectors.shape[0], 3 * a_dev)
    displacement = jnp.dot(
        amplitudes.astype(jnp.bfloat16)[None, :], modes_flat, preferred_element_type=jnp.float32
    ).reshape(3, a_dev)
    bundle = jnp.concatenate([coords + displacement, weights[None, :]], axis=0)
    tile_ids = block_tiles.reshape(entry_count)
    offsets_f = block_offsets.reshape(entry_count, 3).astype(jnp.float32)
    ordinal = jnp.arange(entry_count, dtype=jnp.int32)
    earlier = (ordinal[None, :] < ordinal[:, None]) & (tile_ids[None, :] == tile_ids[:, None])
    slot_of = 2 * tile_ids + jnp.sum(earlier.astype(jnp.int32), axis=1)
    chosen = (jnp.arange(2 * n_tile, dtype=jnp.int32)[:, None] == slot_of[None, :]).astype(
        jnp.float32
    )
    by_block = jnp.transpose(bundle.reshape(4, block_count, atoms_per), (1, 0, 2))
    shift = jnp.concatenate([offsets_f, jnp.zeros((entry_count, 1), jnp.float32)], axis=1)
    rows = jnp.repeat(by_block, per_block, axis=0) + shift[:, :, None]
    send = jnp.dot(chosen, rows.reshape(entry_count, 4 * atoms_per), precision=lax.Precision.HIGHEST)
    got = lax.all_to_all(
        send.reshape(n_tile, 2, 4 * atoms_per), "tile", split_axis=0, concat_axis=0, tiled=True
    )
    slot_count = 2 * n_tile
    group_slots = 32
    groups = slot_count // group_slots
    grouped = jnp.transpose(
        got.reshape(groups, group_slots, 4, atoms_per), (0, 2, 1, 3)
    ).reshape(groups, 4, group_slots * atoms_per)

    def add_group(density, group_rows):
        return (density + splat_tile(group_rows[:3], group_rows[3], edge_len), None)

    partial_density, _ = lax.scan(
        add_group, jnp.zeros((edge_len * edge_len, edge_len), jnp.float32), grouped
    )
    target = density_map.reshape(edge_len * edge_len // 4, edge_len * 4).astype(jnp.float32)
    voxels = float(n_tile * edge_len**3)
    density = ring_sum(partial_density.reshape(edge_len * edge_len // 4, edge_len * 4), "seg")
    totals = small_sum(
        jnp.stack([jnp.sum(density * target), jnp.sum(density * density), jnp.sum(target * target)]),
        "tile",
    )
    gradient = gradient_of(density, target, totals, voxels).reshape(edge_len * edge_len, edge_len)
    correlation = totals[0] / jnp.sqrt(totals[1] * totals[2])

    def pull_group(group_rows):
        return backproject(group_rows[:3], group_rows[3], gradient, edge_len)

    pulled = lax.map(pull_group, grouped)
    pulled = jnp.transpose(
        pulled.reshape(groups, 3, group_slots, atoms_per), (0, 2, 1, 3)
    ).reshape(n_tile, 2, 3 * atoms_per)
    back = lax.all_to_all(pulled, "tile", split_axis=0, concat_axis=0, tiled=True)
    per_entry = jnp.dot(
        chosen.T, back.reshape(slot_count, 3 * atoms_per), precision=lax.Precision.HIGHEST
    )
    forces = jnp.sum(per_entry.reshape(block_count, per_block, 3, atoms_per), axis=1)
    forces = jnp.transpose(forces, (1, 0, 2)).reshape(3, a_dev)
    partial_modes = jnp.dot(
        modes_flat,
        forces.astype(jnp.bfloat16).reshape(3 * a_dev),
        preferred_element_type=jnp.float32,
    )
    total_atoms = a_dev * n_tile * n_seg
    partial_modes = ring_sum(partial_modes.reshape(2, 128), "seg")
    every = lax.all_to_all(
        jnp.broadcast_to(partial_modes[None], (n_tile, 2, 128)),
        "tile",
        split_axis=0,
        concat_axis=0,
        tiled=True,
    )
    mode_grad = jnp.sum(every, axis=0).reshape(-1) / jnp.sqrt(jnp.float32(total_atoms))
    return (forces, mode_grad, correlation)


def solution(mesh):
    return jax.shard_map(
        on_device,
        mesh=mesh,
        in_specs=(
            P(None, ("tile", "seg")),
            P(("tile", "seg")),
            P(None, None, ("tile", "seg")),
            P(),
            P("tile", None),
            P(("tile", "seg"), None),
            P(("tile", "seg"), None, None),
        ),
        out_specs=(P(None, ("tile", "seg")), P(), P()),
        check_vma=False,
    )
```

time: 891 us -> 311 us (0.35)
  blocking collectives: 408 us -> 0 us
  waiting for transfers between devices: 246 us -> 59.3 us
  starting transfers between devices: 0.3 us -> 79.9 us
  local copies, waits for them, and re-layouts: 106 us -> 67.3 us
  between operations: 17.3 us -> 4.23 us
    psum x2 -> x0, blocking collectives: 350 us -> none  [the longest x1 251 us: on_device(): lax.psum((jnp.sum(density * target), jnp.sum(density * density), jnp.sum(...]
    unnamed x4 -> x0, waiting for transfers between devices: 194 us -> none
    all_gather x1 -> x0, blocking collectives: 58.6 us -> none  [on_device(): lax.all_gather(entry_table, 'tile', axis=0, tiled=True)]
    psum x1 -> x0, waiting for transfers between devices: 46.5 us -> none  [on_device(): density = lax.psum(partial_density, 'seg')]
    ppermute x0 -> x13, starting transfers between devices: none -> 41.1 us  [the longest x6 21.2 us: ring_sum(): lax.ppermute(values, axis, [(i, (i + k) % size) for i in range(size)])]
    all_to_all x0 -> x3, starting transfers between devices: none -> 38.9 us  [the longest x1 18.4 us: on_device(): lax.all_to_all(send.reshape(n_tile, 2, 4 * atoms_per), 'tile', split_axis...]
    all_to_all x0 -> x3, waiting for transfers between devices: none -> 35.8 us  [the longest x1 12.2 us: on_device(): lax.all_to_all(pulled, 'tile', split_axis=0, concat_axis=0, tiled=True)]
    ppermute x0 -> x13, waiting for transfers between devices: none -> 23.5 us  [the longest x7 20.5 us: swap_over(): return lax.ppermute(values, axis, [(i, i ^ mask) for i in range(size)])]
  transfers between devices with their start and end apart: 3 -> 16, of which waited for: 3 -> 12; matrix products, arithmetic and copies ran while one was open for 3% -> 1% of each run, Pallas kernels for 0% -> 0%
where the time goes in v1:
time: 311 us; the launch traced here: 309 us
  starting transfers between devices  79.9 us (26%)
  local copies, waits for them, and re-layouts  67.3 us (22%)
  other arithmetic  63.3 us (20%)
  waiting for transfers between devices  59.3 us (19%)
  matrix products  33.7 us (11%)
  between operations  4.23 us (1%)
    reshape x8, local copies, waits for them, and re-layouts, backproject(): contracted = lax.optimization_barrier(contracted).astype(jnp.float32).res...  57.1 us
    reduce_sum x8, other arithmetic, backproject(): force_y = jnp.sum(along_z * jnp.sum(sloped * along_x[None], axis=1), axis=0)  44.3 us
    dot_general x8, matrix products, backproject(): jnp.dot(gradient, y_factors, preferred_element_type=jnp.float32)  26.3 us
    ppermute x6, starting transfers between devices, ring_sum(): lax.ppermute(values, axis, [(i, (i + k) % size) for i in range(size)])  21.2 us
    ppermute x7, waiting for transfers between devices, swap_over(): return lax.ppermute(values, axis, [(i, i ^ mask) for i in range(size)])  20.5 us
    ppermute x7, starting transfers between devices, swap_over(): return lax.ppermute(values, axis, [(i, i ^ mask) for i in range(size)])  19.9 us
    all_to_all x1, starting transfers between devices, on_device(): lax.all_to_all(send.reshape(n_tile, 2, 4 * atoms_per), 'tile', split_axis...  18.4 us
    all_to_all x1, starting transfers between devices, on_device(): lax.all_to_all(pulled, 'tile', split_axis=0, concat_axis=0, tiled=True)  12.5 us
  transfers between devices with their start and end apart: 16, of which 12 were waited for; matrix products, arithmetic and copies ran while one was open for 1% of the time, Pallas kernels for 0%

profile of v1, /device:TPU:1, one launch (start us, length us, event | category | flops | bytes accessed | tf_op | source)
XLA Modules:
  0.0 309.1 jit_solution(2199435039526444326)
XLA Ops:
  6.5 18.4 %all-to-all-start = ((f32[128,2,128]{2,1,0:T(2,128)}), f32[128,2,128]{2,1,0:T(2,128)S(1)}, u32[]{:S(2)}, u32[]{:S(2)}) async-start(f32[128,2,128]{2,1,0:T(2,128)} %copy.75), calls=%async_computation | async-start | bytes 262144 | tf_op jit(solution)/shard_map/all_to_all | solution.py:117
  25.1 12.0 %all-to-all-done = f32[128,2,128]{2,1,0:T(2,128)S(1)} async-done(((f32[128,2,128]{2,1,0:T(2,128)}), f32[128,2,128]{2,1,0:T(2,128)S(1)}, u32[]{:S(2)}, u32[]{:S(2)}) %all-to-all-start) | async-done | bytes 131104 | tf_op jit(solution)/shard_map/all_to_all | solution.py:117
  37.8 12.3 %while.22 = (s32[]{:T(128)}, f32[1024,32]{0,1:T(8,128)S(1)}, f32[8,4,1024]{2,1,0:T(4,128)S(1)}, s32[]{:T(128)}, s32[]{:T(128)}, /*index=5*/s32[]{}) while((s32[]{:T(128)}, f32[1024,32]{0,1:T(8,128)S(1)}, f32[8,4,1024]{2,1,0:T(4,128)S(1)}, s32[]{:T(128)}, s32[]{:T(128)}, /*index=5*/s32[]{}) %tuple.73), condition=%wide.region_2.3_spmd.clone, body=%wide.region_1.2_spmd.clone.sunk | while | flops 69795872 | bytes 5882215 | solution.py:130
  50.5 4.7 %collective-permute-start = (f32[256,128]{1,0:T(8,128)S(1)}, f32[256,128]{1,0:T(8,128)S(1)}, u32[]{:S(2)}, u32[]{:S(2)}) collective-permute-start(f32[256,128]{1,0:T(8,128)S(1)} %reshape.186), channel_id=1, source_target_pairs={{0,2},{1,3},{2,0},{3,1},{4,6},{5,7},{6,4},{7,5},{8,10},{9,11},{10,... | collective-permute-start | bytes 393224 | tf_op jit(solution)/shard_map/ppermute | solution.py:87
  55.1 2.2 collective-permute-start.1
  57.4 4.3 %collective-permute-start.2 = (f32[256,128]{1,0:T(8,128)S(1)}, f32[256,128]{1,0:T(8,128)S(1)}, u32[]{:S(2)}, u32[]{:S(2)}) collective-permute-start(f32[256,128]{1,0:T(8,128)S(1)} %reshape.186), channel_id=1, source_target_pairs={{0,3},{1,0},{2,1},{3,2},{4,7},{5,4},{6,5},{7,6},{8,11},{9,8},{10,9... | collective-permute-start | bytes 393224 | tf_op jit(solution)/shard_map/ppermute | solution.py:87
  66.3 4.3 %collective-permute-start.3 = (f32[3]{0:T(128)S(1)}, f32[3]{0:T(128)S(1)}, u32[]{:S(2)}, u32[]{:S(2)}) collective-permute-start(f32[3]{0:T(128)S(1)} %pad_maximum_fusion), channel_id=1, source_target_pairs={{0,4},{4,0},{8,12},{12,8},{16,20},{20,16},{24,28},{28,24},{32,36},... | collective-permute-start | bytes 44 | tf_op jit(solution)/shard_map/ppermute | solution.py:74
  79.8 2.2 collective-permute-start.5
  82.0 2.9 collective-permute-done.5
  85.0 3.0 collective-permute-start.6
  88.0 5.1 %collective-permute-done.6 = f32[3]{0:T(128)S(1)} collective-permute-done((f32[3]{0:T(128)S(1)}, f32[3]{0:T(128)S(1)}, u32[]{:S(2)}, u32[]{:S(2)}) %collective-permute-start.6) | collective-permute-done | bytes 44 | tf_op jit(solution)/shard_map/ppermute | solution.py:74
  93.2 2.4 collective-permute-start.7
  97.4 2.6 collective-permute-start.8
  100.1 2.6 collective-permute-done.8
  102.6 3.1 %collective-permute-start.9 = (f32[3]{0:T(128)S(1)}, f32[3]{0:T(128)S(1)}, u32[]{:S(2)}, u32[]{:S(2)}) collective-permute-start(f32[3]{0:T(128)S(1)} %add.108), channel_id=1, source_target_pairs={{0,256},{4,260},{8,264},{12,268},{16,272},{20,276},{24,280},{28,28... | collective-permute-start | bytes 44 | tf_op jit(solution)/shard_map/ppermute | solution.py:74
  105.7 5.1 %collective-permute-done.9 = f32[3]{0:T(128)S(1)} collective-permute-done((f32[3]{0:T(128)S(1)}, f32[3]{0:T(128)S(1)}, u32[]{:S(2)}, u32[]{:S(2)}) %collective-permute-start.9) | collective-permute-done | bytes 44 | tf_op jit(solution)/shard_map/ppermute | solution.py:74
  114.4 132.6 %while.21 = (s32[]{:T(128)}, f32[8,3,1024]{2,0,1:T(8,128)S(1)}, f32[8,4,1024]{2,1,0:T(4,128)S(1)}, bf16[1024,32]{1,0:T(8,128)(2,1)S(1)}, s32[]{:T(128)}, /*index=5*/s32[]{:T(128)}, s32[]{}) while((s32[]{:T(128)}, f32[8,3,1024]{2,0,1:T(8,128)S(1)}, f32[8,4,1024]{2,1,0:T(4,128)S(1)}, bf16[1024,32]{1,0:T(8,128)(2,1)S(1)}, s32[]{:T(128)}, ...), condition=%wide.region_13.14_spmd, body=%wide.region_6.13_spmd.sunk | while | flops 143920160 | bytes 28643688 | solution.py:146
  114.7 3.3 %convert_bitcast_fusion.2 = bf16[1024,2048]{0,1:T(8,128)(2,1)} fusion(bf16[1024,32]{1,0:T(8,128)(2,1)S(1)} %get-tuple-element.231, bf16[32,1024]{1,0:T(8,128)(2,1)S(1)} %get-tuple-element.179, bf16[32,1024]{1,0:T(8,128)(2,1)S(1)} %get-tuple-element.180), kind=kOutput, calls=%fused_computation.4.clone.1 | convolution fusion | flops 136577024 | bytes 4390912 | tf_op jit(solution)/shard_map/while/body/eval_jaxpr/dot_general | solution.py:46
  118.0 7.1 %copy.110 = f32[1024,2048]{1,0:T(8,128)} copy(bf16[1024,2048]{0,1:T(8,128)(2,1)} %convert_bitcast_fusion.2) | data formatting | bytes 12582912 | tf_op jit(solution)/shard_map/while/body/eval_jaxpr/reshape | solution.py:52
  125.2 5.5 %fusion.63 = (f32[32,1024]{1,0:T(8,128)S(1)}, f32[32,1024]{1,0:T(8,128)S(1)}, f32[32,1024]{1,0:T(8,128)S(1)}) fusion(f32[32,32,2048]{2,1,0:T(8,128)} %bitcast.151, f32[32,1024]{1,0:T(8,128)S(1)} %fusion.61, f32[32,1024]{1,0:T(8,128)S(1)} %fusion.62), kind=kLoop, calls=%fused_computation.1.clone.1 | loop fusion | flops 6193152 | bytes 9043968 | tf_op jit(solution)/shard_map/while/body/eval_jaxpr/reduce_sum | solution.py:61
  131.3 3.3 %convert_bitcast_fusion.2 = bf16[1024,2048]{0,1:T(8,128)(2,1)} fusion(bf16[1024,32]{1,0:T(8,128)(2,1)S(1)} %get-tuple-element.231, bf16[32,1024]{1,0:T(8,128)(2,1)S(1)} %get-tuple-element.179, bf16[32,1024]{1,0:T(8,128)(2,1)S(1)} %get-tuple-element.180), kind=kOutput, calls=%fused_computation.4.clone.1 | convolution fusion | flops 136577024 | bytes 4390912 | tf_op jit(solution)/shard_map/while/body/eval_jaxpr/dot_general | solution.py:46
  134.6 7.1 %copy.110 = f32[1024,2048]{1,0:T(8,128)} copy(bf16[1024,2048]{0,1:T(8,128)(2,1)} %convert_bitcast_fusion.2) | data formatting | bytes 12582912 | tf_op jit(solution)/shard_map/while/body/eval_jaxpr/reshape | solution.py:52
  141.7 5.5 %fusion.63 = (f32[32,1024]{1,0:T(8,128)S(1)}, f32[32,1024]{1,0:T(8,128)S(1)}, f32[32,1024]{1,0:T(8,128)S(1)}) fusion(f32[32,32,2048]{2,1,0:T(8,128)} %bitcast.151, f32[32,1024]{1,0:T(8,128)S(1)} %fusion.61, f32[32,1024]{1,0:T(8,128)S(1)} %fusion.62), kind=kLoop, calls=%fused_computation.1.clone.1 | loop fusion | flops 6193152 | bytes 9043968 | tf_op jit(solution)/shard_map/while/body/eval_jaxpr/reduce_sum | solution.py:61
  147.8 3.3 %convert_bitcast_fusion.2 = bf16[1024,2048]{0,1:T(8,128)(2,1)} fusion(bf16[1024,32]{1,0:T(8,128)(2,1)S(1)} %get-tuple-element.231, bf16[32,1024]{1,0:T(8,128)(2,1)S(1)} %get-tuple-element.179, bf16[32,1024]{1,0:T(8,128)(2,1)S(1)} %get-tuple-element.180), kind=kOutput, calls=%fused_computation.4.clone.1 | convolution fusion | flops 136577024 | bytes 4390912 | tf_op jit(solution)/shard_map/while/body/eval_jaxpr/dot_general | solution.py:46
  151.1 7.1 %copy.110 = f32[1024,2048]{1,0:T(8,128)} copy(bf16[1024,2048]{0,1:T(8,128)(2,1)} %convert_bitcast_fusion.2) | data formatting | bytes 12582912 | tf_op jit(solution)/shard_map/while/body/eval_jaxpr/reshape | solution.py:52
  158.3 5.5 %fusion.63 = (f32[32,1024]{1,0:T(8,128)S(1)}, f32[32,1024]{1,0:T(8,128)S(1)}, f32[32,1024]{1,0:T(8,128)S(1)}) fusion(f32[32,32,2048]{2,1,0:T(8,128)} %bitcast.151, f32[32,1024]{1,0:T(8,128)S(1)} %fusion.61, f32[32,1024]{1,0:T(8,128)S(1)} %fusion.62), kind=kLoop, calls=%fused_computation.1.clone.1 | loop fusion | flops 6193152 | bytes 9043968 | tf_op jit(solution)/shard_map/while/body/eval_jaxpr/reduce_sum | solution.py:61
  164.4 3.3 %convert_bitcast_fusion.2 = bf16[1024,2048]{0,1:T(8,128)(2,1)} fusion(bf16[1024,32]{1,0:T(8,128)(2,1)S(1)} %get-tuple-element.231, bf16[32,1024]{1,0:T(8,128)(2,1)S(1)} %get-tuple-element.179, bf16[32,1024]{1,0:T(8,128)(2,1)S(1)} %get-tuple-element.180), kind=kOutput, calls=%fused_computation.4.clone.1 | convolution fusion | flops 136577024 | bytes 4390912 | tf_op jit(solution)/shard_map/while/body/eval_jaxpr/dot_general | solution.py:46
  167.7 7.1 %copy.110 = f32[1024,2048]{1,0:T(8,128)} copy(bf16[1024,2048]{0,1:T(8,128)(2,1)} %convert_bitcast_fusion.2) | data formatting | bytes 12582912 | tf_op jit(solution)/shard_map/while/body/eval_jaxpr/reshape | solution.py:52
  174.9 5.5 %fusion.63 = (f32[32,1024]{1,0:T(8,128)S(1)}, f32[32,1024]{1,0:T(8,128)S(1)}, f32[32,1024]{1,0:T(8,128)S(1)}) fusion(f32[32,32,2048]{2,1,0:T(8,128)} %bitcast.151, f32[32,1024]{1,0:T(8,128)S(1)} %fusion.61, f32[32,1024]{1,0:T(8,128)S(1)} %fusion.62), kind=kLoop, calls=%fused_computation.1.clone.1 | loop fusion | flops 6193152 | bytes 9043968 | tf_op jit(solution)/shard_map/while/body/eval_jaxpr/reduce_sum | solution.py:61
  181.0 3.3 %convert_bitcast_fusion.2 = bf16[1024,2048]{0,1:T(8,128)(2,1)} fusion(bf16[1024,32]{1,0:T(8,128)(2,1)S(1)} %get-tuple-element.231, bf16[32,1024]{1,0:T(8,128)(2,1)S(1)} %get-tuple-element.179, bf16[32,1024]{1,0:T(8,128)(2,1)S(1)} %get-tuple-element.180), kind=kOutput, calls=%fused_computation.4.clone.1 | convolution fusion | flops 136577024 | bytes 4390912 | tf_op jit(solution)/shard_map/while/body/eval_jaxpr/dot_general | solution.py:46
  184.3 7.1 %copy.110 = f32[1024,2048]{1,0:T(8,128)} copy(bf16[1024,2048]{0,1:T(8,128)(2,1)} %convert_bitcast_fusion.2) | data formatting | bytes 12582912 | tf_op jit(solution)/shard_map/while/body/eval_jaxpr/reshape | solution.py:52
  191.5 5.5 %fusion.63 = (f32[32,1024]{1,0:T(8,128)S(1)}, f32[32,1024]{1,0:T(8,128)S(1)}, f32[32,1024]{1,0:T(8,128)S(1)}) fusion(f32[32,32,2048]{2,1,0:T(8,128)} %bitcast.151, f32[32,1024]{1,0:T(8,128)S(1)} %fusion.61, f32[32,1024]{1,0:T(8,128)S(1)} %fusion.62), kind=kLoop, calls=%fused_computation.1.clone.1 | loop fusion | flops 6193152 | bytes 9043968 | tf_op jit(solution)/shard_map/while/body/eval_jaxpr/reduce_sum | solution.py:61
  197.6 3.3 %convert_bitcast_fusion.2 = bf16[1024,2048]{0,1:T(8,128)(2,1)} fusion(bf16[1024,32]{1,0:T(8,128)(2,1)S(1)} %get-tuple-element.231, bf16[32,1024]{1,0:T(8,128)(2,1)S(1)} %get-tuple-element.179, bf16[32,1024]{1,0:T(8,128)(2,1)S(1)} %get-tuple-element.180), kind=kOutput, calls=%fused_computation.4.clone.1 | convolution fusion | flops 136577024 | bytes 4390912 | tf_op jit(solution)/shard_map/while/body/eval_jaxpr/dot_general | solution.py:46
  200.9 7.1 %copy.110 = f32[1024,2048]{1,0:T(8,128)} copy(bf16[1024,2048]{0,1:T(8,128)(2,1)} %convert_bitcast_fusion.2) | data formatting | bytes 12582912 | tf_op jit(solution)/shard_map/while/body/eval_jaxpr/reshape | solution.py:52
  208.0 5.5 %fusion.63 = (f32[32,1024]{1,0:T(8,128)S(1)}, f32[32,1024]{1,0:T(8,128)S(1)}, f32[32,1024]{1,0:T(8,128)S(1)}) fusion(f32[32,32,2048]{2,1,0:T(8,128)} %bitcast.151, f32[32,1024]{1,0:T(8,128)S(1)} %fusion.61, f32[32,1024]{1,0:T(8,128)S(1)} %fusion.62), kind=kLoop, calls=%fused_computation.1.clone.1 | loop fusion | flops 6193152 | bytes 9043968 | tf_op jit(solution)/shard_map/while/body/eval_jaxpr/reduce_sum | solution.py:61
  214.1 3.3 %convert_bitcast_fusion.2 = bf16[1024,2048]{0,1:T(8,128)(2,1)} fusion(bf16[1024,32]{1,0:T(8,128)(2,1)S(1)} %get-tuple-element.231, bf16[32,1024]{1,0:T(8,128)(2,1)S(1)} %get-tuple-element.179, bf16[32,1024]{1,0:T(8,128)(2,1)S(1)} %get-tuple-element.180), kind=kOutput, calls=%fused_computation.4.clone.1 | convolution fusion | flops 136577024 | bytes 4390912 | tf_op jit(solution)/shard_map/while/body/eval_jaxpr/dot_general | solution.py:46
  217.4 7.1 %copy.110 = f32[1024,2048]{1,0:T(8,128)} copy(bf16[1024,2048]{0,1:T(8,128)(2,1)} %convert_bitcast_fusion.2) | data formatting | bytes 12582912 | tf_op jit(solution)/shard_map/while/body/eval_jaxpr/reshape | solution.py:52
  224.6 5.5 %fusion.63 = (f32[32,1024]{1,0:T(8,128)S(1)}, f32[32,1024]{1,0:T(8,128)S(1)}, f32[32,1024]{1,0:T(8,128)S(1)}) fusion(f32[32,32,2048]{2,1,0:T(8,128)} %bitcast.151, f32[32,1024]{1,0:T(8,128)S(1)} %fusion.61, f32[32,1024]{1,0:T(8,128)S(1)} %fusion.62), kind=kLoop, calls=%fused_computation.1.clone.1 | loop fusion | flops 6193152 | bytes 9043968 | tf_op jit(solution)/shard_map/while/body/eval_jaxpr/reduce_sum | solution.py:61
  230.7 3.3 %convert_bitcast_fusion.2 = bf16[1024,2048]{0,1:T(8,128)(2,1)} fusion(bf16[1024,32]{1,0:T(8,128)(2,1)S(1)} %get-tuple-element.231, bf16[32,1024]{1,0:T(8,128)(2,1)S(1)} %get-tuple-element.179, bf16[32,1024]{1,0:T(8,128)(2,1)S(1)} %get-tuple-element.180), kind=kOutput, calls=%fused_computation.4.clone.1 | convolution fusion | flops 136577024 | bytes 4390912 | tf_op jit(solution)/shard_map/while/body/eval_jaxpr/dot_general | solution.py:46
  234.0 7.1 %copy.110 = f32[1024,2048]{1,0:T(8,128)} copy(bf16[1024,2048]{0,1:T(8,128)(2,1)} %convert_bitcast_fusion.2) | data formatting | bytes 12582912 | tf_op jit(solution)/shard_map/while/body/eval_jaxpr/reshape | solution.py:52
  241.2 5.5 %fusion.63 = (f32[32,1024]{1,0:T(8,128)S(1)}, f32[32,1024]{1,0:T(8,128)S(1)}, f32[32,1024]{1,0:T(8,128)S(1)}) fusion(f32[32,32,2048]{2,1,0:T(8,128)} %bitcast.151, f32[32,1024]{1,0:T(8,128)S(1)} %fusion.61, f32[32,1024]{1,0:T(8,128)S(1)} %fusion.62), kind=kLoop, calls=%fused_computation.1.clone.1 | loop fusion | flops 6193152 | bytes 9043968 | tf_op jit(solution)/shard_map/while/body/eval_jaxpr/reduce_sum | solution.py:61
  248.4 12.5 %all-to-all-start.1 = ((f32[128,2,96]{2,1,0:T(2,128)}), f32[128,2,96]{2,1,0:T(2,128)S(1)}, u32[]{:S(2)}, u32[]{:S(2)}) async-start(f32[128,2,96]{2,1,0:T(2,128)} %reshape.189), calls=%async_computation.1 | async-start | bytes 262144 | tf_op jit(solution)/shard_map/all_to_all | solution.py:150
  261.0 12.2 %all-to-all-done.1 = f32[128,2,96]{2,1,0:T(2,128)S(1)} async-done(((f32[128,2,96]{2,1,0:T(2,128)}), f32[128,2,96]{2,1,0:T(2,128)S(1)}, u32[]{:S(2)}, u32[]{:S(2)}) %all-to-all-start.1) | async-done | bytes 98336 | tf_op jit(solution)/shard_map/all_to_all | solution.py:150
  274.2 3.5 %collective-permute-start.10 = (f32[2,128]{1,0:T(2,128)S(1)}, f32[2,128]{1,0:T(2,128)S(1)}, u32[]{:S(2)}, u32[]{:S(2)}) collective-permute-start(f32[2,128]{1,0:T(2,128)S(1)} %bitcast.168), channel_id=1, source_target_pairs={{0,2},{1,3},{2,0},{3,1},{4,6},{5,7},{6,4},{7,5},{8,10},{9,11},{10,... | collective-permute-start | bytes 3080 | tf_op jit(solution)/shard_map/ppermute | solution.py:87
  277.7 4.2 %collective-permute-start.11 = (f32[2,128]{1,0:T(2,128)S(1)}, f32[2,128]{1,0:T(2,128)S(1)}, u32[]{:S(2)}, u32[]{:S(2)}) collective-permute-start(f32[2,128]{1,0:T(2,128)S(1)} %bitcast.169), channel_id=1, source_target_pairs={{0,1},{1,2},{2,3},{3,0},{4,5},{5,6},{6,7},{7,4},{8,9},{9,10},{10,1... | collective-permute-start | bytes 3080 | tf_op jit(solution)/shard_map/ppermute | solution.py:87
  282.0 2.2 collective-permute-start.12
  287.0 7.9 %all-to-all-start.2 = ((f32[128,2,128]{2,1,0:T(2,128)}), f32[128,2,128]{2,1,0:T(2,128)S(1)}, u32[]{:S(2)}, u32[]{:S(2)}) async-start(f32[128,2,128]{2,1,0:T(2,128)} %broadcast_in_dim.14), calls=%async_computation.2 | async-start | bytes 262144 | tf_op jit(solution)/shard_map/all_to_all | solution.py:163
  295.6 11.6 %all-to-all-done.2 = f32[128,2,128]{2,1,0:T(2,128)S(1)} async-done(((f32[128,2,128]{2,1,0:T(2,128)}), f32[128,2,128]{2,1,0:T(2,128)S(1)}, u32[]{:S(2)}, u32[]{:S(2)}) %all-to-all-start.2) | async-done | bytes 131104 | tf_op jit(solution)/shard_map/all_to_all | solution.py:163
  (221 shorter events, 46.5 us)
Async XLA Ops:
  0.6 4.1 %copy-start.2 = (f32[3,1024]{1,0:T(4,128)S(1)}, f32[3,1024]{1,0:T(4,128)}, u32[]{:S(2)}) copy-start(f32[3,1024]{1,0:T(4,128)} %param.11) | copy-start | bytes 36868
  0.6 4.2 %copy-start.4 = (f32[1024]{0:T(1024)S(1)}, f32[1024]{0:T(1024)}, u32[]{:S(2)}) copy-start(f32[1024]{0:T(1024)} %param.12) | copy-start | bytes 12292
  0.7 4.3 %copy-start.3 = (s32[32,4,3]{0,1,2:T(4,128)S(1)}, s32[32,4,3]{0,1,2:T(4,128)}, u32[]{:S(2)}) copy-start(s32[32,4,3]{0,1,2:T(4,128)} %param.17) | copy-start | bytes 4612
  0.7 24.3 %copy-start.1 = (bf16[1,32768]{1,0:T(2,128)(2,1)S(1)}, bf16[1,32768]{1,0:T(2,128)(2,1)}, u32[]{:S(2)}) copy-start(bf16[1,32768]{1,0:T(2,128)(2,1)} %param.15) | copy-start | bytes 196612
  6.5 30.6 %all-to-all-start = ((f32[128,2,128]{2,1,0:T(2,128)}), f32[128,2,128]{2,1,0:T(2,128)S(1)}, u32[]{:S(2)}, u32[]{:S(2)}) async-start(f32[128,2,128]{2,1,0:T(2,128)} %copy.75), calls=%async_computation | async-start | bytes 262144 | tf_op jit(solution)/shard_map/all_to_all | solution.py:117
  50.5 12.1 %collective-permute-start = (f32[256,128]{1,0:T(8,128)S(1)}, f32[256,128]{1,0:T(8,128)S(1)}, u32[]{:S(2)}, u32[]{:S(2)}) collective-permute-start(f32[256,128]{1,0:T(8,128)S(1)} %reshape.186), channel_id=1, source_target_pairs={{0,2},{1,3},{2,0},{3,1},{4,6},{5,7},{6,4},{7,5},{8,10},{9,11},{10,... | collective-permute-start | bytes 393224 | tf_op jit(solution)/shard_map/ppermute | solution.py:87
  55.1 7.5 %collective-permute-start.1 = (f32[256,128]{1,0:T(8,128)S(1)}, f32[256,128]{1,0:T(8,128)S(1)}, u32[]{:S(2)}, u32[]{:S(2)}) collective-permute-start(f32[256,128]{1,0:T(8,128)S(1)} %reshape.186), channel_id=1, source_target_pairs={{0,1},{1,2},{2,3},{3,0},{4,5},{5,6},{6,7},{7,4},{8,9},{9,10},{10,1... | collective-permute-start | bytes 393224 | tf_op jit(solution)/shard_map/ppermute | solution.py:87
  57.4 6.2 %collective-permute-start.2 = (f32[256,128]{1,0:T(8,128)S(1)}, f32[256,128]{1,0:T(8,128)S(1)}, u32[]{:S(2)}, u32[]{:S(2)}) collective-permute-start(f32[256,128]{1,0:T(8,128)S(1)} %reshape.186), channel_id=1, source_target_pairs={{0,3},{1,0},{2,1},{3,2},{4,7},{5,4},{6,5},{7,6},{8,11},{9,8},{10,9... | collective-permute-start | bytes 393224 | tf_op jit(solution)/shard_map/ppermute | solution.py:87
  66.3 5.1 %collective-permute-start.3 = (f32[3]{0:T(128)S(1)}, f32[3]{0:T(128)S(1)}, u32[]{:S(2)}, u32[]{:S(2)}) collective-permute-start(f32[3]{0:T(128)S(1)} %pad_maximum_fusion), channel_id=1, source_target_pairs={{0,4},{4,0},{8,12},{12,8},{16,20},{20,16},{24,28},{28,24},{32,36},... | collective-permute-start | bytes 44 | tf_op jit(solution)/shard_map/ppermute | solution.py:74
  73.5 4.3 %collective-permute-start.4 = (f32[3]{0:T(128)S(1)}, f32[3]{0:T(128)S(1)}, u32[]{:S(2)}, u32[]{:S(2)}) collective-permute-start(f32[3]{0:T(128)S(1)} %fusion.43), channel_id=1, source_target_pairs={{0,8},{4,12},{8,0},{12,4},{16,24},{20,28},{24,16},{28,20},{32,40},... | collective-permute-start | bytes 44 | tf_op jit(solution)/shard_map/ppermute | solution.py:74
  79.8 5.2 %collective-permute-start.5 = (f32[3]{0:T(128)S(1)}, f32[3]{0:T(128)S(1)}, u32[]{:S(2)}, u32[]{:S(2)}) collective-permute-start(f32[3]{0:T(128)S(1)} %fusion.44), channel_id=1, source_target_pairs={{0,16},{4,20},{8,24},{12,28},{16,0},{20,4},{24,8},{28,12},{32,48},... | collective-permute-start | bytes 44 | tf_op jit(solution)/shard_map/ppermute | solution.py:74
  85.0 8.2 %collective-permute-start.6 = (f32[3]{0:T(128)S(1)}, f32[3]{0:T(128)S(1)}, u32[]{:S(2)}, u32[]{:S(2)}) collective-permute-start(f32[3]{0:T(128)S(1)} %add.105), channel_id=1, source_target_pairs={{0,32},{4,36},{8,40},{12,44},{16,48},{20,52},{24,56},{28,60},{32,0... | collective-permute-start | bytes 44 | tf_op jit(solution)/shard_map/ppermute | solution.py:74
  93.2 4.3 %collective-permute-start.7 = (f32[3]{0:T(128)S(1)}, f32[3]{0:T(128)S(1)}, u32[]{:S(2)}, u32[]{:S(2)}) collective-permute-start(f32[3]{0:T(128)S(1)} %add.106), channel_id=1, source_target_pairs={{0,64},{4,68},{8,72},{12,76},{16,80},{20,84},{24,88},{28,92},{32,9... | collective-permute-start | bytes 44 | tf_op jit(solution)/shard_map/ppermute | solution.py:74
  97.4 5.2 %collective-permute-start.8 = (f32[3]{0:T(128)S(1)}, f32[3]{0:T(128)S(1)}, u32[]{:S(2)}, u32[]{:S(2)}) collective-permute-start(f32[3]{0:T(128)S(1)} %add.107), channel_id=1, source_target_pairs={{0,128},{4,132},{8,136},{12,140},{16,144},{20,148},{24,152},{28,15... | collective-permute-start | bytes 44 | tf_op jit(solution)/shard_map/ppermute | solution.py:74
  102.6 8.2 %collective-permute-start.9 = (f32[3]{0:T(128)S(1)}, f32[3]{0:T(128)S(1)}, u32[]{:S(2)}, u32[]{:S(2)}) collective-permute-start(f32[3]{0:T(128)S(1)} %add.108), channel_id=1, source_target_pairs={{0,256},{4,260},{8,264},{12,268},{16,272},{20,276},{24,280},{28,28... | collective-permute-start | bytes 44 | tf_op jit(solution)/shard_map/ppermute | solution.py:74
  114.4 159.3 %copy-start = (bf16[256,3,1024]{2,0,1:T(8,128)(2,1)S(1)}, bf16[256,3,1024]{2,0,1:T(8,128)(2,1)}, u32[]{:S(2)}) copy-start(bf16[256,3,1024]{2,0,1:T(8,128)(2,1)} %param.13) | copy-start | bytes 4718596
  248.4 24.9 %all-to-all-start.1 = ((f32[128,2,96]{2,1,0:T(2,128)}), f32[128,2,96]{2,1,0:T(2,128)S(1)}, u32[]{:S(2)}, u32[]{:S(2)}) async-start(f32[128,2,96]{2,1,0:T(2,128)} %reshape.189), calls=%async_computation.1 | async-start | bytes 262144 | tf_op jit(solution)/shard_map/all_to_all | solution.py:150
  274.2 10.1 %collective-permute-start.10 = (f32[2,128]{1,0:T(2,128)S(1)}, f32[2,128]{1,0:T(2,128)S(1)}, u32[]{:S(2)}, u32[]{:S(2)}) collective-permute-start(f32[2,128]{1,0:T(2,128)S(1)} %bitcast.168), channel_id=1, source_target_pairs={{0,2},{1,3},{2,0},{3,1},{4,6},{5,7},{6,4},{7,5},{8,10},{9,11},{10,... | collective-permute-start | bytes 3080 | tf_op jit(solution)/shard_map/ppermute | solution.py:87
  277.7 6.5 %collective-permute-start.11 = (f32[2,128]{1,0:T(2,128)S(1)}, f32[2,128]{1,0:T(2,128)S(1)}, u32[]{:S(2)}, u32[]{:S(2)}) collective-permute-start(f32[2,128]{1,0:T(2,128)S(1)} %bitcast.169), channel_id=1, source_target_pairs={{0,1},{1,2},{2,3},{3,0},{4,5},{5,6},{6,7},{7,4},{8,9},{9,10},{10,1... | collective-permute-start | bytes 3080 | tf_op jit(solution)/shard_map/ppermute | solution.py:87
  282.0 4.3 %collective-permute-start.12 = (f32[2,128]{1,0:T(2,128)S(1)}, f32[2,128]{1,0:T(2,128)S(1)}, u32[]{:S(2)}, u32[]{:S(2)}) collective-permute-start(f32[2,128]{1,0:T(2,128)S(1)} %bitcast.170), channel_id=1, source_target_pairs={{0,3},{1,0},{2,1},{3,2},{4,7},{5,4},{6,5},{7,6},{8,11},{9,8},{10,9... | collective-permute-start | bytes 3080 | tf_op jit(solution)/shard_map/ppermute | solution.py:87
  287.0 20.2 %all-to-all-start.2 = ((f32[128,2,128]{2,1,0:T(2,128)}), f32[128,2,128]{2,1,0:T(2,128)S(1)}, u32[]{:S(2)}, u32[]{:S(2)}) async-start(f32[128,2,128]{2,1,0:T(2,128)} %broadcast_in_dim.14), calls=%async_computation.2 | async-start | bytes 262144 | tf_op jit(solution)/shard_map/all_to_all | solution.py:163

commit v2 on v1

v2 whole, which is shorter than its diff:
```python
import jax
import jax.numpy as jnp
from jax import lax
from jax.experimental import pallas as pl
from jax.experimental.pallas import tpu as pltpu
from jax.sharding import Mesh
from jax.sharding import PartitionSpec as P

EDGE = 32
ATOM_BLOCK = 32
PLANE = EDGE * EDGE
LANES = 128
CHUNK = 256

inverse_var = 1.0 / 2.25


def factors(places):
    centers = lax.broadcasted_iota(jnp.int32, (EDGE, places.shape[1]), 0).astype(jnp.float32) + 0.5
    distance = centers - places
    profile = jnp.exp(-0.5 * inverse_var * distance * distance)
    return profile, inverse_var * distance * profile


def unpack_rows(got_ref, place_ref):
    pairs = got_ref.shape[0] // 4
    left = lax.broadcasted_iota(jnp.int32, (pairs, LANES), 1) < LANES // 2
    for part in range(2):
        even = got_ref[pl.ds(part, pairs, stride=4), :]
        odd = got_ref[pl.ds(2 + part, pairs, stride=4), :]
        place_ref[2 * part] = jnp.where(left, even, pltpu.roll(odd, LANES // 2, 1))
        place_ref[2 * part + 1] = jnp.where(left, pltpu.roll(even, LANES // 2, 1), odd)


def chunk_row(place_ref, component, start):
    rows = CHUNK // LANES
    return jnp.concatenate([place_ref[component, pl.ds(start + i, 1), :] for i in range(rows)], axis=1)


def splat_kernel(got_ref, out_ref, place_ref, line_ref, plane_ref):
    unpack_rows(got_ref, place_ref)
    per = plane_ref.shape[0]
    rows = CHUNK // LANES
    out_ref[0] = jnp.zeros_like(out_ref[0])

    @pl.loop(0, place_ref.shape[1] // (rows * per))
    def _(step):
        for part in range(per):
            start = (step * per + part) * rows
            along_x = factors(chunk_row(place_ref, 0, start))[0].astype(jnp.bfloat16)
            along_y = factors(chunk_row(place_ref, 1, start))[0]
            along_z = factors(chunk_row(place_ref, 2, start))[0]
            masses = chunk_row(place_ref, 3, start)
            along_y = (masses * along_y).astype(jnp.bfloat16)
            line_ref[part] = along_z.astype(jnp.bfloat16).astype(jnp.float32)
            for z in range(EDGE):
                line = jnp.broadcast_to(line_ref[part, pl.ds(z, 1), :], (EDGE, CHUNK))
                plane_ref[part, pl.ds(z * EDGE, EDGE), :] = line.astype(jnp.bfloat16) * along_x
            out_ref[0] += lax.dot_general(
                along_y,
                plane_ref[part],
                (((1,), (1,)), ((), ())),
                preferred_element_type=jnp.float32,
            )

    for copy in range(1, out_ref.shape[0]):
        out_ref[copy] = out_ref[0]


def pull_kernel(got_ref, parts_ref, target_ref, out_ref, place_ref, line_ref, plane_ref, row_ref, sum_ref):
    unpack_rows(got_ref, place_ref)
    per = plane_ref.shape[0]
    rows = CHUNK // LANES
    target = target_ref[...]
    density = (parts_ref[0] + parts_ref[2]) + (parts_ref[1] + parts_ref[3])
    wide = target.astype(jnp.float32)
    high = density.astype(jnp.bfloat16)
    rest = density - high.astype(jnp.float32)
    middle = rest.astype(jnp.bfloat16)
    low = (rest - middle.astype(jnp.float32)).astype(jnp.bfloat16)
    row_ref[0:EDGE] = target
    row_ref[EDGE : 2 * EDGE] = high
    row_ref[2 * EDGE : 3 * EDGE] = middle
    row_ref[3 * EDGE : 4 * EDGE] = low

    @pl.loop(0, place_ref.shape[1] // (rows * per))
    def _(step):
        for part in range(per):
            start = (step * per + part) * rows
            profile_x, slope_x = factors(chunk_row(place_ref, 0, start))
            profile_y, slope_y = factors(chunk_row(place_ref, 1, start))
            profile_z, slope_z = factors(chunk_row(place_ref, 2, start))
            masses = chunk_row(place_ref, 3, start)
            profile_x = profile_x.astype(jnp.bfloat16)
            slope_x = slope_x.astype(jnp.bfloat16)
            along_y = (masses * profile_y).astype(jnp.bfloat16).astype(jnp.float32)
            slope_y = (masses * slope_y).astype(jnp.bfloat16).astype(jnp.float32)
            line_ref[part, 0] = profile_z.astype(jnp.bfloat16).astype(jnp.float32)
            line_ref[part, 1] = slope_z.astype(jnp.bfloat16).astype(jnp.float32)
            for z in range(EDGE):
                line = jnp.broadcast_to(line_ref[part, 0, pl.ds(z, 1), :], (EDGE, CHUNK))
                slope_line = jnp.broadcast_to(line_ref[part, 1, pl.ds(z, 1), :], (EDGE, CHUNK))
                line = line.astype(jnp.bfloat16)
                slope_line = slope_line.astype(jnp.bfloat16)
                place = pl.ds(z * EDGE, EDGE)
                plane_ref[part, place, pl.ds(0, CHUNK)] = line * slope_x
                plane_ref[part, place, pl.ds(CHUNK, CHUNK)] = line * profile_x
                plane_ref[part, place, pl.ds(2 * CHUNK, CHUNK)] = slope_line * profile_x
            for component, weight in enumerate((along_y, slope_y, along_y)):
                pulled = jnp.dot(
                    row_ref[...],
                    plane_ref[part, :, pl.ds(component * CHUNK, CHUNK)],
                    preferred_element_type=jnp.float32,
                )
                model = (pulled[EDGE : 2 * EDGE] + pulled[2 * EDGE : 3 * EDGE]) + pulled[3 * EDGE :]
                sums = (
                    jnp.sum(pulled[:EDGE] * weight, axis=0, keepdims=True),
                    jnp.sum(model * weight, axis=0, keepdims=True),
                )
                for kind in range(2):
                    for i in range(rows):
                        sum_ref[kind, component, pl.ds(start + i, 1), :] = sums[kind][
                            :, i * LANES : (i + 1) * LANES
                        ]

    pairs = place_ref.shape[1]
    left = lax.broadcasted_iota(jnp.int32, (pairs, LANES), 1) < LANES // 2
    for component in range(3):
        first, second = sum_ref[0, component], sum_ref[1, component]
        out_ref[pl.ds(component, pairs, stride=8), :] = jnp.where(
            left, first, pltpu.roll(second, LANES // 2, 1)
        )
        out_ref[pl.ds(4 + component, pairs, stride=8), :] = jnp.where(
            left, pltpu.roll(first, LANES // 2, 1), second
        )
    lane = lax.broadcasted_iota(jnp.int32, (2 * pairs, LANES), 1)
    totals = jnp.zeros((2 * pairs, LANES), jnp.float32)
    for place, product in enumerate((density * wide, density * density, wide * wide)):
        totals = jnp.where(lane == place, jnp.sum(product), totals)
    out_ref[pl.ds(3, 2 * pairs, stride=4), :] = totals


def splat(got, copies):
    pairs = got.shape[0] // 4
    return pl.pallas_call(
        splat_kernel,
        out_shape=jax.ShapeDtypeStruct((copies, EDGE, PLANE), jnp.float32),
        in_specs=[pl.BlockSpec(memory_space=pltpu.VMEM)],
        out_specs=pl.BlockSpec(memory_space=pltpu.VMEM),
        scratch_shapes=[
            pltpu.VMEM((4, pairs, LANES), jnp.float32),
            pltpu.VMEM((2, EDGE, CHUNK), jnp.float32),
            pltpu.VMEM((2, PLANE, CHUNK), jnp.bfloat16),
        ],
        compiler_params=pltpu.CompilerParams(vmem_limit_bytes=32 * 2**20),
        cost_estimate=pl.CostEstimate(flops=2**29, bytes_accessed=2**20, transcendentals=2**20),
        name="splat",
    )(got)


def pull(got, parts, target):
    pairs = got.shape[0] // 4
    return pl.pallas_call(
        pull_kernel,
        out_shape=jax.ShapeDtypeStruct((8 * pairs, LANES), jnp.float32),
        in_specs=[pl.BlockSpec(memory_space=pltpu.VMEM)] * 3,
        out_specs=pl.BlockSpec(memory_space=pltpu.VMEM),
        scratch_shapes=[
            pltpu.VMEM((4, pairs, LANES), jnp.float32),
            pltpu.VMEM((2, 2, EDGE, CHUNK), jnp.float32),
            pltpu.VMEM((2, PLANE, 3 * CHUNK), jnp.bfloat16),
            pltpu.VMEM((4 * EDGE, PLANE), jnp.bfloat16),
            pltpu.VMEM((2, 3, pairs, LANES), jnp.float32),
        ],
        compiler_params=pltpu.CompilerParams(vmem_limit_bytes=32 * 2**20),
        cost_estimate=pl.CostEstimate(flops=2**32, bytes_accessed=2**20, transcendentals=2**20),
        name="pull",
    )(got, parts, target)


TILE_AXES = ("y", "z", "core")


def exchange(values, axes):
    return lax.all_to_all(values, axes, split_axis=0, concat_axis=0, tiled=True)


def sum_over(values, axes):
    copies = jnp.broadcast_to(values[None], (lax.axis_size(axes),) + values.shape)
    return jnp.sum(exchange(copies, axes), axis=0)


def on_device(coords, weights, mode_vectors, amplitudes, density_map, block_tiles, block_offsets):
    atoms_per = ATOM_BLOCK
    a_dev = coords.shape[1]
    block_count, per_block = block_tiles.shape
    entry_count = block_count * per_block
    n_tile = lax.axis_size(TILE_AXES)
    n_seg = lax.axis_size("seg")
    modes_flat = mode_vectors.reshape(mode_vectors.shape[0], 3 * a_dev)
    displacement = jnp.dot(
        amplitudes.astype(jnp.bfloat16)[None, :], modes_flat, preferred_element_type=jnp.float32
    ).reshape(3, a_dev)
    bundle = jnp.concatenate([coords + displacement, weights[None, :]], axis=0)
    tile_ids = block_tiles.reshape(entry_count)
    offsets_f = block_offsets.reshape(entry_count, 3).astype(jnp.float32)
    ordinal = jnp.arange(entry_count, dtype=jnp.int32)
    earlier = (ordinal[None, :] < ordinal[:, None]) & (tile_ids[None, :] == tile_ids[:, None])
    rank = jnp.sum(earlier.astype(jnp.int32), axis=1)
    tiles = jnp.arange(n_tile, dtype=jnp.int32)
    chosen = (
        (tile_ids[None, None, :] == tiles[None, :, None])
        & (rank[None, None, :] == jnp.arange(2, dtype=jnp.int32)[:, None, None])
    ).astype(jnp.float32)
    by_block = jnp.transpose(bundle.reshape(4, block_count, atoms_per), (1, 0, 2))
    shift = jnp.concatenate([offsets_f, jnp.zeros((entry_count, 1), jnp.float32)], axis=1)
    rows = jnp.repeat(by_block, per_block, axis=0) + shift[:, :, None]
    send = jnp.einsum("rte,eca->tcra", chosen, rows, precision=lax.Precision.HIGHEST)
    got = exchange(send.reshape(n_tile, 2, LANES), TILE_AXES).reshape(2 * n_tile, LANES)

    target = jnp.transpose(density_map.reshape(PLANE, EDGE))
    parts = exchange(splat(got, n_seg), "seg")
    pulled = pull(got, parts, target)
    back = exchange(pulled.reshape(n_tile, 4, LANES), TILE_AXES)

    voxels = float(n_tile * EDGE**3)
    totals = jnp.sum(back[:, 3, :3], axis=0)
    root = jnp.sqrt(totals[1] * totals[2])
    correlation = totals[0] / root
    half = LANES // 2
    slot_forces = voxels * (
        back[:, :3, :half] / root - correlation * back[:, :3, half:] / totals[1]
    ).reshape(n_tile, 3, 2, atoms_per)
    to_block = jnp.sum(chosen.reshape(2, n_tile, block_count, per_block), axis=3)
    forces = jnp.einsum(
        "rtb,tcra->cba", to_block, slot_forces, precision=lax.Precision.HIGHEST
    ).reshape(3, a_dev)
    partial_modes = jnp.dot(
        modes_flat,
        forces.astype(jnp.bfloat16).reshape(3 * a_dev),
        preferred_element_type=jnp.float32,
    )
    total_atoms = a_dev * n_tile * n_seg
    mode_sum = sum_over(sum_over(partial_modes.reshape(2, LANES), ("z", "core")), ("y", "seg"))
    mode_grad = mode_sum.reshape(-1) / jnp.sqrt(jnp.float32(total_atoms))
    return (forces, mode_grad, correlation)


def solution(mesh):
    split = Mesh(mesh.devices.reshape(8, 8, 2, 4), TILE_AXES + ("seg",))
    every = TILE_AXES + ("seg",)
    return jax.shard_map(
        on_device,
        mesh=split,
        in_specs=(
            P(None, every),
            P(every),
            P(None, None, every),
            P(),
            P(TILE_AXES, None),
            P(every, None),
            P(every, None, None),
        ),
        out_specs=(P(None, every), P(), P()),
        check_vma=False,
    )
```

time: 311 us -> 122 us (0.39)
  starting transfers between devices: 79.9 us -> 15.4 us
  other arithmetic: 63.3 us -> 2.94 us
  local copies, waits for them, and re-layouts: 67.3 us -> 7.06 us
  blocking collectives: 0 us -> 42.3 us
  matrix products: 33.7 us -> 1.69 us
  waiting for transfers between devices: 59.3 us -> 29.4 us
  Pallas kernels: 0 us -> 18.9 us
    reshape x15 -> x4, local copies, waits for them, and re-layouts: 59.6 us -> 1.08 us  [the longest x1 0.7 us: on_device(): forces = jnp.einsum('rtb,tcra->cba', to_block, slot_forces, precision=lax...]
    reduce_sum x20 -> x5, other arithmetic: 46.9 us -> 0.51 us  [the longest x1 0.18 us: on_device(): rank = jnp.sum(earlier.astype(jnp.int32), axis=1)]
    all_to_all x0 -> x2, blocking collectives: none -> 42.3 us  [exchange(): return lax.all_to_all(values, axes, split_axis=0, concat_axis=0, tiled=True)]
    ppermute x13 -> x0, starting transfers between devices: 41.1 us -> none  [the longest x6 21.2 us: ring_sum(): lax.ppermute(values, axis, [(i, (i + k) % size) for i in range(size)])]
    dot_general x18 -> x2, matrix products: 32.7 us -> 0.68 us  [the longest x1 0.45 us: on_device(): jnp.einsum('rte,eca->tcra', chosen, rows, precision=lax.Precision.HIGHEST)]
    ppermute x13 -> x0, waiting for transfers between devices: 23.5 us -> none  [the longest x7 20.5 us: swap_over(): return lax.ppermute(values, axis, [(i, i ^ mask) for i in range(size)])]
    all_to_all x3, starting transfers between devices: 38.9 us -> 15.4 us  [exchange(): return lax.all_to_all(values, axes, split_axis=0, concat_axis=0, tiled=True)]
    pallas_call x0 -> x2, Pallas kernels: none -> 18.9 us  [the longest x1 11 us: pull(): pl.pallas_call(pull_kernel, out_shape=jax.ShapeDtypeStruct((8 * pairs, LA...]
  transfers between devices with their start and end apart: 16 -> 3, of which waited for: 12 -> 3; matrix products, arithmetic and copies ran while one was open for 1% -> 1% of each run, Pallas kernels for 0% -> 0%
where the time goes in v2:
time: 122 us
  blocking collectives  42.3 us (35%)
  waiting for transfers between devices  29.4 us (24%)
  Pallas kernels  18.9 us (15%)
  starting transfers between devices  15.4 us (13%)
  local copies, waits for them, and re-layouts  7.06 us (6%)
  between operations  3.96 us (3%)
  other arithmetic  2.94 us (2%)
  matrix products  1.69 us (1%)
    all_to_all x2, blocking collectives, exchange(): return lax.all_to_all(values, axes, split_axis=0, concat_axis=0, tiled=True)  42.3 us
    all_to_all x3, waiting for transfers between devices, exchange(): return lax.all_to_all(values, axes, split_axis=0, concat_axis=0, tiled=True)  29.4 us
    all_to_all x3, starting transfers between devices, exchange(): return lax.all_to_all(values, axes, split_axis=0, concat_axis=0, tiled=True)  15.4 us
    pallas_call x1, Pallas kernels, pull(): pl.pallas_call(pull_kernel, out_shape=jax.ShapeDtypeStruct((8 * pairs, LA...  11 us
    pallas_call x1, Pallas kernels, splat(): pl.pallas_call(splat_kernel, out_shape=jax.ShapeDtypeStruct((copies, EDGE...  7.96 us
    unnamed x14, local copies, waits for them, and re-layouts  2.92 us
  transfers between devices with their start and end apart: 3, of which 3 were waited for; matrix products, arithmetic and copies ran while one was open for 1% of the time, Pallas kernels for 0%

profile of v2, /device:TPU:1, one launch (start us, length us, event | category | flops | bytes accessed | tf_op | source)
XLA Modules:
  0.0 121.7 jit_solution(6587984891183913075)
XLA Ops:
  0.6 0.8 copy.61
  1.4 0.1 eq.65
  1.5 0.2 convert_reduce_fusion.1
  1.7 0.8 concatenate.12
  2.5 0.7 convert_element_type.22
  3.2 1.7 %copy.59 = bf16[256,3,1024]{0,2,1:T(8,128)(2,1)S(1)} copy(bf16[256,3,1024]{2,0,1:T(8,128)(2,1)} %param.9) | data formatting | bytes 3145728 | tf_op args[2]
  4.9 0.0 copy-start.2
  4.9 0.0 copy-start.4
  4.9 0.5 fusion.2
  5.4 0.2 copy-done.2
  5.6 0.1 concatenate.11
  5.7 0.0 copy-done.4
  5.7 0.1 copy.60
  5.8 0.1 convert_element_type.24
  6.0 0.5 fusion.4
  6.5 0.1 copy.63
  6.6 30.7 %all_to_all.25 = f32[128,2,128]{2,1,0:T(2,128)S(1)} all-to-all(f32[128,2,128]{2,1,0:T(2,128)S(1)} %copy.63), channel_id=1, replica_groups=mesh['y'=8,'z'=8,'core'=2,'seg'=4] {'y','z','core'}, dimensions={0} | all-to-all | bytes 262144 | tf_op jit(solution)/shard_map/all_to_all | solution.py:185
  37.3 8.0 %splat.1 = f32[4,32,1024]{2,1,0:T(8,128)} custom-call(f32[256,128]{1,0:T(8,128)S(1)} %bitcast.55), custom_call_target="tpu_custom_call" | custom-call | flops 536870912 | bytes 1048576 | tf_op jit(solution)/shard_map/splat/pallas_call | solution.py:145
  45.2 4.0 %all-to-all-start.1 = ((f32[4,32,1024]{2,1,0:T(8,128)}), f32[4,32,1024]{2,1,0:T(8,128)S(1)}, u32[]{:S(2)}, u32[]{:S(2)}) async-start(f32[4,32,1024]{2,1,0:T(8,128)} %splat.1), calls=%async_computation.1 | async-start | bytes 1048576 | tf_op jit(solution)/shard_map/all_to_all | solution.py:185
  49.3 0.1 eq.77
  49.4 0.4 reduce.1
  49.7 0.2 reshape.120
  49.9 0.1 copy.64
  50.0 0.1 copy.67
  50.1 7.3 %all-to-all-done.1.parts_ref = f32[4,32,1024]{2,1,0:T(8,128)S(1)} async-done(((f32[4,32,1024]{2,1,0:T(8,128)}), f32[4,32,1024]{2,1,0:T(8,128)S(1)}, u32[]{:S(2)}, u32[]{:S(2)}) %all-to-all-start.1) | async-done | bytes 524320 | tf_op jit(solution)/shard_map/all_to_all | solution.py:185
  57.4 11.0 %pull.1 = f32[512,128]{1,0:T(8,128)} custom-call(f32[256,128]{1,0:T(8,128)S(1)} %bitcast.56, f32[4,32,1024]{2,1,0:T(8,128)S(1)} %all-to-all-done.1.parts_ref, bf16[32,1024]{1,0:T(8,128)(2,1)S(1)} %bitcast.57), custom_call_target="tpu_custom_call" | custom-call | flops 4294967296 | bytes 1048576 | tf_op jit(solution)/shard_map/pull/pallas_call | solution.py:163
  68.4 7.5 %all-to-all-start.2 = ((f32[128,4,128]{2,1,0:T(4,128)}), f32[128,4,128]{2,1,0:T(4,128)S(1)}, u32[]{:S(2)}, u32[]{:S(2)}) async-start(f32[128,4,128]{2,1,0:T(4,128)} %bitcast.12), calls=%async_computation.2 | async-start | bytes 524288 | tf_op jit(solution)/shard_map/all_to_all | solution.py:185
  76.0 0.1 iota_compare_fusion
  76.1 0.1 convert_reduce_fusion
  76.2 14.1 %all-to-all-done.2 = f32[128,4,128]{2,1,0:T(4,128)S(1)} async-done(((f32[128,4,128]{2,1,0:T(4,128)}), f32[128,4,128]{2,1,0:T(4,128)S(1)}, u32[]{:S(2)}, u32[]{:S(2)}) %all-to-all-start.2) | async-done | bytes 262176 | tf_op jit(solution)/shard_map/all_to_all | solution.py:185
  90.3 0.2 fusion.14
  90.5 0.1 copy.81
  90.7 0.1 copy.80
  90.8 0.2 slice_reduce_fusion
  90.9 0.6 fusion.15
  93.5 0.7 subtract_multiply_fusion
  94.2 0.2 fusion.16
  94.4 0.1 copy.69
  94.5 0.1 reshape.134
  94.6 0.0 copy-done
  94.6 0.5 fusion
  95.1 11.6 %all_to_all.26 = f32[16,2,128]{2,1,0:T(2,128)S(1)} all-to-all(f32[16,2,128]{2,1,0:T(2,128)S(1)} %broadcast_in_dim.7), channel_id=1, replica_groups=mesh['y'=8,'z'=8,'core'=2,'seg'=4] {'z','core'}, dimensions={0} | all-to-all | bytes 32768 | tf_op jit(solution)/shard_map/all_to_all | solution.py:185
  106.8 0.6 broadcast_in_dim.8
  107.4 3.9 %all-to-all-start.4 = ((f32[32,2,128]{2,1,0:T(2,128)}), f32[32,2,128]{2,1,0:T(2,128)S(1)}, u32[]{:S(2)}, u32[]{:S(2)}) async-start(f32[32,2,128]{2,1,0:T(2,128)} %broadcast_in_dim.8), calls=%async_computation.4 | async-start | bytes 65536 | tf_op jit(solution)/shard_map/all_to_all | solution.py:185
  111.2 0.1 copy.68
  111.3 0.7 reshape.122
  112.0 7.9 %all-to-all-done.4 = f32[32,2,128]{2,1,0:T(2,128)S(1)} async-done(((f32[32,2,128]{2,1,0:T(2,128)}), f32[32,2,128]{2,1,0:T(2,128)S(1)}, u32[]{:S(2)}, u32[]{:S(2)}) %all-to-all-start.4) | async-done | bytes 32800 | tf_op jit(solution)/shard_map/all_to_all | solution.py:185
  120.0 0.6 multiply_bitcast_fusion
  (17 shorter events, 0.2 us)
Async XLA Ops:
  4.9 0.7 copy-start.2
  4.9 0.8 copy-start.4
  37.3 12.1 %copy-start.1 = (bf16[1,32768]{1,0:T(2,128)(2,1)S(1)}, bf16[1,32768]{1,0:T(2,128)(2,1)}, u32[]{:S(2)}) copy-start(bf16[1,32768]{1,0:T(2,128)(2,1)} %param.11) | copy-start | bytes 196612
  45.2 12.2 %all-to-all-start.1 = ((f32[4,32,1024]{2,1,0:T(8,128)}), f32[4,32,1024]{2,1,0:T(8,128)S(1)}, u32[]{:S(2)}, u32[]{:S(2)}) async-start(f32[4,32,1024]{2,1,0:T(8,128)} %splat.1), calls=%async_computation.1 | async-start | bytes 1048576 | tf_op jit(solution)/shard_map/all_to_all | solution.py:185
  57.4 18.6 %copy-start.3 = (s32[32,4]{0,1:T(4,128)S(1)}, s32[32,4]{0,1:T(4,128)}, u32[]{:S(2)}) copy-start(s32[32,4]{0,1:T(4,128)} %param.12) | copy-start | bytes 1540
  68.4 26.2 %copy-start = (bf16[256,3,1024]{2,0,1:T(8,128)(2,1)S(1)}, bf16[256,3,1024]{2,0,1:T(8,128)(2,1)}, u32[]{:S(2)}) copy-start(bf16[256,3,1024]{2,0,1:T(8,128)(2,1)} %param.9) | copy-start | bytes 4718596
  68.4 21.9 %all-to-all-start.2 = ((f32[128,4,128]{2,1,0:T(4,128)}), f32[128,4,128]{2,1,0:T(4,128)S(1)}, u32[]{:S(2)}, u32[]{:S(2)}) async-start(f32[128,4,128]{2,1,0:T(4,128)} %bitcast.12), calls=%async_computation.2 | async-start | bytes 524288 | tf_op jit(solution)/shard_map/all_to_all | solution.py:185
  107.4 12.6 %all-to-all-start.4 = ((f32[32,2,128]{2,1,0:T(2,128)}), f32[32,2,128]{2,1,0:T(2,128)S(1)}, u32[]{:S(2)}, u32[]{:S(2)}) async-start(f32[32,2,128]{2,1,0:T(2,128)} %broadcast_in_dim.8), calls=%async_computation.4 | async-start | bytes 65536 | tf_op jit(solution)/shard_map/all_to_all | solution.py:185

commit v3 on v2

v3 whole, which is shorter than its diff:
```python
import jax
import jax.numpy as jnp
from jax import lax
from jax.experimental import pallas as pl
from jax.experimental.pallas import tpu as pltpu
from jax.sharding import Mesh
from jax.sharding import PartitionSpec as P

EDGE = 32
ATOM_BLOCK = 32
PLANE = EDGE * EDGE
LANES = 128
CHUNK = 256

inverse_var = 1.0 / 2.25


def factors(places):
    centers = lax.broadcasted_iota(jnp.int32, (EDGE, places.shape[1]), 0).astype(jnp.float32) + 0.5
    distance = centers - places
    profile = jnp.exp(-0.5 * inverse_var * distance * distance)
    return profile, inverse_var * distance * profile


def exact_parts(values):
    high = values.astype(jnp.bfloat16)
    rest = values - high.astype(jnp.float32)
    middle = rest.astype(jnp.bfloat16)
    return high, middle, (rest - middle.astype(jnp.float32)).astype(jnp.bfloat16)


def against_rows(left, right):
    return lax.dot_general(
        left, right, (((1,), (1,)), ((), ())), preferred_element_type=jnp.float32
    )


def quarter_of(shape):
    return lax.broadcasted_iota(jnp.int32, shape, 1) // ATOM_BLOCK


def regroup(rows, target):
    quarter = quarter_of(rows[0].shape)
    result = jnp.zeros_like(rows[0])
    for i in range(4):
        moved = pltpu.roll(rows[i], ((i - target) % 4) * ATOM_BLOCK, 1) if i != target else rows[i]
        result = jnp.where(quarter == i, moved, result)
    return result


def pack_kernel(*refs):
    sources, (send_ref, pick_ref), (cell_ref, block_ref) = refs[:6], refs[6:8], refs[8:10]
    local, sems = refs[10:16], refs[16]
    copies = [
        pltpu.make_async_copy(source, place, sems.at[i])
        for i, (source, place) in enumerate(zip(sources, local))
    ]
    for copy in copies:
        copy.start()
    tiles_ref, offsets_ref, amps_ref, coords_ref, weights_ref, modes_ref = local
    n_tile = send_ref.shape[0] // 2
    blocks = block_ref.shape[0]
    cells = cell_ref.shape[1]
    for copy in copies[:2]:
        copy.wait()
    shape = (n_tile, blocks)
    tile_of_row = lax.broadcasted_iota(jnp.int32, shape, 0)
    row = lax.broadcasted_iota(jnp.int32, (blocks, blocks), 0)
    column = lax.broadcasted_iota(jnp.int32, (blocks, blocks), 1)
    before = jnp.where(row < column, 1.0, 0.0).astype(jnp.bfloat16)
    same = jnp.where(row == column, 1.0, 0.0).astype(jnp.bfloat16)
    ones = jnp.ones((blocks, blocks), jnp.bfloat16)
    seen = jnp.zeros(shape, jnp.float32)
    picks = [jnp.zeros(shape, jnp.float32) for _ in range(2)]
    shifts = [jnp.zeros((n_tile, LANES), jnp.float32) for _ in range(2)]
    for k in range(tiles_ref.shape[0]):
        named = jnp.where(tiles_ref[pl.ds(k, 1), :] == tile_of_row, 1.0, 0.0)
        flags = named.astype(jnp.bfloat16)
        rank = seen + jnp.dot(flags, before, preferred_element_type=jnp.float32)
        seen = seen + jnp.dot(flags, ones, preferred_element_type=jnp.float32)
        offsets = [
            jnp.broadcast_to(offsets_ref[c, pl.ds(k, 1), :].astype(jnp.float32), (ATOM_BLOCK, blocks))
            for c in range(3)
        ]
        offsets = jnp.concatenate(offsets + [jnp.zeros((ATOM_BLOCK, blocks), jnp.float32)], axis=0)
        for slot in range(2):
            mine = jnp.where(rank == float(slot), named, 0.0)
            picks[slot] = picks[slot] + mine
            shifts[slot] = shifts[slot] + against_rows(
                mine.astype(jnp.bfloat16), offsets.astype(jnp.bfloat16)
            )
    for copy in copies[2:]:
        copy.wait()
    amps = jnp.broadcast_to(amps_ref[...], (16, amps_ref.shape[1])).astype(jnp.bfloat16)
    for component in range(3):
        moved = jnp.dot(amps, modes_ref[component], preferred_element_type=jnp.float32)
        places = coords_ref[pl.ds(component, 1), :] + moved[0:1]
        for cell in range(cells):
            cell_ref[component, pl.ds(cell, 1), :] = places[:, cell * LANES : (cell + 1) * LANES]
    cell_ref[3] = weights_ref[...]
    for i in range(4):
        block_ref[pl.ds(i, cells, stride=4), :] = regroup([cell_ref[c] for c in range(4)], i)
    parts = exact_parts(block_ref[...])
    for slot in range(2):
        pick = picks[slot].astype(jnp.bfloat16)
        high, middle, low = [jnp.dot(pick, part, preferred_element_type=jnp.float32) for part in parts]
        send_ref[pl.ds(slot, n_tile, stride=2), :] = ((high + middle) + low) + shifts[slot]
        pick_ref[slot] = against_rows(same, pick).astype(jnp.bfloat16)


def finish_kernel(voxels, atoms, back_ref, pick_ref, modes_ref, forces_ref, spread_ref, score_ref, block_ref):
    n_tile = pick_ref.shape[2]
    lane = lax.broadcasted_iota(jnp.int32, (1, LANES), 1)
    totals = jnp.sum(back_ref[pl.ds(3, n_tile, stride=4), :], axis=0, keepdims=True)
    srm, srr, smm = [
        jnp.sum(jnp.where(lane == i, totals, 0.0), axis=1, keepdims=True) for i in range(3)
    ]
    root = jnp.sqrt(srr * smm)
    score = srm / root
    score_ref[...] = jnp.broadcast_to(score, score_ref.shape)
    map_scale = voxels / root
    model_scale = voxels * (score / srr)
    cells = forces_ref.shape[1] // LANES
    modes = jnp.zeros((1, modes_ref.shape[1]), jnp.float32)
    for component in range(3):
        pulled = back_ref[pl.ds(component, n_tile, stride=4), :]
        pulled = pulled * map_scale - pltpu.roll(pulled, LANES // 2, 1) * model_scale
        parts = exact_parts(pulled)
        first, second = [
            sum([jnp.dot(pick_ref[slot], part, preferred_element_type=jnp.float32) for part in parts[::-1]])
            for slot in range(2)
        ]
        block_ref[component] = first + pltpu.roll(second, LANES - ATOM_BLOCK, 1)
        rows = regroup([block_ref[component, pl.ds(i, cells, stride=4), :] for i in range(4)], 0)
        for cell in range(cells):
            forces_ref[pl.ds(component, 1), cell * LANES : (cell + 1) * LANES] = rows[cell : cell + 1]
        force = jnp.broadcast_to(forces_ref[pl.ds(component, 1), :], (16, forces_ref.shape[1]))
        modes = modes + against_rows(force.astype(jnp.bfloat16), modes_ref[component])[0:1]
    modes = modes / jnp.sqrt(jnp.float32(atoms))
    half = spread_ref.shape[0] // 2
    for part in range(2):
        spread_ref[pl.ds(part, half, stride=2), :] = jnp.broadcast_to(
            modes[:, part * LANES : (part + 1) * LANES], (half, LANES)
        )


def unpack_rows(got_ref, place_ref):
    groups = got_ref.shape[0] // 4
    rows = [got_ref[pl.ds(i, groups, stride=4), :] for i in range(4)]
    for component in range(4):
        place_ref[component] = regroup(rows, component)


def chunk_row(place_ref, component, chunk):
    rows = CHUNK // LANES
    return jnp.concatenate(
        [place_ref[component, pl.ds(chunk * rows + i, 1), :] for i in range(rows)], axis=1
    )


def pipeline(chunks, build, use):
    build(0, 0)

    @pl.loop(0, chunks // 2)
    def _(step):
        build(1, 2 * step + 1)
        use(0, 2 * step)
        build(0, jnp.minimum(2 * step + 2, chunks - 1))
        use(1, 2 * step + 1)


def splat_kernel(got_ref, out_ref, place_ref, line_ref, weight_ref, plane_ref):
    unpack_rows(got_ref, place_ref)
    out_ref[0] = jnp.zeros_like(out_ref[0])

    def build(slot, chunk):
        along_x = factors(chunk_row(place_ref, 0, chunk))[0].astype(jnp.bfloat16)
        along_y = factors(chunk_row(place_ref, 1, chunk))[0]
        along_z = factors(chunk_row(place_ref, 2, chunk))[0]
        weight_ref[slot] = (chunk_row(place_ref, 3, chunk) * along_y).astype(jnp.bfloat16)
        line_ref[slot] = along_z.astype(jnp.bfloat16).astype(jnp.float32)
        for z in range(EDGE):
            line = jnp.broadcast_to(line_ref[slot, pl.ds(z, 1), :], (EDGE, CHUNK))
            plane_ref[slot, pl.ds(z * EDGE, EDGE), :] = line.astype(jnp.bfloat16) * along_x

    def use(slot, chunk):
        out_ref[0] += against_rows(weight_ref[slot], plane_ref[slot])

    pipeline(place_ref.shape[1] * LANES // CHUNK, build, use)
    for copy in range(1, out_ref.shape[0]):
        out_ref[copy] = out_ref[0]


def pull_kernel(got_ref, parts_ref, target_ref, out_ref, place_ref, line_ref, weight_ref, plane_ref, row_ref, sum_ref):
    unpack_rows(got_ref, place_ref)
    target = target_ref[...]
    density = (parts_ref[0] + parts_ref[2]) + (parts_ref[1] + parts_ref[3])
    wide = target.astype(jnp.float32)
    high, middle, _ = exact_parts(density)
    row_ref[0:EDGE] = target
    row_ref[EDGE : 2 * EDGE] = high
    row_ref[2 * EDGE : 3 * EDGE] = middle

    def build(slot, chunk):
        profile_x, slope_x = factors(chunk_row(place_ref, 0, chunk))
        profile_y, slope_y = factors(chunk_row(place_ref, 1, chunk))
        profile_z, slope_z = factors(chunk_row(place_ref, 2, chunk))
        masses = chunk_row(place_ref, 3, chunk)
        profile_x = profile_x.astype(jnp.bfloat16)
        slope_x = slope_x.astype(jnp.bfloat16)
        weight_ref[slot, 0] = (masses * profile_y).astype(jnp.bfloat16).astype(jnp.float32)
        weight_ref[slot, 1] = (masses * slope_y).astype(jnp.bfloat16).astype(jnp.float32)
        line_ref[slot, 0] = profile_z.astype(jnp.bfloat16).astype(jnp.float32)
        line_ref[slot, 1] = slope_z.astype(jnp.bfloat16).astype(jnp.float32)
        for z in range(EDGE):
            line = jnp.broadcast_to(line_ref[slot, 0, pl.ds(z, 1), :], (EDGE, CHUNK))
            slope_line = jnp.broadcast_to(line_ref[slot, 1, pl.ds(z, 1), :], (EDGE, CHUNK))
            line = line.astype(jnp.bfloat16)
            slope_line = slope_line.astype(jnp.bfloat16)
            place = pl.ds(z * EDGE, EDGE)
            plane_ref[slot, place, pl.ds(0, CHUNK)] = line * slope_x
            plane_ref[slot, place, pl.ds(CHUNK, CHUNK)] = line * profile_x
            plane_ref[slot, place, pl.ds(2 * CHUNK, CHUNK)] = slope_line * profile_x

    def use(slot, chunk):
        rows = CHUNK // LANES
        for component, weight in enumerate((0, 1, 0)):
            pulled = jnp.dot(
                row_ref[...],
                plane_ref[slot, :, pl.ds(component * CHUNK, CHUNK)],
                preferred_element_type=jnp.float32,
            )
            weight = weight_ref[slot, weight]
            model = pulled[EDGE : 2 * EDGE] + pulled[2 * EDGE :]
            sums = (
                jnp.sum(pulled[:EDGE] * weight, axis=0, keepdims=True),
                jnp.sum(model * weight, axis=0, keepdims=True),
            )
            for kind in range(2):
                for i in range(rows):
                    sum_ref[kind, component, pl.ds(chunk * rows + i, 1), :] = sums[kind][
                        :, i * LANES : (i + 1) * LANES
                    ]

    pipeline(place_ref.shape[1] * LANES // CHUNK, build, use)
    pairs = place_ref.shape[1]
    left = lax.broadcasted_iota(jnp.int32, (pairs, LANES), 1) < LANES // 2
    for component in range(3):
        first, second = sum_ref[0, component], sum_ref[1, component]
        out_ref[pl.ds(component, pairs, stride=8), :] = jnp.where(
            left, first, pltpu.roll(second, LANES // 2, 1)
        )
        out_ref[pl.ds(4 + component, pairs, stride=8), :] = jnp.where(
            left, pltpu.roll(first, LANES // 2, 1), second
        )
    lane = lax.broadcasted_iota(jnp.int32, (2 * pairs, LANES), 1)
    totals = jnp.zeros((2 * pairs, LANES), jnp.float32)
    for place, product in enumerate((density * wide, density * density, wide * wide)):
        totals = jnp.where(lane == place, jnp.sum(product), totals)
    out_ref[pl.ds(3, 2 * pairs, stride=4), :] = totals


def call(kernel, name, out_shape, scratch, flops, *operands, source=pltpu.VMEM, limit=32):
    vmem = pl.BlockSpec(memory_space=pltpu.VMEM)
    return pl.pallas_call(
        kernel,
        out_shape=out_shape,
        in_specs=[pl.BlockSpec(memory_space=source)] * len(operands),
        out_specs=jax.tree.map(lambda _: vmem, out_shape),
        scratch_shapes=[pltpu.VMEM(*entry) if isinstance(entry, tuple) else entry for entry in scratch],
        compiler_params=pltpu.CompilerParams(vmem_limit_bytes=limit * 2**20),
        cost_estimate=pl.CostEstimate(flops=flops, bytes_accessed=2**20, transcendentals=2**20),
        name=name,
    )(*operands)


def pack(coords, weights, modes, amplitudes, tiles, offsets, n_tile):
    blocks = tiles.shape[1]
    operands = (tiles, offsets, amplitudes, coords, weights, modes)
    return call(
        pack_kernel,
        "pack",
        (
            jax.ShapeDtypeStruct((2 * n_tile, LANES), jnp.float32),
            jax.ShapeDtypeStruct((2, blocks, n_tile), jnp.bfloat16),
        ),
        [((4, weights.shape[0], LANES), jnp.float32), ((blocks, LANES), jnp.float32)]
        + [(operand.shape, operand.dtype) for operand in operands]
        + [pltpu.SemaphoreType.DMA((len(operands),))],
        2**26,
        *operands,
        source=pltpu.HBM,
        limit=60,
    )


def finish(back, picks, modes, voxels, atoms, copies):
    blocks = picks.shape[1]
    return call(
        lambda *refs: finish_kernel(voxels, atoms, *refs),
        "finish",
        (
            jax.ShapeDtypeStruct((3, modes.shape[2]), jnp.float32),
            jax.ShapeDtypeStruct((2 * copies, LANES), jnp.float32),
            jax.ShapeDtypeStruct((1, LANES), jnp.float32),
        ),
        [((3, blocks, LANES), jnp.float32)],
        2**26,
        back,
        picks,
        modes,
    )


def splat(got, copies):
    groups = got.shape[0] // 4
    return call(
        splat_kernel,
        "splat",
        jax.ShapeDtypeStruct((copies, EDGE, PLANE), jnp.float32),
        [
            ((4, groups, LANES), jnp.float32),
            ((2, EDGE, CHUNK), jnp.float32),
            ((2, EDGE, CHUNK), jnp.bfloat16),
            ((2, PLANE, CHUNK), jnp.bfloat16),
        ],
        2**29,
        got,
    )


def pull(got, parts, target):
    groups = got.shape[0] // 4
    return call(
        pull_kernel,
        "pull",
        jax.ShapeDtypeStruct((8 * groups, LANES), jnp.float32),
        [
            ((4, groups, LANES), jnp.float32),
            ((2, 2, EDGE, CHUNK), jnp.float32),
            ((2, 2, EDGE, CHUNK), jnp.float32),
            ((2, PLANE, 3 * CHUNK), jnp.bfloat16),
            ((3 * EDGE, PLANE), jnp.bfloat16),
            ((2, 3, groups, LANES), jnp.float32),
        ],
        2**32,
        got,
        parts,
        target,
    )


TILE_AXES = ("y", "z", "core")


def exchange(values, axes):
    return lax.all_to_all(values, axes, split_axis=0, concat_axis=0, tiled=True)


def on_device(coords, weights, mode_vectors, amplitudes, density_map, block_tiles, block_offsets):
    a_dev = coords.shape[1]
    n_tile = lax.axis_size(TILE_AXES)
    n_seg = lax.axis_size("seg")
    modes = jnp.transpose(mode_vectors, (1, 0, 2))
    send, picks = pack(
        coords,
        weights.reshape(a_dev // LANES, LANES),
        modes,
        amplitudes.reshape(1, -1),
        block_tiles.T,
        jnp.transpose(block_offsets, (2, 1, 0)),
        n_tile,
    )
    got = exchange(send.reshape(n_tile, 2, LANES), TILE_AXES).reshape(2 * n_tile, LANES)
    target = jnp.transpose(density_map.reshape(PLANE, EDGE))
    parts = exchange(splat(got, n_seg), "seg")
    pulled = pull(got, parts, target)
    back = exchange(pulled.reshape(n_tile, 4, LANES), TILE_AXES).reshape(4 * n_tile, LANES)
    near, far = ("z", "core"), ("y", "seg")
    forces, spread, score = finish(
        back, picks, modes, float(n_tile * EDGE**3), a_dev * n_tile * n_seg, lax.axis_size(near)
    )
    near_sum = jnp.sum(exchange(spread.reshape(-1, 2, LANES), near), axis=0)
    copies = jnp.broadcast_to(near_sum[None], (lax.axis_size(far), 2, LANES))
    mode_grad = jnp.sum(exchange(copies, far), axis=0).reshape(-1)
    return (forces, mode_grad, score[0, 0])


def solution(mesh):
    split = Mesh(mesh.devices.reshape(8, 8, 2, 4), TILE_AXES + ("seg",))
    every = TILE_AXES + ("seg",)
    return jax.shard_map(
        on_device,
        mesh=split,
        in_specs=(
            P(None, every),
            P(every),
            P(None, None, every),
            P(),
            P(TILE_AXES, None),
            P(every, None),
            P(every, None, None),
        ),
        out_specs=(P(None, every), P(), P()),
        check_vma=False,
    )
```

time: 122 us -> 113 us (0.926)
  blocking collectives: 42.3 us -> 75.7 us
  waiting for transfers between devices: 29.4 us -> 7.26 us
  starting transfers between devices: 15.4 us -> 4.01 us
  local copies, waits for them, and re-layouts: 7.06 us -> 0.29 us
  Pallas kernels: 18.9 us -> 24 us
  between operations: 3.96 us -> 0.67 us
  other arithmetic: 2.94 us -> 1 us
  matrix products: 1.69 us -> 0 us
    all_to_all x2 -> x4, blocking collectives: 42.3 us -> 75.7 us  [exchange(): return lax.all_to_all(values, axes, split_axis=0, concat_axis=0, tiled=True)]
    all_to_all x3 -> x1, waiting for transfers between devices: 29.4 us -> 7.26 us  [exchange(): return lax.all_to_all(values, axes, split_axis=0, concat_axis=0, tiled=True)]
    all_to_all x3 -> x1, starting transfers between devices: 15.4 us -> 4.01 us  [exchange(): return lax.all_to_all(values, axes, split_axis=0, concat_axis=0, tiled=True)]
    pallas_call x2 -> x4, Pallas kernels: 18.9 us -> 24 us  [call(): pl.pallas_call(kernel, out_shape=out_shape, in_specs=[pl.BlockSpec(memory...]
    unnamed x14 -> x6, local copies, waits for them, and re-layouts: 2.92 us -> 0.01 us
  transfers between devices with their start and end apart: 3 -> 1, of which waited for: 3 -> 1; matrix products, arithmetic and copies ran while one was open for 1% -> 1% of each run, Pallas kernels for 0% -> 0%
where the time goes in v3:
time: 113 us
  blocking collectives  75.7 us (67%)
  Pallas kernels  24 us (21%)
  waiting for transfers between devices  7.26 us (6%)
  starting transfers between devices  4.01 us (4%)
    all_to_all x4, blocking collectives, exchange(): return lax.all_to_all(values, axes, split_axis=0, concat_axis=0, tiled=True)  75.7 us
    pallas_call x4, Pallas kernels, call(): pl.pallas_call(kernel, out_shape=out_shape, in_specs=[pl.BlockSpec(memory...  24 us
    all_to_all x1, waiting for transfers between devices, exchange(): return lax.all_to_all(values, axes, split_axis=0, concat_axis=0, tiled=True)  7.26 us
    all_to_all x1, starting transfers between devices, exchange(): return lax.all_to_all(values, axes, split_axis=0, concat_axis=0, tiled=True)  4.01 us
  transfers between devices with their start and end apart: 1, of which 1 were waited for; matrix products, arithmetic and copies ran while one was open for 1% of the time, Pallas kernels for 0%

profile of v3, /device:TPU:1, one launch (start us, length us, event | category | flops | bytes accessed | tf_op | source)
XLA Modules:
  0.0 112.9 jit_solution(1097457254768248143)
XLA Ops:
  0.6 2.8 %pack.1 = (f32[256,128]{1,0:T(8,128)}, bf16[2,32,128]{2,1,0:T(8,128)(2,1)}) custom-call(s32[4,32]{1,0:T(4,128)} %bitcast.26, s32[3,4,32]{2,1,0:T(4,128)} %bitcast.24, f32[1,256]{1,0:T(1,128)} %bitcast.27, f32[3,1024]{1,0:T(4,128)} %refs_3_.1, f32[8,128]{1,0:T(8,128)} %bitcast.25, bf16[3,256,1024]{2,1,0:T(8,128)(2,1)} %bitcast.20), custom_call_target="tpu_custom_call" | custom-call | flops 67108864 | bytes 1048576 | tf_op jit(solution)/shard_map/pack/pallas_call | solution.py:265
  3.4 30.6 %all_to_all.25 = f32[128,2,128]{2,1,0:T(2,128)S(1)} all-to-all(f32[128,2,128]{2,1,0:T(2,128)} %bitcast.22), channel_id=1, replica_groups=mesh['y'=8,'z'=8,'core'=2,'seg'=4] {'y','z','core'}, dimensions={0} | all-to-all | bytes 262144 | tf_op jit(solution)/shard_map/all_to_all | solution.py:357
  34.1 0.0 copy-start.2
  34.1 7.8 %splat.1 = f32[4,32,1024]{2,1,0:T(8,128)} custom-call(f32[256,128]{1,0:T(8,128)S(1)} %bitcast.16), custom_call_target="tpu_custom_call" | custom-call | flops 536870912 | bytes 1048576 | tf_op jit(solution)/shard_map/splat/pallas_call | solution.py:265
  41.9 4.0 %all-to-all-start.1 = ((f32[4,32,1024]{2,1,0:T(8,128)}), f32[4,32,1024]{2,1,0:T(8,128)S(1)}, u32[]{:S(2)}, u32[]{:S(2)}) async-start(f32[4,32,1024]{2,1,0:T(8,128)} %splat.1), calls=%async_computation.1 | async-start | bytes 1048576 | tf_op jit(solution)/shard_map/all_to_all | solution.py:357
  45.9 0.0 copy-done.2
  45.9 0.4 reduce
  46.2 0.2 reshape.38
  46.4 0.1 copy.12
  46.5 7.3 %all-to-all-done.1.parts_ref = f32[4,32,1024]{2,1,0:T(8,128)S(1)} async-done(((f32[4,32,1024]{2,1,0:T(8,128)}), f32[4,32,1024]{2,1,0:T(8,128)S(1)}, u32[]{:S(2)}, u32[]{:S(2)}) %all-to-all-start.1) | async-done | bytes 524320 | tf_op jit(solution)/shard_map/all_to_all | solution.py:357
  53.8 0.0 copy-start
  53.8 0.0 copy-start.1
  53.8 11.4 %pull.1 = f32[512,128]{1,0:T(8,128)S(1)} custom-call(f32[256,128]{1,0:T(8,128)S(1)} %bitcast.17, f32[4,32,1024]{2,1,0:T(8,128)S(1)} %all-to-all-done.1.parts_ref, bf16[32,1024]{1,0:T(8,128)(2,1)S(1)} %bitcast.18), custom_call_target="tpu_custom_call" | custom-call | flops 4294967296 | bytes 1048576 | tf_op jit(solution)/shard_map/pull/pallas_call | solution.py:265
  65.2 21.5 %all_to_all.26 = f32[128,4,128]{2,1,0:T(4,128)S(1)} all-to-all(f32[128,4,128]{2,1,0:T(4,128)S(1)} %bitcast.15), channel_id=1, replica_groups=mesh['y'=8,'z'=8,'core'=2,'seg'=4] {'y','z','core'}, dimensions={0} | all-to-all | bytes 524288 | tf_op jit(solution)/shard_map/all_to_all | solution.py:357
  86.7 0.0 copy-done
  86.7 0.0 copy-done.1
  86.8 2.0 %finish.1 = (f32[3,1024]{1,0:T(4,128)}, f32[32,128]{1,0:T(8,128)S(1)}, f32[1,128]{1,0:T(1,128)}) custom-call(f32[512,128]{1,0:T(8,128)S(1)} %bitcast.14, bf16[2,32,128]{2,1,0:T(8,128)(2,1)S(1)} %copy-done.1, bf16[3,256,1024]{2,1,0:T(8,128)(2,1)S(1)} %bitcast.21), custom_call_target="tpu_custom_call" | custom-call | flops 67108864 | bytes 1048576 | tf_op jit(solution)/shard_map/finish/pallas_call | solution.py:265
  88.7 11.5 %all_to_all.27 = f32[16,2,128]{2,1,0:T(2,128)S(1)} all-to-all(f32[16,2,128]{2,1,0:T(2,128)S(1)} %bitcast.19), channel_id=1, replica_groups=mesh['y'=8,'z'=8,'core'=2,'seg'=4] {'z','core'}, dimensions={0} | all-to-all | bytes 32768 | tf_op jit(solution)/shard_map/all_to_all | solution.py:357
  100.3 12.0 %all_to_all.28 = f32[32,2,128]{2,1,0:T(2,128)S(1)} all-to-all(f32[32,2,128]{2,1,0:T(2,128)S(1)} %broadcast_in_dim.2), channel_id=1, replica_groups=mesh['y'=8,'z'=8,'core'=2,'seg'=4] {'y','seg'}, dimensions={0} | all-to-all | bytes 65536 | tf_op jit(solution)/shard_map/all_to_all | solution.py:357
  112.3 0.6 reduce_sum.19
  (2 shorter events, 0.0 us)
Async XLA Ops:
  34.1 11.8 %copy-start.2 = (bf16[1,32768]{1,0:T(2,128)(2,1)S(1)}, bf16[1,32768]{1,0:T(2,128)(2,1)}, u32[]{:S(2)}) copy-start(bf16[1,32768]{1,0:T(2,128)(2,1)} %param.11) | copy-start | bytes 196612
  41.9 11.9 %all-to-all-start.1 = ((f32[4,32,1024]{2,1,0:T(8,128)}), f32[4,32,1024]{2,1,0:T(8,128)S(1)}, u32[]{:S(2)}, u32[]{:S(2)}) async-start(f32[4,32,1024]{2,1,0:T(8,128)} %splat.1), calls=%async_computation.1 | async-start | bytes 1048576 | tf_op jit(solution)/shard_map/all_to_all | solution.py:357
  53.8 33.0 %copy-start = (bf16[256,3,1024]{2,0,1:T(8,128)(2,1)S(1)}, bf16[256,3,1024]{2,0,1:T(8,128)(2,1)}, u32[]{:S(2)}) copy-start(bf16[256,3,1024]{2,0,1:T(8,128)(2,1)} %param.9) | copy-start | bytes 4718596
  53.8 33.0 %copy-start.1 = (bf16[2,32,128]{2,1,0:T(8,128)(2,1)S(1)}, bf16[2,32,128]{2,1,0:T(8,128)(2,1)}, u32[]{:S(2)}) copy-start(bf16[2,32,128]{2,1,0:T(8,128)(2,1)} %get-tuple-element.9.refs_1_) | copy-start | bytes 49156

commit v4 on v3

--- a/solution.py
+++ b/solution.py
@@ -10,7 +10,8 @@
 ATOM_BLOCK = 32
 PLANE = EDGE * EDGE
 LANES = 128
-CHUNK = 256
+SPLAT_CHUNK = 512
+PULL_CHUNK = 256
 
 inverse_var = 1.0 / 2.25
 
@@ -151,8 +152,8 @@
         place_ref[component] = regroup(rows, component)
 
 
-def chunk_row(place_ref, component, chunk):
-    rows = CHUNK // LANES
+def chunk_row(place_ref, component, chunk, size):
+    rows = size // LANES
     return jnp.concatenate(
         [place_ref[component, pl.ds(chunk * rows + i, 1), :] for i in range(rows)], axis=1
     )
@@ -169,80 +170,82 @@
         use(1, 2 * step + 1)
 
 
-def splat_kernel(got_ref, out_ref, place_ref, line_ref, weight_ref, plane_ref):
+def build_plane(place_ref, line_ref, plane_ref, slot, chunk, size):
+    along_x = factors(chunk_row(place_ref, 0, chunk, size))[0].astype(jnp.bfloat16)
+    along_z = factors(chunk_row(place_ref, 2, chunk, size))[0].astype(jnp.bfloat16)
+    line_ref[slot] = along_z.astype(jnp.float32)
+    for z in range(EDGE):
+        line = jnp.broadcast_to(line_ref[slot, pl.ds(z, 1), :], (EDGE, size))
+        plane_ref[slot, pl.ds(z * EDGE, EDGE), :] = line.astype(jnp.bfloat16) * along_x
+
+
+def splat_kernel(got_ref, out_ref, place_ref, line_ref, weight_ref, plane_ref, sum_ref):
+    size = plane_ref.shape[2]
     unpack_rows(got_ref, place_ref)
-    out_ref[0] = jnp.zeros_like(out_ref[0])
+    sum_ref[...] = jnp.zeros_like(sum_ref)
 
     def build(slot, chunk):
-        along_x = factors(chunk_row(place_ref, 0, chunk))[0].astype(jnp.bfloat16)
-        along_y = factors(chunk_row(place_ref, 1, chunk))[0]
-        along_z = factors(chunk_row(place_ref, 2, chunk))[0]
-        weight_ref[slot] = (chunk_row(place_ref, 3, chunk) * along_y).astype(jnp.bfloat16)
-        line_ref[slot] = along_z.astype(jnp.bfloat16).astype(jnp.float32)
-        for z in range(EDGE):
-            line = jnp.broadcast_to(line_ref[slot, pl.ds(z, 1), :], (EDGE, CHUNK))
-            plane_ref[slot, pl.ds(z * EDGE, EDGE), :] = line.astype(jnp.bfloat16) * along_x
+        build_plane(place_ref, line_ref, plane_ref, slot, chunk, size)
+        along_y = factors(chunk_row(place_ref, 1, chunk, size))[0]
+        weight_ref[slot] = (chunk_row(place_ref, 3, chunk, size) * along_y).astype(jnp.bfloat16)
 
     def use(slot, chunk):
-        out_ref[0] += against_rows(weight_ref[slot], plane_ref[slot])
-
-    pipeline(place_ref.shape[1] * LANES // CHUNK, build, use)
-    for copy in range(1, out_ref.shape[0]):
-        out_ref[copy] = out_ref[0]
+        sum_ref[...] += against_rows(plane_ref[slot], weight_ref[slot])
+
+    pipeline(place_ref.shape[1] * LANES // size, build, use)
+    total = sum_ref[...].T
+    for copy in range(out_ref.shape[0]):
+        out_ref[copy] = total
 
 
 def pull_kernel(got_ref, parts_ref, target_ref, out_ref, place_ref, line_ref, weight_ref, plane_ref, row_ref, sum_ref):
+    size = plane_ref.shape[2]
     unpack_rows(got_ref, place_ref)
-    target = target_ref[...]
     density = (parts_ref[0] + parts_ref[2]) + (parts_ref[1] + parts_ref[3])
-    wide = target.astype(jnp.float32)
-    high, middle, _ = exact_parts(density)
-    row_ref[0:EDGE] = target
-    row_ref[EDGE : 2 * EDGE] = high
-    row_ref[2 * EDGE : 3 * EDGE] = middle
+    wide = target_ref[...].astype(jnp.float32)
+    voxel = lax.broadcasted_iota(jnp.int32, (EDGE, PLANE), 1)
+    middle = EDGE / 2
+    center_x = (voxel % EDGE).astype(jnp.float32) + (0.5 - middle)
+    center_z = (voxel // EDGE).astype(jnp.float32) + (0.5 - middle)
+    row_ref[0:EDGE] = target_ref[...]
+    places = [(wide * center_x, 1), (wide * center_z, 3), (density, 5), (density * center_x, 7), (density * center_z, 9)]
+    for values, place in places:
+        high, low, _ = exact_parts(values)
+        row_ref[place * EDGE : (place + 1) * EDGE] = high
+        row_ref[(place + 1) * EDGE : (place + 2) * EDGE] = low
 
     def build(slot, chunk):
-        profile_x, slope_x = factors(chunk_row(place_ref, 0, chunk))
-        profile_y, slope_y = factors(chunk_row(place_ref, 1, chunk))
-        profile_z, slope_z = factors(chunk_row(place_ref, 2, chunk))
-        masses = chunk_row(place_ref, 3, chunk)
-        profile_x = profile_x.astype(jnp.bfloat16)
-        slope_x = slope_x.astype(jnp.bfloat16)
+        build_plane(place_ref, line_ref, plane_ref, slot, chunk, size)
+        profile_y, slope_y = factors(chunk_row(place_ref, 1, chunk, size))
+        masses = chunk_row(place_ref, 3, chunk, size)
         weight_ref[slot, 0] = (masses * profile_y).astype(jnp.bfloat16).astype(jnp.float32)
         weight_ref[slot, 1] = (masses * slope_y).astype(jnp.bfloat16).astype(jnp.float32)
-        line_ref[slot, 0] = profile_z.astype(jnp.bfloat16).astype(jnp.float32)
-        line_ref[slot, 1] = slope_z.astype(jnp.bfloat16).astype(jnp.float32)
-        for z in range(EDGE):
-            line = jnp.broadcast_to(line_ref[slot, 0, pl.ds(z, 1), :], (EDGE, CHUNK))
-            slope_line = jnp.broadcast_to(line_ref[slot, 1, pl.ds(z, 1), :], (EDGE, CHUNK))
-            line = line.astype(jnp.bfloat16)
-            slope_line = slope_line.astype(jnp.bfloat16)
-            place = pl.ds(z * EDGE, EDGE)
-            plane_ref[slot, place, pl.ds(0, CHUNK)] = line * slope_x
-            plane_ref[slot, place, pl.ds(CHUNK, CHUNK)] = line * profile_x
-            plane_ref[slot, place, pl.ds(2 * CHUNK, CHUNK)] = slope_line * profile_x
 
     def use(slot, chunk):
-        rows = CHUNK // LANES
-        for component, weight in enumerate((0, 1, 0)):
-            pulled = jnp.dot(
-                row_ref[...],
-                plane_ref[slot, :, pl.ds(component * CHUNK, CHUNK)],
-                preferred_element_type=jnp.float32,
-            )
-            weight = weight_ref[slot, weight]
-            model = pulled[EDGE : 2 * EDGE] + pulled[2 * EDGE :]
-            sums = (
-                jnp.sum(pulled[:EDGE] * weight, axis=0, keepdims=True),
-                jnp.sum(model * weight, axis=0, keepdims=True),
-            )
-            for kind in range(2):
+        rows = size // LANES
+        pulled = jnp.dot(row_ref[...], plane_ref[slot], preferred_element_type=jnp.float32)
+        block = [pulled[i * EDGE : (i + 1) * EDGE] for i in range(11)]
+        along_y, slope_y = weight_ref[slot, 0], weight_ref[slot, 1]
+        place_x = chunk_row(place_ref, 0, chunk, size) - middle
+        place_z = chunk_row(place_ref, 2, chunk, size) - middle
+        kinds = (
+            (block[0], block[1] + block[2], block[3] + block[4]),
+            (block[5] + block[6], block[7] + block[8], block[9] + block[10]),
+        )
+        for kind, (plain, by_x, by_z) in enumerate(kinds):
+            whole, force_y, moment_x, moment_z = [
+                jnp.sum(values * weight, axis=0, keepdims=True)
+                for values, weight in ((plain, along_y), (plain, slope_y), (by_x, along_y), (by_z, along_y))
+            ]
+            force_x = inverse_var * (moment_x - place_x * whole)
+            force_z = inverse_var * (moment_z - place_z * whole)
+            for component, force in enumerate((force_x, force_y, force_z)):
                 for i in range(rows):
-                    sum_ref[kind, component, pl.ds(chunk * rows + i, 1), :] = sums[kind][
+                    sum_ref[kind, component, pl.ds(chunk * rows + i, 1), :] = force[
                         :, i * LANES : (i + 1) * LANES
                     ]
 
-    pipeline(place_ref.shape[1] * LANES // CHUNK, build, use)
+    pipeline(place_ref.shape[1] * LANES // size, build, use)
     pairs = place_ref.shape[1]
     left = lax.broadcasted_iota(jnp.int32, (pairs, LANES), 1) < LANES // 2
     for component in range(3):
@@ -314,15 +317,17 @@
 
 def splat(got, copies):
     groups = got.shape[0] // 4
+    size = min(SPLAT_CHUNK, groups * LANES // 2)
     return call(
         splat_kernel,
         "splat",
         jax.ShapeDtypeStruct((copies, EDGE, PLANE), jnp.float32),
         [
             ((4, groups, LANES), jnp.float32),
-            ((2, EDGE, CHUNK), jnp.float32),
-            ((2, EDGE, CHUNK), jnp.bfloat16),
-            ((2, PLANE, CHUNK), jnp.bfloat16),
+            ((2, EDGE, size), jnp.float32),
+            ((2, EDGE, size), jnp.bfloat16),
+            ((2, PLANE, size), jnp.bfloat16),
+            ((PLANE, EDGE), jnp.float32),
         ],
         2**29,
         got,
@@ -331,16 +336,17 @@
 
 def pull(got, parts, target):
     groups = got.shape[0] // 4
+    size = min(PULL_CHUNK, groups * LANES // 2)
     return call(
         pull_kernel,
         "pull",
         jax.ShapeDtypeStruct((8 * groups, LANES), jnp.float32),
         [
             ((4, groups, LANES), jnp.float32),
-            ((2, 2, EDGE, CHUNK), jnp.float32),
-            ((2, 2, EDGE, CHUNK), jnp.float32),
-            ((2, PLANE, 3 * CHUNK), jnp.bfloat16),
-            ((3 * EDGE, PLANE), jnp.bfloat16),
+            ((2, EDGE, size), jnp.float32),
+            ((2, 2, EDGE, size), jnp.float32),
+            ((2, PLANE, size), jnp.bfloat16),
+            ((11 * EDGE, PLANE), jnp.bfloat16),
             ((2, 3, groups, LANES), jnp.float32),
         ],
         2**32,

time: 113 us -> 111 us (0.982)
  Pallas kernels: 24 us -> 21.9 us
    pallas_call x4, Pallas kernels: 24 us -> 21.9 us  [call(): pl.pallas_call(kernel, out_shape=out_shape, in_specs=[pl.BlockSpec(memory...]
where the time goes in v4:
time: 111 us
  blocking collectives  75.7 us (68%)
  Pallas kernels  21.9 us (20%)
  waiting for transfers between devices  7.26 us (7%)
  starting transfers between devices  4.01 us (4%)
    all_to_all x4, blocking collectives, exchange(): return lax.all_to_all(values, axes, split_axis=0, concat_axis=0, tiled=True)  75.7 us
    pallas_call x4, Pallas kernels, call(): pl.pallas_call(kernel, out_shape=out_shape, in_specs=[pl.BlockSpec(memory...  21.9 us
    all_to_all x1, waiting for transfers between devices, exchange(): return lax.all_to_all(values, axes, split_axis=0, concat_axis=0, tiled=True)  7.26 us
    all_to_all x1, starting transfers between devices, exchange(): return lax.all_to_all(values, axes, split_axis=0, concat_axis=0, tiled=True)  4.01 us
  transfers between devices with their start and end apart: 1, of which 1 were waited for; matrix products, arithmetic and copies ran while one was open for 1% of the time, Pallas kernels for 0%

profile of v4, /device:TPU:1, one launch (start us, length us, event | category | flops | bytes accessed | tf_op | source)
XLA Modules:
  0.0 110.8 jit_solution(11830138216373853311)
XLA Ops:
  0.6 2.8 %pack.1 = (f32[256,128]{1,0:T(8,128)}, bf16[2,32,128]{2,1,0:T(8,128)(2,1)}) custom-call(s32[4,32]{1,0:T(4,128)} %bitcast.26, s32[3,4,32]{2,1,0:T(4,128)} %bitcast.24, f32[1,256]{1,0:T(1,128)} %bitcast.27, f32[3,1024]{1,0:T(4,128)} %refs_3_.1, f32[8,128]{1,0:T(8,128)} %bitcast.25, bf16[3,256,1024]{2,1,0:T(8,128)(2,1)} %bitcast.20), custom_call_target="tpu_custom_call" | custom-call | flops 67108864 | bytes 1048576 | tf_op jit(solution)/shard_map/pack/pallas_call | solution.py:268
  3.4 30.6 %all_to_all.25 = f32[128,2,128]{2,1,0:T(2,128)S(1)} all-to-all(f32[128,2,128]{2,1,0:T(2,128)} %bitcast.22), channel_id=1, replica_groups=mesh['y'=8,'z'=8,'core'=2,'seg'=4] {'y','z','core'}, dimensions={0} | all-to-all | bytes 262144 | tf_op jit(solution)/shard_map/all_to_all | solution.py:363
  34.1 0.0 copy-start.2
  34.1 7.2 %splat.1 = f32[4,32,1024]{2,1,0:T(8,128)} custom-call(f32[256,128]{1,0:T(8,128)S(1)} %bitcast.16), custom_call_target="tpu_custom_call" | custom-call | flops 536870912 | bytes 1048576 | tf_op jit(solution)/shard_map/splat/pallas_call | solution.py:268
  41.3 4.0 %all-to-all-start.1 = ((f32[4,32,1024]{2,1,0:T(8,128)}), f32[4,32,1024]{2,1,0:T(8,128)S(1)}, u32[]{:S(2)}, u32[]{:S(2)}) async-start(f32[4,32,1024]{2,1,0:T(8,128)} %splat.1), calls=%async_computation.1 | async-start | bytes 1048576 | tf_op jit(solution)/shard_map/all_to_all | solution.py:363
  45.3 0.0 copy-done.2
  45.3 0.4 reduce
  45.7 0.2 reshape.38
  45.8 0.1 copy.12
  46.0 7.3 %all-to-all-done.1.parts_ref = f32[4,32,1024]{2,1,0:T(8,128)S(1)} async-done(((f32[4,32,1024]{2,1,0:T(8,128)}), f32[4,32,1024]{2,1,0:T(8,128)S(1)}, u32[]{:S(2)}, u32[]{:S(2)}) %all-to-all-start.1) | async-done | bytes 524320 | tf_op jit(solution)/shard_map/all_to_all | solution.py:363
  53.2 0.0 copy-start
  53.2 0.0 copy-start.1
  53.2 9.9 %pull.1 = f32[512,128]{1,0:T(8,128)S(1)} custom-call(f32[256,128]{1,0:T(8,128)S(1)} %bitcast.17, f32[4,32,1024]{2,1,0:T(8,128)S(1)} %all-to-all-done.1.parts_ref, bf16[32,1024]{1,0:T(8,128)(2,1)S(1)} %bitcast.18), custom_call_target="tpu_custom_call" | custom-call | flops 4294967296 | bytes 1048576 | tf_op jit(solution)/shard_map/pull/pallas_call | solution.py:268
  63.1 21.5 %all_to_all.26 = f32[128,4,128]{2,1,0:T(4,128)S(1)} all-to-all(f32[128,4,128]{2,1,0:T(4,128)S(1)} %bitcast.15), channel_id=1, replica_groups=mesh['y'=8,'z'=8,'core'=2,'seg'=4] {'y','z','core'}, dimensions={0} | all-to-all | bytes 524288 | tf_op jit(solution)/shard_map/all_to_all | solution.py:363
  84.6 0.0 copy-done
  84.6 0.0 copy-done.1
  84.6 2.0 %finish.1 = (f32[3,1024]{1,0:T(4,128)}, f32[32,128]{1,0:T(8,128)S(1)}, f32[1,128]{1,0:T(1,128)}) custom-call(f32[512,128]{1,0:T(8,128)S(1)} %bitcast.14, bf16[2,32,128]{2,1,0:T(8,128)(2,1)S(1)} %copy-done.1, bf16[3,256,1024]{2,1,0:T(8,128)(2,1)S(1)} %bitcast.21), custom_call_target="tpu_custom_call" | custom-call | flops 67108864 | bytes 1048576 | tf_op jit(solution)/shard_map/finish/pallas_call | solution.py:268
  86.6 11.5 %all_to_all.27 = f32[16,2,128]{2,1,0:T(2,128)S(1)} all-to-all(f32[16,2,128]{2,1,0:T(2,128)S(1)} %bitcast.19), channel_id=1, replica_groups=mesh['y'=8,'z'=8,'core'=2,'seg'=4] {'z','core'}, dimensions={0} | all-to-all | bytes 32768 | tf_op jit(solution)/shard_map/all_to_all | solution.py:363
  98.1 12.0 %all_to_all.28 = f32[32,2,128]{2,1,0:T(2,128)S(1)} all-to-all(f32[32,2,128]{2,1,0:T(2,128)S(1)} %broadcast_in_dim.2), channel_id=1, replica_groups=mesh['y'=8,'z'=8,'core'=2,'seg'=4] {'y','seg'}, dimensions={0} | all-to-all | bytes 65536 | tf_op jit(solution)/shard_map/all_to_all | solution.py:363
  110.2 0.6 reduce_sum.19
  (2 shorter events, 0.0 us)
Async XLA Ops:
  34.1 11.2 %copy-start.2 = (bf16[1,32768]{1,0:T(2,128)(2,1)S(1)}, bf16[1,32768]{1,0:T(2,128)(2,1)}, u32[]{:S(2)}) copy-start(bf16[1,32768]{1,0:T(2,128)(2,1)} %param.11) | copy-start | bytes 196612
  41.3 11.9 %all-to-all-start.1 = ((f32[4,32,1024]{2,1,0:T(8,128)}), f32[4,32,1024]{2,1,0:T(8,128)S(1)}, u32[]{:S(2)}, u32[]{:S(2)}) async-start(f32[4,32,1024]{2,1,0:T(8,128)} %splat.1), calls=%async_computation.1 | async-start | bytes 1048576 | tf_op jit(solution)/shard_map/all_to_all | solution.py:363
  53.2 31.4 %copy-start = (bf16[256,3,1024]{2,0,1:T(8,128)(2,1)S(1)}, bf16[256,3,1024]{2,0,1:T(8,128)(2,1)}, u32[]{:S(2)}) copy-start(bf16[256,3,1024]{2,0,1:T(8,128)(2,1)} %param.9) | copy-start | bytes 4718596
  53.2 31.4 %copy-start.1 = (bf16[2,32,128]{2,1,0:T(8,128)(2,1)S(1)}, bf16[2,32,128]{2,1,0:T(8,128)(2,1)}, u32[]{:S(2)}) copy-start(bf16[2,32,128]{2,1,0:T(8,128)(2,1)} %get-tuple-element.9.refs_1_) | copy-start | bytes 49156

commit v5 on v4

--- a/solution.py
+++ b/solution.py
@@ -11,7 +11,8 @@
 PLANE = EDGE * EDGE
 LANES = 128
 SPLAT_CHUNK = 512
-PULL_CHUNK = 256
+PULL_CHUNK = 512
+WIDTH = 256
 
 inverse_var = 1.0 / 2.25
 
@@ -190,7 +191,9 @@
         weight_ref[slot] = (chunk_row(place_ref, 3, chunk, size) * along_y).astype(jnp.bfloat16)
 
     def use(slot, chunk):
-        sum_ref[...] += against_rows(plane_ref[slot], weight_ref[slot])
+        for half in range(2):
+            rows = pl.ds(half * PLANE // 2, PLANE // 2)
+            sum_ref[rows, :] += against_rows(plane_ref[slot, rows, :], weight_ref[slot])
 
     pipeline(place_ref.shape[1] * LANES // size, build, use)
     total = sum_ref[...].T
@@ -222,10 +225,15 @@
         weight_ref[slot, 1] = (masses * slope_y).astype(jnp.bfloat16).astype(jnp.float32)
 
     def use(slot, chunk):
+        width = min(WIDTH, size)
+        for part in range(size // width):
+            use_part(slot, chunk * (size // width) + part, pl.ds(part * width, width), width)
+
+    def use_part(slot, chunk, atoms, size):
         rows = size // LANES
-        pulled = jnp.dot(row_ref[...], plane_ref[slot], preferred_element_type=jnp.float32)
+        pulled = jnp.dot(row_ref[...], plane_ref[slot, :, atoms], preferred_element_type=jnp.float32)
         block = [pulled[i * EDGE : (i + 1) * EDGE] for i in range(11)]
-        along_y, slope_y = weight_ref[slot, 0], weight_ref[slot, 1]
+        along_y, slope_y = weight_ref[slot, 0, :, atoms], weight_ref[slot, 1, :, atoms]
         place_x = chunk_row(place_ref, 0, chunk, size) - middle
         place_z = chunk_row(place_ref, 2, chunk, size) - middle
         kinds = (
@@ -382,7 +390,7 @@
     parts = exchange(splat(got, n_seg), "seg")
     pulled = pull(got, parts, target)
     back = exchange(pulled.reshape(n_tile, 4, LANES), TILE_AXES).reshape(4 * n_tile, LANES)
-    near, far = ("z", "core"), ("y", "seg")
+    near, far = ("core", "seg"), ("y", "z")
     forces, spread, score = finish(
         back, picks, modes, float(n_tile * EDGE**3), a_dev * n_tile * n_seg, lax.axis_size(near)
     )

time: 111 us -> 110 us (level)
  Pallas kernels: 21.9 us -> 20.5 us
    pallas_call x4, Pallas kernels: 21.9 us -> 20.5 us  [call(): pl.pallas_call(kernel, out_shape=out_shape, in_specs=[pl.BlockSpec(memory...]
where the time goes in v5:
time: 110 us
  blocking collectives  76 us (69%)
  Pallas kernels  20.5 us (19%)
  waiting for transfers between devices  7.26 us (7%)
  starting transfers between devices  4.01 us (4%)
    all_to_all x4, blocking collectives, exchange(): return lax.all_to_all(values, axes, split_axis=0, concat_axis=0, tiled=True)  76 us
    pallas_call x4, Pallas kernels, call(): pl.pallas_call(kernel, out_shape=out_shape, in_specs=[pl.BlockSpec(memory...  20.5 us
    all_to_all x1, waiting for transfers between devices, exchange(): return lax.all_to_all(values, axes, split_axis=0, concat_axis=0, tiled=True)  7.26 us
    all_to_all x1, starting transfers between devices, exchange(): return lax.all_to_all(values, axes, split_axis=0, concat_axis=0, tiled=True)  4.01 us
  transfers between devices with their start and end apart: 1, of which 1 were waited for; matrix products, arithmetic and copies ran while one was open for 1% of the time, Pallas kernels for 0%

profile of v5, /device:TPU:1, one launch (start us, length us, event | category | flops | bytes accessed | tf_op | source)
XLA Modules:
  0.0 109.7 jit_solution(7625475197562243004)
XLA Ops:
  0.6 2.8 %pack.1 = (f32[256,128]{1,0:T(8,128)}, bf16[2,32,128]{2,1,0:T(8,128)(2,1)}) custom-call(s32[4,32]{1,0:T(4,128)} %bitcast.26, s32[3,4,32]{2,1,0:T(4,128)} %bitcast.24, f32[1,256]{1,0:T(1,128)} %bitcast.27, f32[3,1024]{1,0:T(4,128)} %refs_3_.1, f32[8,128]{1,0:T(8,128)} %bitcast.25, bf16[3,256,1024]{2,1,0:T(8,128)(2,1)} %bitcast.20), custom_call_target="tpu_custom_call" | custom-call | flops 67108864 | bytes 1048576 | tf_op jit(solution)/shard_map/pack/pallas_call | solution.py:276
  3.4 30.6 %all_to_all.25 = f32[128,2,128]{2,1,0:T(2,128)S(1)} all-to-all(f32[128,2,128]{2,1,0:T(2,128)} %bitcast.22), channel_id=1, replica_groups=mesh['y'=8,'z'=8,'core'=2,'seg'=4] {'y','z','core'}, dimensions={0} | all-to-all | bytes 262144 | tf_op jit(solution)/shard_map/all_to_all | solution.py:371
  34.1 0.0 copy-start.2
  34.1 7.3 %splat.1 = f32[4,32,1024]{2,1,0:T(8,128)} custom-call(f32[256,128]{1,0:T(8,128)S(1)} %bitcast.16), custom_call_target="tpu_custom_call" | custom-call | flops 536870912 | bytes 1048576 | tf_op jit(solution)/shard_map/splat/pallas_call | solution.py:276
  41.3 4.0 %all-to-all-start.1 = ((f32[4,32,1024]{2,1,0:T(8,128)}), f32[4,32,1024]{2,1,0:T(8,128)S(1)}, u32[]{:S(2)}, u32[]{:S(2)}) async-start(f32[4,32,1024]{2,1,0:T(8,128)} %splat.1), calls=%async_computation.1 | async-start | bytes 1048576 | tf_op jit(solution)/shard_map/all_to_all | solution.py:371
  45.4 0.0 copy-done.2
  45.4 0.4 reduce
  45.7 0.2 reshape.38
  45.9 0.1 copy.12
  46.0 7.3 %all-to-all-done.1.parts_ref = f32[4,32,1024]{2,1,0:T(8,128)S(1)} async-done(((f32[4,32,1024]{2,1,0:T(8,128)}), f32[4,32,1024]{2,1,0:T(8,128)S(1)}, u32[]{:S(2)}, u32[]{:S(2)}) %all-to-all-start.1) | async-done | bytes 524320 | tf_op jit(solution)/shard_map/all_to_all | solution.py:371
  53.3 0.0 copy-start
  53.3 0.0 copy-start.1
  53.3 8.5 %pull.1 = f32[512,128]{1,0:T(8,128)S(1)} custom-call(f32[256,128]{1,0:T(8,128)S(1)} %bitcast.17, f32[4,32,1024]{2,1,0:T(8,128)S(1)} %all-to-all-done.1.parts_ref, bf16[32,1024]{1,0:T(8,128)(2,1)S(1)} %bitcast.18), custom_call_target="tpu_custom_call" | custom-call | flops 4294967296 | bytes 1048576 | tf_op jit(solution)/shard_map/pull/pallas_call | solution.py:276
  61.7 21.5 %all_to_all.26 = f32[128,4,128]{2,1,0:T(4,128)S(1)} all-to-all(f32[128,4,128]{2,1,0:T(4,128)S(1)} %bitcast.15), channel_id=1, replica_groups=mesh['y'=8,'z'=8,'core'=2,'seg'=4] {'y','z','core'}, dimensions={0} | all-to-all | bytes 524288 | tf_op jit(solution)/shard_map/all_to_all | solution.py:371
  83.2 0.0 copy-done
  83.2 0.0 copy-done.1
  83.2 2.0 %finish.1 = (f32[3,1024]{1,0:T(4,128)}, f32[16,128]{1,0:T(8,128)S(1)}, f32[1,128]{1,0:T(1,128)}) custom-call(f32[512,128]{1,0:T(8,128)S(1)} %bitcast.14, bf16[2,32,128]{2,1,0:T(8,128)(2,1)S(1)} %copy-done.1, bf16[3,256,1024]{2,1,0:T(8,128)(2,1)S(1)} %bitcast.21), custom_call_target="tpu_custom_call" | custom-call | flops 67108864 | bytes 1048576 | tf_op jit(solution)/shard_map/finish/pallas_call | solution.py:276
  85.2 8.9 %all_to_all.27 = f32[8,2,128]{2,1,0:T(2,128)S(1)} all-to-all(f32[8,2,128]{2,1,0:T(2,128)S(1)} %bitcast.19), channel_id=1, replica_groups=mesh['y'=8,'z'=8,'core'=2,'seg'=4] {'core','seg'}, dimensions={0} | all-to-all | bytes 16384 | tf_op jit(solution)/shard_map/all_to_all | solution.py:371
  94.2 14.9 %all_to_all.28 = f32[64,2,128]{2,1,0:T(2,128)S(1)} all-to-all(f32[64,2,128]{2,1,0:T(2,128)S(1)} %broadcast_in_dim.2), channel_id=1, replica_groups=mesh['y'=8,'z'=8,'core'=2,'seg'=4] {'y','z'}, dimensions={0} | all-to-all | bytes 131072 | tf_op jit(solution)/shard_map/all_to_all | solution.py:371
  109.1 0.6 reduce_sum.19
  (2 shorter events, 0.0 us)
Async XLA Ops:
  34.1 11.3 %copy-start.2 = (bf16[1,32768]{1,0:T(2,128)(2,1)S(1)}, bf16[1,32768]{1,0:T(2,128)(2,1)}, u32[]{:S(2)}) copy-start(bf16[1,32768]{1,0:T(2,128)(2,1)} %param.11) | copy-start | bytes 196612
  41.3 11.9 %all-to-all-start.1 = ((f32[4,32,1024]{2,1,0:T(8,128)}), f32[4,32,1024]{2,1,0:T(8,128)S(1)}, u32[]{:S(2)}, u32[]{:S(2)}) async-start(f32[4,32,1024]{2,1,0:T(8,128)} %splat.1), calls=%async_computation.1 | async-start | bytes 1048576 | tf_op jit(solution)/shard_map/all_to_all | solution.py:371
  53.3 30.0 %copy-start = (bf16[256,3,1024]{2,0,1:T(8,128)(2,1)S(1)}, bf16[256,3,1024]{2,0,1:T(8,128)(2,1)}, u32[]{:S(2)}) copy-start(bf16[256,3,1024]{2,0,1:T(8,128)(2,1)} %param.9) | copy-start | bytes 4718596
  53.3 30.0 %copy-start.1 = (bf16[2,32,128]{2,1,0:T(8,128)(2,1)S(1)}, bf16[2,32,128]{2,1,0:T(8,128)(2,1)}, u32[]{:S(2)}) copy-start(bf16[2,32,128]{2,1,0:T(8,128)(2,1)} %get-tuple-element.9.refs_1_) | copy-start | bytes 49156

commit v6 on v5

--- a/solution.py
+++ b/solution.py
@@ -1,3 +1,5 @@
+import math
+
 import jax
 import jax.numpy as jnp
 from jax import lax
@@ -15,12 +17,13 @@
 WIDTH = 256
 
 inverse_var = 1.0 / 2.25
+half_log = -0.5 * inverse_var / math.log(2.0)
 
 
 def factors(places):
     centers = lax.broadcasted_iota(jnp.int32, (EDGE, places.shape[1]), 0).astype(jnp.float32) + 0.5
     distance = centers - places
-    profile = jnp.exp(-0.5 * inverse_var * distance * distance)
+    profile = jnp.exp2(half_log * (distance * distance))
     return profile, inverse_var * distance * profile
 
 
@@ -167,7 +170,7 @@
     def _(step):
         build(1, 2 * step + 1)
         use(0, 2 * step)
-        build(0, jnp.minimum(2 * step + 2, chunks - 1))
+        build(0, jnp.minimum(2 * step + 2, chunks - 2))
         use(1, 2 * step + 1)
 
 
@@ -177,7 +180,7 @@
     line_ref[slot] = along_z.astype(jnp.float32)
     for z in range(EDGE):
         line = jnp.broadcast_to(line_ref[slot, pl.ds(z, 1), :], (EDGE, size))
-        plane_ref[slot, pl.ds(z * EDGE, EDGE), :] = line.astype(jnp.bfloat16) * along_x
+        plane_ref[pl.ds(z * EDGE, EDGE), :] = line.astype(jnp.bfloat16) * along_x
 
 
 def splat_kernel(got_ref, out_ref, place_ref, line_ref, weight_ref, plane_ref, sum_ref):
@@ -186,7 +189,7 @@
     sum_ref[...] = jnp.zeros_like(sum_ref)
 
     def build(slot, chunk):
-        build_plane(place_ref, line_ref, plane_ref, slot, chunk, size)
+        build_plane(place_ref, line_ref, plane_ref.at[slot], slot, chunk, size)
         along_y = factors(chunk_row(place_ref, 1, chunk, size))[0]
         weight_ref[slot] = (chunk_row(place_ref, 3, chunk, size) * along_y).astype(jnp.bfloat16)
 
@@ -201,63 +204,104 @@
         out_ref[copy] = total
 
 
-def pull_kernel(got_ref, parts_ref, target_ref, out_ref, place_ref, line_ref, weight_ref, plane_ref, row_ref, sum_ref):
-    size = plane_ref.shape[2]
+middle = EDGE / 2
+
+
+def voxel_centers():
+    voxel = lax.broadcasted_iota(jnp.int32, (EDGE, PLANE), 1)
+    return [part.astype(jnp.float32) + (0.5 - middle) for part in (voxel % EDGE, voxel // EDGE)]
+
+
+def store_rows(row_ref, arrays):
+    place = 0
+    for values in arrays:
+        terms = (values,) if values.dtype == jnp.bfloat16 else exact_parts(values)[:2]
+        for term in terms:
+            row_ref[place : place + EDGE] = term
+            place += EDGE
+
+
+def take_forces(sum_ref, chunk, sums, weights, places):
+    plain, by_x, by_z = sums
+    along_y, slope_y = [weight.astype(jnp.float32) for weight in weights]
+    whole, force_y, moment_x, moment_z = [
+        jnp.sum(values * weight, axis=0, keepdims=True)
+        for values, weight in ((plain, along_y), (plain, slope_y), (by_x, along_y), (by_z, along_y))
+    ]
+    force_x = inverse_var * (moment_x - (places[0] - middle) * whole)
+    force_z = inverse_var * (moment_z - (places[1] - middle) * whole)
+    rows = whole.shape[1] // LANES
+    for component, force in enumerate((force_x, force_y, force_z)):
+        for i in range(rows):
+            sum_ref[component, pl.ds(chunk * rows + i, 1), :] = force[:, i * LANES : (i + 1) * LANES]
+
+
+def shape_kernel(got_ref, target_ref, even_ref, odd_ref, weight_ref, place_ref, sum_ref, line_ref, row_ref):
+    planes = (even_ref, odd_ref)
+    size = even_ref.shape[2]
+    width = min(WIDTH, size)
     unpack_rows(got_ref, place_ref)
-    density = (parts_ref[0] + parts_ref[2]) + (parts_ref[1] + parts_ref[3])
     wide = target_ref[...].astype(jnp.float32)
-    voxel = lax.broadcasted_iota(jnp.int32, (EDGE, PLANE), 1)
-    middle = EDGE / 2
-    center_x = (voxel % EDGE).astype(jnp.float32) + (0.5 - middle)
-    center_z = (voxel // EDGE).astype(jnp.float32) + (0.5 - middle)
-    row_ref[0:EDGE] = target_ref[...]
-    places = [(wide * center_x, 1), (wide * center_z, 3), (density, 5), (density * center_x, 7), (density * center_z, 9)]
-    for values, place in places:
-        high, low, _ = exact_parts(values)
-        row_ref[place * EDGE : (place + 1) * EDGE] = high
-        row_ref[(place + 1) * EDGE : (place + 2) * EDGE] = low
+    center_x, center_z = voxel_centers()
+    store_rows(row_ref, (target_ref[...], wide * center_x, wide * center_z))
 
     def build(slot, chunk):
-        build_plane(place_ref, line_ref, plane_ref, slot, chunk, size)
+        build_plane(place_ref, line_ref, planes[slot].at[chunk // 2], slot, chunk, size)
         profile_y, slope_y = factors(chunk_row(place_ref, 1, chunk, size))
         masses = chunk_row(place_ref, 3, chunk, size)
-        weight_ref[slot, 0] = (masses * profile_y).astype(jnp.bfloat16).astype(jnp.float32)
-        weight_ref[slot, 1] = (masses * slope_y).astype(jnp.bfloat16).astype(jnp.float32)
+        weight_ref[slot, chunk // 2, 0] = (masses * profile_y).astype(jnp.bfloat16)
+        weight_ref[slot, chunk // 2, 1] = (masses * slope_y).astype(jnp.bfloat16)
 
     def use(slot, chunk):
-        width = min(WIDTH, size)
         for part in range(size // width):
-            use_part(slot, chunk * (size // width) + part, pl.ds(part * width, width), width)
-
-    def use_part(slot, chunk, atoms, size):
-        rows = size // LANES
-        pulled = jnp.dot(row_ref[...], plane_ref[slot, :, atoms], preferred_element_type=jnp.float32)
-        block = [pulled[i * EDGE : (i + 1) * EDGE] for i in range(11)]
-        along_y, slope_y = weight_ref[slot, 0, :, atoms], weight_ref[slot, 1, :, atoms]
-        place_x = chunk_row(place_ref, 0, chunk, size) - middle
-        place_z = chunk_row(place_ref, 2, chunk, size) - middle
-        kinds = (
-            (block[0], block[1] + block[2], block[3] + block[4]),
-            (block[5] + block[6], block[7] + block[8], block[9] + block[10]),
-        )
-        for kind, (plain, by_x, by_z) in enumerate(kinds):
-            whole, force_y, moment_x, moment_z = [
-                jnp.sum(values * weight, axis=0, keepdims=True)
-                for values, weight in ((plain, along_y), (plain, slope_y), (by_x, along_y), (by_z, along_y))
-            ]
-            force_x = inverse_var * (moment_x - place_x * whole)
-            force_z = inverse_var * (moment_z - place_z * whole)
-            for component, force in enumerate((force_x, force_y, force_z)):
-                for i in range(rows):
-                    sum_ref[kind, component, pl.ds(chunk * rows + i, 1), :] = force[
-                        :, i * LANES : (i + 1) * LANES
-                    ]
+            atoms = pl.ds(part * width, width)
+            small = chunk * (size // width) + part
+            pulled = jnp.dot(
+                row_ref[...], planes[slot][chunk // 2, :, atoms], preferred_element_type=jnp.float32
+            )
+            block = [pulled[i * EDGE : (i + 1) * EDGE] for i in range(5)]
+            take_forces(
+                sum_ref,
+                small,
+                (block[0], block[1] + block[2], block[3] + block[4]),
+                [weight_ref[slot, chunk // 2, i, :, atoms] for i in range(2)],
+                [chunk_row(place_ref, i, small, width) for i in (0, 2)],
+            )
 
     pipeline(place_ref.shape[1] * LANES // size, build, use)
+
+
+def pull_kernel(parts_ref, target_ref, even_ref, odd_ref, weight_ref, place_ref, map_ref, out_ref, row_ref, sum_ref):
+    planes = (even_ref, odd_ref)
+    size = even_ref.shape[2]
+    width = min(WIDTH, size)
+    density = (parts_ref[0] + parts_ref[2]) + (parts_ref[1] + parts_ref[3])
+    center_x, center_z = voxel_centers()
+    store_rows(row_ref, (density, density * center_x, density * center_z))
+
+    @pl.loop(0, even_ref.shape[0])
+    def _(step):
+        for slot in range(2):
+            for part in range(size // width):
+                atoms = pl.ds(part * width, width)
+                small = (2 * step + slot) * (size // width) + part
+                pulled = jnp.dot(
+                    row_ref[...], planes[slot][step, :, atoms], preferred_element_type=jnp.float32
+                )
+                block = [pulled[i * EDGE : (i + 1) * EDGE] for i in range(6)]
+                take_forces(
+                    sum_ref,
+                    small,
+                    (block[0] + block[1], block[2] + block[3], block[4] + block[5]),
+                    [weight_ref[slot, step, i, :, atoms] for i in range(2)],
+                    [chunk_row(place_ref, i, small, width) for i in (0, 2)],
+                )
+
+    wide = target_ref[...].astype(jnp.float32)
     pairs = place_ref.shape[1]
     left = lax.broadcasted_iota(jnp.int32, (pairs, LANES), 1) < LANES // 2
     for component in range(3):
-        first, second = sum_ref[0, component], sum_ref[1, component]
+        first, second = map_ref[component], sum_ref[component]
         out_ref[pl.ds(component, pairs, stride=8), :] = jnp.where(
             left, first, pltpu.roll(second, LANES // 2, 1)
         )
@@ -342,25 +386,48 @@
     )
 
 
-def pull(got, parts, target):
+def shape(got, target):
     groups = got.shape[0] // 4
-    size = min(PULL_CHUNK, groups * LANES // 2)
+    atoms = groups * LANES
+    size = min(PULL_CHUNK, atoms // 2)
+    chunks = atoms // size
+    plane = pltpu.VMEM((chunks // 2, PLANE, size), jnp.bfloat16)
+    return call(
+        shape_kernel,
+        "shape",
+        (
+            plane,
+            plane,
+            pltpu.VMEM((2, chunks // 2, 2, EDGE, size), jnp.bfloat16),
+            pltpu.VMEM((4, groups, LANES), jnp.float32),
+            pltpu.VMEM((3, groups, LANES), jnp.float32),
+        ),
+        [
+            ((2, EDGE, size), jnp.float32),
+            ((5 * EDGE, PLANE), jnp.bfloat16),
+        ],
+        2**32,
+        got,
+        target,
+        limit=8,
+    )
+
+
+def pull(parts, target, shapes):
+    groups = shapes[3].shape[1]
     return call(
         pull_kernel,
         "pull",
         jax.ShapeDtypeStruct((8 * groups, LANES), jnp.float32),
         [
-            ((4, groups, LANES), jnp.float32),
-            ((2, EDGE, size), jnp.float32),
-            ((2, 2, EDGE, size), jnp.float32),
-            ((2, PLANE, size), jnp.bfloat16),
-            ((11 * EDGE, PLANE), jnp.bfloat16),
-            ((2, 3, groups, LANES), jnp.float32),
+            ((6 * EDGE, PLANE), jnp.bfloat16),
+            ((3, groups, LANES), jnp.float32),
         ],
         2**32,
-        got,
         parts,
         target,
+        *shapes,
+        limit=8,
     )
 
 
@@ -388,9 +455,9 @@
     got = exchange(send.reshape(n_tile, 2, LANES), TILE_AXES).reshape(2 * n_tile, LANES)
     target = jnp.transpose(density_map.reshape(PLANE, EDGE))
     parts = exchange(splat(got, n_seg), "seg")
-    pulled = pull(got, parts, target)
+    pulled = pull(parts, target, shape(got, target))
     back = exchange(pulled.reshape(n_tile, 4, LANES), TILE_AXES).reshape(4 * n_tile, LANES)
-    near, far = ("core", "seg"), ("y", "z")
+    near, far = ("z", "core"), ("y", "seg")
     forces, spread, score = finish(
         back, picks, modes, float(n_tile * EDGE**3), a_dev * n_tile * n_seg, lax.axis_size(near)
     )

time: 110 us -> 118 us (1.073)
  blocking collectives: 76 us -> 46.1 us
  starting transfers between devices: 4.01 us -> 22.4 us
  local copies, waits for them, and re-layouts: 0.3 us -> 13.5 us
  waiting for transfers between devices: 7.26 us -> 10.7 us
  Pallas kernels: 20.5 us -> 22.4 us
    all_to_all x4 -> x3, blocking collectives: 76 us -> 46.1 us  [exchange(): return lax.all_to_all(values, axes, split_axis=0, concat_axis=0, tiled=True)]
    all_to_all x1 -> x2, starting transfers between devices: 4.01 us -> 22.4 us  [exchange(): return lax.all_to_all(values, axes, split_axis=0, concat_axis=0, tiled=True)]
    unnamed x6 -> x12, local copies, waits for them, and re-layouts: 0.01 us -> 13.2 us
    all_to_all x1 -> x2, waiting for transfers between devices: 7.26 us -> 10.7 us  [exchange(): return lax.all_to_all(values, axes, split_axis=0, concat_axis=0, tiled=True)]
    pallas_call x4 -> x5, Pallas kernels: 20.5 us -> 22.4 us  [call(): pl.pallas_call(kernel, out_shape=out_shape, in_specs=[pl.BlockSpec(memory...]
  transfers between devices with their start and end apart: 1 -> 2, of which waited for: 1 -> 1; matrix products, arithmetic and copies ran while one was open for 1% -> 1% of each run, Pallas kernels for 0% -> 4%
where the time goes in v6:
time: 118 us
  blocking collectives  46.1 us (39%)
  Pallas kernels  22.4 us (19%)
  starting transfers between devices  22.4 us (19%)
  local copies, waits for them, and re-layouts  13.5 us (11%)
  waiting for transfers between devices  10.7 us (9%)
  other arithmetic  1.9 us (2%)
    all_to_all x3, blocking collectives, exchange(): return lax.all_to_all(values, axes, split_axis=0, concat_axis=0, tiled=True)  46.1 us
    all_to_all x2, starting transfers between devices, exchange(): return lax.all_to_all(values, axes, split_axis=0, concat_axis=0, tiled=True)  22.4 us
    pallas_call x5, Pallas kernels, call(): pl.pallas_call(kernel, out_shape=out_shape, in_specs=[pl.BlockSpec(memory...  22.4 us
    unnamed x12, local copies, waits for them, and re-layouts  13.2 us
    all_to_all x2, waiting for transfers between devices, exchange(): return lax.all_to_all(values, axes, split_axis=0, concat_axis=0, tiled=True)  10.7 us
  transfers between devices with their start and end apart: 2, of which 1 were waited for; matrix products, arithmetic and copies ran while one was open for 1% of the time, Pallas kernels for 4%

profile of v6, /device:TPU:1, one launch (start us, length us, event | category | flops | bytes accessed | tf_op | source)
XLA Modules:
  0.0 117.6 jit_solution(1846255423441836246)
XLA Ops:
  0.6 2.8 %pack.1 = (f32[256,128]{1,0:T(8,128)}, bf16[2,32,128]{2,1,0:T(8,128)(2,1)}) custom-call(s32[4,32]{1,0:T(4,128)} %bitcast.27, s32[3,4,32]{2,1,0:T(4,128)} %bitcast.25, f32[1,256]{1,0:T(1,128)} %bitcast.28, f32[3,1024]{1,0:T(4,128)} %refs_3_.1, f32[8,128]{1,0:T(8,128)} %bitcast.26, bf16[3,256,1024]{2,1,0:T(8,128)(2,1)} %bitcast.21), custom_call_target="tpu_custom_call" | custom-call | flops 67108864 | bytes 1048576 | tf_op jit(solution)/shard_map/pack/pallas_call | solution.py:320
  3.4 18.4 %all-to-all-start = ((f32[128,2,128]{2,1,0:T(2,128)}), f32[128,2,128]{2,1,0:T(2,128)S(1)}, u32[]{:S(2)}, u32[]{:S(2)}) async-start(f32[128,2,128]{2,1,0:T(2,128)} %bitcast.23), calls=%async_computation | async-start | bytes 262144 | tf_op jit(solution)/shard_map/all_to_all | solution.py:438
  21.9 1.3 %reduce = bf16[32768]{0:T(1024)(128)(2,1)S(1)} reduce(bf16[1,32768]{1,0:T(2,128)(2,1)} %param.11, bf16[]{:T(256)} %constant.5), dimensions={0}, to_apply=%param.11.reduce_sub_computation | reduce | bytes 131074 | tf_op args[4]
  23.1 0.2 reshape.38
  23.3 0.1 copy.12
  23.4 10.7 %all-to-all-done = f32[128,2,128]{2,1,0:T(2,128)S(1)} async-done(((f32[128,2,128]{2,1,0:T(2,128)}), f32[128,2,128]{2,1,0:T(2,128)S(1)}, u32[]{:S(2)}, u32[]{:S(2)}) %all-to-all-start) | async-done | bytes 131104 | tf_op jit(solution)/shard_map/all_to_all | solution.py:438
  34.1 7.2 %splat.1 = f32[4,32,1024]{2,1,0:T(8,128)} custom-call(f32[256,128]{1,0:T(8,128)S(1)} %bitcast.18), custom_call_target="tpu_custom_call" | custom-call | flops 536870912 | bytes 1048576 | tf_op jit(solution)/shard_map/splat/pallas_call | solution.py:320
  41.3 4.0 %all-to-all-start.1 = ((f32[4,32,1024]{2,1,0:T(8,128)}), f32[4,32,1024]{2,1,0:T(8,128)S(1)}, u32[]{:S(2)}, u32[]{:S(2)}) async-start(f32[4,32,1024]{2,1,0:T(8,128)} %splat.1), calls=%async_computation.1 | async-start | bytes 1048576 | tf_op jit(solution)/shard_map/all_to_all | solution.py:438
  45.3 5.3 %shape.1 = (bf16[8,1024,512]{2,1,0:T(8,128)(2,1)S(1)}, bf16[8,1024,512]{2,1,0:T(8,128)(2,1)S(1)}, bf16[2,8,2,32,512]{4,3,2,1,0:T(8,128)(2,1)S(1)}, f32[4,64,128]{2,1,0:T(8,128)S(1)}, f32[3,64,128]{2,1,0:T(8,128)S(1)}) custom-call(f32[256,128]{1,0:T(8,128)S(1)} %bitcast.19, bf16[32,1024]{1,0:T(8,128)(2,1)S(1)} %bitcast.15), custom_call_target="tpu_custom_call" | custom-call | flops 4294967296 | bytes 1048576 | tf_op jit(solution)/shard_map/shape/pallas_call | solution.py:320
  50.6 0.0 copy-start
  50.6 3.2 %copy-done = bf16[8,1024,512]{2,1,0:T(8,128)(2,1)} copy-done((bf16[8,1024,512]{2,1,0:T(8,128)(2,1)}, bf16[8,1024,512]{2,1,0:T(8,128)(2,1)S(1)}, u32[]{:S(2)}) %copy-start) | copy-done | bytes 8388632
  53.8 0.0 copy-start.2
  53.8 3.2 %copy-done.2 = bf16[8,1024,512]{2,1,0:T(8,128)(2,1)} copy-done((bf16[8,1024,512]{2,1,0:T(8,128)(2,1)}, bf16[8,1024,512]{2,1,0:T(8,128)(2,1)S(1)}, u32[]{:S(2)}) %copy-start.2) | copy-done | bytes 8388632
  57.0 0.0 all-to-all-done.1.parts_ref
  57.0 0.0 copy-start.1
  57.0 3.4 %copy-done.1 = bf16[8,1024,512]{2,1,0:T(8,128)(2,1)S(1)} copy-done((bf16[8,1024,512]{2,1,0:T(8,128)(2,1)S(1)}, bf16[8,1024,512]{2,1,0:T(8,128)(2,1)}, u32[]{:S(2)}) %copy-start.1) | copy-done | bytes 8388632
  60.4 0.0 copy-start.3
  60.4 3.4 %copy-done.3 = bf16[8,1024,512]{2,1,0:T(8,128)(2,1)S(1)} copy-done((bf16[8,1024,512]{2,1,0:T(8,128)(2,1)S(1)}, bf16[8,1024,512]{2,1,0:T(8,128)(2,1)}, u32[]{:S(2)}) %copy-start.3) | copy-done | bytes 8388632
  63.8 0.0 copy-start.4
  63.8 0.0 copy-start.5
  63.8 5.1 %pull.1 = f32[512,128]{1,0:T(8,128)S(1)} custom-call(f32[4,32,1024]{2,1,0:T(8,128)S(1)} %all-to-all-done.1.parts_ref, bf16[32,1024]{1,0:T(8,128)(2,1)S(1)} %bitcast.16, bf16[8,1024,512]{2,1,0:T(8,128)(2,1)S(1)} %copy-done.1, bf16[8,1024,512]{2,1,0:T(8,128)(2,1)S(1)} %copy-done.3, bf16[2,8,2,32,512]{4,3,2,1,0:T(8,128)(2,1)S(1)} %get-tuple-element.16.weight_ref, ...), custom_call_target="tpu_custom_call" | custom-call | flops 4294967296 | bytes 1048576 | tf_op jit(solution)/shard_map/pull/pallas_call | solution.py:320
  68.9 20.2 %all_to_all.25 = f32[128,4,128]{2,1,0:T(4,128)S(1)} all-to-all(f32[128,4,128]{2,1,0:T(4,128)S(1)} %bitcast.14), channel_id=1, replica_groups=mesh['y'=8,'z'=8,'core'=2,'seg'=4] {'y','z','core'}, dimensions={0} | all-to-all | bytes 524288 | tf_op jit(solution)/shard_map/all_to_all | solution.py:438
  89.1 0.0 copy-done.4
  89.1 0.0 copy-done.5
  89.1 2.0 %finish.1 = (f32[3,1024]{1,0:T(4,128)}, f32[32,128]{1,0:T(8,128)S(1)}, f32[1,128]{1,0:T(1,128)}) custom-call(f32[512,128]{1,0:T(8,128)S(1)} %bitcast.17, bf16[2,32,128]{2,1,0:T(8,128)(2,1)S(1)} %copy-done.5, bf16[3,256,1024]{2,1,0:T(8,128)(2,1)S(1)} %bitcast.22), custom_call_target="tpu_custom_call" | custom-call | flops 67108864 | bytes 1048576 | tf_op jit(solution)/shard_map/finish/pallas_call | solution.py:320
  91.1 11.5 %all_to_all.26 = f32[16,2,128]{2,1,0:T(2,128)S(1)} all-to-all(f32[16,2,128]{2,1,0:T(2,128)S(1)} %bitcast.20), channel_id=1, replica_groups=mesh['y'=8,'z'=8,'core'=2,'seg'=4] {'z','core'}, dimensions={0} | all-to-all | bytes 32768 | tf_op jit(solution)/shard_map/all_to_all | solution.py:438
  102.6 14.4 %all_to_all.27 = f32[32,2,128]{2,1,0:T(2,128)S(1)} all-to-all(f32[32,2,128]{2,1,0:T(2,128)S(1)} %broadcast_in_dim.2), channel_id=1, replica_groups=mesh['y'=8,'z'=8,'core'=2,'seg'=4] {'y','seg'}, dimensions={0} | all-to-all | bytes 65536 | tf_op jit(solution)/shard_map/all_to_all | solution.py:438
  117.0 0.6 reduce_sum.19
  (2 shorter events, 0.0 us)
Async XLA Ops:
  3.4 30.6 %all-to-all-start = ((f32[128,2,128]{2,1,0:T(2,128)}), f32[128,2,128]{2,1,0:T(2,128)S(1)}, u32[]{:S(2)}, u32[]{:S(2)}) async-start(f32[128,2,128]{2,1,0:T(2,128)} %bitcast.23), calls=%async_computation | async-start | bytes 262144 | tf_op jit(solution)/shard_map/all_to_all | solution.py:438
  41.3 15.7 %all-to-all-start.1 = ((f32[4,32,1024]{2,1,0:T(8,128)}), f32[4,32,1024]{2,1,0:T(8,128)S(1)}, u32[]{:S(2)}, u32[]{:S(2)}) async-start(f32[4,32,1024]{2,1,0:T(8,128)} %splat.1), calls=%async_computation.1 | async-start | bytes 1048576 | tf_op jit(solution)/shard_map/all_to_all | solution.py:438
  50.6 3.2 %copy-start = (bf16[8,1024,512]{2,1,0:T(8,128)(2,1)}, bf16[8,1024,512]{2,1,0:T(8,128)(2,1)S(1)}, u32[]{:S(2)}) copy-start(bf16[8,1024,512]{2,1,0:T(8,128)(2,1)S(1)} %get-tuple-element.14.even_ref) | copy-start | bytes 25165828
  53.8 3.2 %copy-start.2 = (bf16[8,1024,512]{2,1,0:T(8,128)(2,1)}, bf16[8,1024,512]{2,1,0:T(8,128)(2,1)S(1)}, u32[]{:S(2)}) copy-start(bf16[8,1024,512]{2,1,0:T(8,128)(2,1)S(1)} %get-tuple-element.15.odd_ref) | copy-start | bytes 25165828
  57.0 3.4 %copy-start.1 = (bf16[8,1024,512]{2,1,0:T(8,128)(2,1)S(1)}, bf16[8,1024,512]{2,1,0:T(8,128)(2,1)}, u32[]{:S(2)}) copy-start(bf16[8,1024,512]{2,1,0:T(8,128)(2,1)} %copy-done) | copy-start | bytes 25165828
  60.4 3.4 %copy-start.3 = (bf16[8,1024,512]{2,1,0:T(8,128)(2,1)S(1)}, bf16[8,1024,512]{2,1,0:T(8,128)(2,1)}, u32[]{:S(2)}) copy-start(bf16[8,1024,512]{2,1,0:T(8,128)(2,1)} %copy-done.2) | copy-start | bytes 25165828
  63.8 25.3 %copy-start.4 = (bf16[256,3,1024]{2,0,1:T(8,128)(2,1)S(1)}, bf16[256,3,1024]{2,0,1:T(8,128)(2,1)}, u32[]{:S(2)}) copy-start(bf16[256,3,1024]{2,0,1:T(8,128)(2,1)} %param.9) | copy-start | bytes 4718596
  63.8 25.3 %copy-start.5 = (bf16[2,32,128]{2,1,0:T(8,128)(2,1)S(1)}, bf16[2,32,128]{2,1,0:T(8,128)(2,1)}, u32[]{:S(2)}) copy-start(bf16[2,32,128]{2,1,0:T(8,128)(2,1)} %get-tuple-element.19.refs_1_) | copy-start | bytes 49156

commit v7 on v6

--- a/solution.py
+++ b/solution.py
@@ -12,19 +12,30 @@
 ATOM_BLOCK = 32
 PLANE = EDGE * EDGE
 LANES = 128
-SPLAT_CHUNK = 512
-PULL_CHUNK = 512
+CHUNK = 512
 WIDTH = 256
 
+STEP = 4
+HIGHS = EDGE // STEP
+MIDDLE = EDGE / 2
+FAR = 40.0
+
 inverse_var = 1.0 / 2.25
-half_log = -0.5 * inverse_var / math.log(2.0)
-
-
-def factors(places):
-    centers = lax.broadcasted_iota(jnp.int32, (EDGE, places.shape[1]), 0).astype(jnp.float32) + 0.5
+rate = 0.5 * inverse_var / math.log(2.0)
+
+
+def row_number(rows, columns):
+    return lax.broadcasted_iota(jnp.int32, (rows, columns), 0)
+
+
+def factors(places, centers):
     distance = centers - places
-    profile = jnp.exp2(half_log * (distance * distance))
+    profile = jnp.exp2(-rate * (distance * distance))
     return profile, inverse_var * distance * profile
+
+
+def centers_of(columns):
+    return row_number(EDGE, columns).astype(jnp.float32) + 0.5
 
 
 def exact_parts(values):
@@ -174,42 +185,75 @@
         use(1, 2 * step + 1)
 
 
-def build_plane(place_ref, line_ref, plane_ref, slot, chunk, size):
-    along_x = factors(chunk_row(place_ref, 0, chunk, size))[0].astype(jnp.bfloat16)
-    along_z = factors(chunk_row(place_ref, 2, chunk, size))[0].astype(jnp.bfloat16)
-    line_ref[slot] = along_z.astype(jnp.float32)
-    for z in range(EDGE):
-        line = jnp.broadcast_to(line_ref[slot, pl.ds(z, 1), :], (EDGE, size))
-        plane_ref[pl.ds(z * EDGE, EDGE), :] = line.astype(jnp.bfloat16) * along_x
-
-
-def splat_kernel(got_ref, out_ref, place_ref, line_ref, weight_ref, plane_ref, sum_ref):
-    size = plane_ref.shape[2]
+def pair_of_lines(line_ref, z, size):
+    return jnp.concatenate(
+        [jnp.broadcast_to(line_ref[pl.ds(z + i, 1), :], (HIGHS, size)) for i in range(2)], axis=0
+    )
+
+
+def splat_kernel(got_ref, out_ref, place_ref, line_ref, even_ref, odd_ref, even_weight_ref, odd_weight_ref, sum_ref):
+    size = even_ref.shape[1]
+    planes, weights = (even_ref, odd_ref), (even_weight_ref, odd_weight_ref)
     unpack_rows(got_ref, place_ref)
     sum_ref[...] = jnp.zeros_like(sum_ref)
+    lows = [low + 0.5 - STEP / 2 for low in range(STEP)]
 
     def build(slot, chunk):
-        build_plane(place_ref, line_ref, plane_ref.at[slot], slot, chunk, size)
-        along_y = factors(chunk_row(place_ref, 1, chunk, size))[0]
-        weight_ref[slot] = (chunk_row(place_ref, 3, chunk, size) * along_y).astype(jnp.bfloat16)
+        place_x, place_y, place_z, masses = [chunk_row(place_ref, i, chunk, size) for i in range(4)]
+        place_x = place_x - MIDDLE
+        coarse = STEP * row_number(HIGHS, size).astype(jnp.float32) + (STEP / 2 - MIDDLE)
+        along_x = factors(place_x, coarse)[0]
+        line_ref[slot] = factors(place_z, centers_of(size))[0]
+        for z in range(0, EDGE, 2):
+            line = pair_of_lines(line_ref.at[slot], z, size)
+            block = line * jnp.concatenate([along_x, along_x], axis=0)
+            planes[slot][pl.ds(z * HIGHS, 2 * HIGHS), :] = block.astype(jnp.bfloat16)
+        along_y = masses * factors(place_y, centers_of(size))[0]
+        near = jnp.clip(place_x, -FAR, FAR)
+        for low in range(STEP):
+            fine = jnp.exp2((2.0 * rate * lows[low]) * near)
+            weights[slot][pl.ds(low * EDGE, EDGE), :] = (along_y * fine).astype(jnp.bfloat16)
 
     def use(slot, chunk):
-        for half in range(2):
-            rows = pl.ds(half * PLANE // 2, PLANE // 2)
-            sum_ref[rows, :] += against_rows(plane_ref[slot, rows, :], weight_ref[slot])
+        width = min(WIDTH, size)
+        for part in range(size // width):
+            atoms = pl.ds(part * width, width)
+            sum_ref[...] += against_rows(planes[slot][:, atoms], weights[slot][:, atoms])
 
     pipeline(place_ref.shape[1] * LANES // size, build, use)
     total = sum_ref[...].T
-    for copy in range(out_ref.shape[0]):
-        out_ref[copy] = total
-
-
-middle = EDGE / 2
+    high = (lax.broadcasted_iota(jnp.int32, (EDGE, EDGE * HIGHS), 1) % HIGHS).astype(jnp.float32)
+    coarse = STEP * high + (STEP / 2 - MIDDLE)
+    for low in range(STEP):
+        scale = jnp.exp2(-rate * (2.0 * lows[low] * coarse + lows[low] ** 2))
+        block = total[low * EDGE : (low + 1) * EDGE] * scale
+        for copy in range(out_ref.shape[0]):
+            out_ref[copy, :, pl.ds(low * EDGE * HIGHS, EDGE * HIGHS)] = block
+
+
+def build_shape(place_ref, line_ref, plane_ref, weight_ref, chunk, size):
+    place_x, place_y, place_z, masses = [chunk_row(place_ref, i, chunk, size) for i in range(4)]
+    row = row_number(EDGE, size)
+    centers = (STEP * (row % HIGHS) + row // HIGHS).astype(jnp.float32) + 0.5
+    along_x = factors(place_x, centers)[0]
+    doubled = []
+    for low in range(STEP):
+        block = along_x[low * HIGHS : (low + 1) * HIGHS]
+        doubled.append(jnp.concatenate([block, block], axis=0).astype(jnp.bfloat16))
+    line_ref[...] = factors(place_z, centers_of(size))[0].astype(jnp.bfloat16).astype(jnp.float32)
+    for z in range(0, EDGE, 2):
+        line = pair_of_lines(line_ref, z, size).astype(jnp.bfloat16)
+        for low in range(STEP):
+            plane_ref[pl.ds(low * EDGE * HIGHS + z * HIGHS, 2 * HIGHS), :] = line * doubled[low]
+    profile_y, slope_y = factors(place_y, centers_of(size))
+    weight_ref[0] = (masses * profile_y).astype(jnp.bfloat16).astype(jnp.float32)
+    weight_ref[1] = (masses * slope_y).astype(jnp.bfloat16).astype(jnp.float32)
 
 
 def voxel_centers():
     voxel = lax.broadcasted_iota(jnp.int32, (EDGE, PLANE), 1)
-    return [part.astype(jnp.float32) + (0.5 - middle) for part in (voxel % EDGE, voxel // EDGE)]
+    low, z, high = voxel // (EDGE * HIGHS), voxel // HIGHS % EDGE, voxel % HIGHS
+    return [part.astype(jnp.float32) + (0.5 - MIDDLE) for part in (STEP * high + low, z)]
 
 
 def store_rows(row_ref, arrays):
@@ -223,80 +267,60 @@
 
 def take_forces(sum_ref, chunk, sums, weights, places):
     plain, by_x, by_z = sums
-    along_y, slope_y = [weight.astype(jnp.float32) for weight in weights]
+    along_y, slope_y = weights
     whole, force_y, moment_x, moment_z = [
         jnp.sum(values * weight, axis=0, keepdims=True)
         for values, weight in ((plain, along_y), (plain, slope_y), (by_x, along_y), (by_z, along_y))
     ]
-    force_x = inverse_var * (moment_x - (places[0] - middle) * whole)
-    force_z = inverse_var * (moment_z - (places[1] - middle) * whole)
+    force_x = inverse_var * (moment_x - (places[0] - MIDDLE) * whole)
+    force_z = inverse_var * (moment_z - (places[1] - MIDDLE) * whole)
     rows = whole.shape[1] // LANES
     for component, force in enumerate((force_x, force_y, force_z)):
         for i in range(rows):
             sum_ref[component, pl.ds(chunk * rows + i, 1), :] = force[:, i * LANES : (i + 1) * LANES]
 
 
-def shape_kernel(got_ref, target_ref, even_ref, odd_ref, weight_ref, place_ref, sum_ref, line_ref, row_ref):
+def pull_rows(single, place_ref, row_ref, sum_ref, line_ref, even_ref, odd_ref, weight_ref):
     planes = (even_ref, odd_ref)
-    size = even_ref.shape[2]
+    size = even_ref.shape[1]
     width = min(WIDTH, size)
+
+    def build(slot, chunk):
+        build_shape(place_ref, line_ref.at[slot], planes[slot], weight_ref.at[slot], chunk, size)
+
+    def use(slot, chunk):
+        for part in range(size // width):
+            atoms = pl.ds(part * width, width)
+            small = chunk * (size // width) + part
+            pulled = jnp.dot(row_ref[...], planes[slot][:, atoms], preferred_element_type=jnp.float32)
+            block = [pulled[i : i + EDGE] for i in range(0, pulled.shape[0], EDGE)]
+            plain = block[0] if single else block[0] + block[1]
+            block = block[1:] if single else block[2:]
+            take_forces(
+                sum_ref,
+                small,
+                (plain, block[0] + block[1], block[2] + block[3]),
+                [weight_ref[slot, i, :, atoms] for i in range(2)],
+                [chunk_row(place_ref, i, small, width) for i in (0, 2)],
+            )
+
+    pipeline(place_ref.shape[1] * LANES // size, build, use)
+
+
+def map_kernel(got_ref, target_ref, sum_ref, place_ref, row_ref, *scratch):
     unpack_rows(got_ref, place_ref)
     wide = target_ref[...].astype(jnp.float32)
     center_x, center_z = voxel_centers()
     store_rows(row_ref, (target_ref[...], wide * center_x, wide * center_z))
-
-    def build(slot, chunk):
-        build_plane(place_ref, line_ref, planes[slot].at[chunk // 2], slot, chunk, size)
-        profile_y, slope_y = factors(chunk_row(place_ref, 1, chunk, size))
-        masses = chunk_row(place_ref, 3, chunk, size)
-        weight_ref[slot, chunk // 2, 0] = (masses * profile_y).astype(jnp.bfloat16)
-        weight_ref[slot, chunk // 2, 1] = (masses * slope_y).astype(jnp.bfloat16)
-
-    def use(slot, chunk):
-        for part in range(size // width):
-            atoms = pl.ds(part * width, width)
-            small = chunk * (size // width) + part
-            pulled = jnp.dot(
-                row_ref[...], planes[slot][chunk // 2, :, atoms], preferred_element_type=jnp.float32
-            )
-            block = [pulled[i * EDGE : (i + 1) * EDGE] for i in range(5)]
-            take_forces(
-                sum_ref,
-                small,
-                (block[0], block[1] + block[2], block[3] + block[4]),
-                [weight_ref[slot, chunk // 2, i, :, atoms] for i in range(2)],
-                [chunk_row(place_ref, i, small, width) for i in (0, 2)],
-            )
-
-    pipeline(place_ref.shape[1] * LANES // size, build, use)
-
-
-def pull_kernel(parts_ref, target_ref, even_ref, odd_ref, weight_ref, place_ref, map_ref, out_ref, row_ref, sum_ref):
-    planes = (even_ref, odd_ref)
-    size = even_ref.shape[2]
-    width = min(WIDTH, size)
+    pull_rows(True, place_ref, row_ref, sum_ref, *scratch)
+
+
+def pull_kernel(got_ref, parts_ref, target_ref, map_ref, out_ref, place_ref, row_ref, sum_ref, *scratch):
+    unpack_rows(got_ref, place_ref)
     density = (parts_ref[0] + parts_ref[2]) + (parts_ref[1] + parts_ref[3])
     center_x, center_z = voxel_centers()
     store_rows(row_ref, (density, density * center_x, density * center_z))
-
-    @pl.loop(0, even_ref.shape[0])
-    def _(step):
-        for slot in range(2):
-            for part in range(size // width):
-                atoms = pl.ds(part * width, width)
-                small = (2 * step + slot) * (size // width) + part
-                pulled = jnp.dot(
-                    row_ref[...], planes[slot][step, :, atoms], preferred_element_type=jnp.float32
-                )
-                block = [pulled[i * EDGE : (i + 1) * EDGE] for i in range(6)]
-                take_forces(
-                    sum_ref,
-                    small,
-                    (block[0] + block[1], block[2] + block[3], block[4] + block[5]),
-                    [weight_ref[slot, step, i, :, atoms] for i in range(2)],
-                    [chunk_row(place_ref, i, small, width) for i in (0, 2)],
-                )
-
+    pull_rows(False, place_ref, row_ref, sum_ref, *scratch)
     wide = target_ref[...].astype(jnp.float32)
     pairs = place_ref.shape[1]
     left = lax.broadcasted_iota(jnp.int32, (pairs, LANES), 1) < LANES // 2
@@ -369,7 +393,9 @@
 
 def splat(got, copies):
     groups = got.shape[0] // 4
-    size = min(SPLAT_CHUNK, groups * LANES // 2)
+    size = min(CHUNK, groups * LANES // 2)
+    plane = ((EDGE * HIGHS, size), jnp.bfloat16)
+    weight = ((EDGE * STEP, size), jnp.bfloat16)
     return call(
         splat_kernel,
         "splat",
@@ -377,57 +403,53 @@
         [
             ((4, groups, LANES), jnp.float32),
             ((2, EDGE, size), jnp.float32),
-            ((2, EDGE, size), jnp.bfloat16),
-            ((2, PLANE, size), jnp.bfloat16),
-            ((PLANE, EDGE), jnp.float32),
+            plane,
+            plane,
+            weight,
+            weight,
+            ((EDGE * HIGHS, EDGE * STEP), jnp.float32),
         ],
         2**29,
         got,
     )
 
 
-def shape(got, target):
+def shape_scratch(groups):
+    size = min(CHUNK, groups * LANES // 2)
+    plane = ((PLANE, size), jnp.bfloat16)
+    return [((2, EDGE, size), jnp.float32), plane, plane, ((2, 2, EDGE, size), jnp.float32)]
+
+
+def pull_map(got, target):
     groups = got.shape[0] // 4
-    atoms = groups * LANES
-    size = min(PULL_CHUNK, atoms // 2)
-    chunks = atoms // size
-    plane = pltpu.VMEM((chunks // 2, PLANE, size), jnp.bfloat16)
     return call(
-        shape_kernel,
-        "shape",
-        (
-            plane,
-            plane,
-            pltpu.VMEM((2, chunks // 2, 2, EDGE, size), jnp.bfloat16),
-            pltpu.VMEM((4, groups, LANES), jnp.float32),
-            pltpu.VMEM((3, groups, LANES), jnp.float32),
-        ),
-        [
-            ((2, EDGE, size), jnp.float32),
-            ((5 * EDGE, PLANE), jnp.bfloat16),
-        ],
+        map_kernel,
+        "pull_map",
+        jax.ShapeDtypeStruct((3, groups, LANES), jnp.float32),
+        [((4, groups, LANES), jnp.float32), ((5 * EDGE, PLANE), jnp.bfloat16)] + shape_scratch(groups),
         2**32,
         got,
         target,
-        limit=8,
-    )
-
-
-def pull(parts, target, shapes):
-    groups = shapes[3].shape[1]
+    )
+
+
+def pull(got, parts, target, from_map):
+    groups = got.shape[0] // 4
     return call(
         pull_kernel,
         "pull",
         jax.ShapeDtypeStruct((8 * groups, LANES), jnp.float32),
         [
+            ((4, groups, LANES), jnp.float32),
             ((6 * EDGE, PLANE), jnp.bfloat16),
             ((3, groups, LANES), jnp.float32),
-        ],
+        ]
+        + shape_scratch(groups),
         2**32,
+        got,
         parts,
         target,
-        *shapes,
-        limit=8,
+        from_map,
     )
 
 
@@ -453,9 +475,10 @@
         n_tile,
     )
     got = exchange(send.reshape(n_tile, 2, LANES), TILE_AXES).reshape(2 * n_tile, LANES)
-    target = jnp.transpose(density_map.reshape(PLANE, EDGE))
+    target = density_map.reshape(EDGE, HIGHS, STEP, EDGE)
+    target = jnp.transpose(target, (3, 2, 0, 1)).reshape(EDGE, PLANE)
     parts = exchange(splat(got, n_seg), "seg")
-    pulled = pull(parts, target, shape(got, target))
+    pulled = pull(got, parts, target, pull_map(got, target))
     back = exchange(pulled.reshape(n_tile, 4, LANES), TILE_AXES).reshape(4 * n_tile, LANES)
     near, far = ("z", "core"), ("y", "seg")
     forces, spread, score = finish(

time: 118 us -> 104 us (0.88)
  local copies, waits for them, and re-layouts: 13.5 us -> 0.34 us
  waiting for transfers between devices: 10.7 us -> 14.3 us
  Pallas kernels: 22.4 us -> 19.6 us
    unnamed x12 -> x6, local copies, waits for them, and re-layouts: 13.2 us -> 0.02 us
    all_to_all x2, waiting for transfers between devices: 10.7 us -> 14.3 us  [exchange(): return lax.all_to_all(values, axes, split_axis=0, concat_axis=0, tiled=True)]
    pallas_call x5, Pallas kernels: 22.4 us -> 19.6 us  [call(): pl.pallas_call(kernel, out_shape=out_shape, in_specs=[pl.BlockSpec(memory...]
  transfers between devices with their start and end apart: 2 -> 2, of which waited for: 1 -> 2; matrix products, arithmetic and copies ran while one was open for 1% -> 1% of each run, Pallas kernels for 4% -> 5%
where the time goes in v7:
time: 104 us; the launch traced here: 103 us
  blocking collectives  45 us (43%)
  starting transfers between devices  22.5 us (22%)
  Pallas kernels  19.6 us (19%)
  waiting for transfers between devices  14.3 us (14%)
    all_to_all x3, blocking collectives, exchange(): return lax.all_to_all(values, axes, split_axis=0, concat_axis=0, tiled=True)  45 us
    all_to_all x2, starting transfers between devices, exchange(): return lax.all_to_all(values, axes, split_axis=0, concat_axis=0, tiled=True)  22.5 us
    pallas_call x5, Pallas kernels, call(): pl.pallas_call(kernel, out_shape=out_shape, in_specs=[pl.BlockSpec(memory...  19.6 us
    all_to_all x2, waiting for transfers between devices, exchange(): return lax.all_to_all(values, axes, split_axis=0, concat_axis=0, tiled=True)  14.3 us
  transfers between devices with their start and end apart: 2, of which 2 were waited for; matrix products, arithmetic and copies ran while one was open for 1% of the time, Pallas kernels for 5%

profile of v7, /device:TPU:1, one launch (start us, length us, event | category | flops | bytes accessed | tf_op | source)
XLA Modules:
  0.0 103.4 jit_solution(6906797524678167088)
XLA Ops:
  0.6 0.0 copy-start.2
  0.6 2.8 %pack.1 = (f32[256,128]{1,0:T(8,128)}, bf16[2,32,128]{2,1,0:T(8,128)(2,1)}) custom-call(s32[4,32]{1,0:T(4,128)} %bitcast.29, s32[3,4,32]{2,1,0:T(4,128)} %bitcast.27, f32[1,256]{1,0:T(1,128)} %bitcast.30, f32[3,1024]{1,0:T(4,128)} %refs_3_.1, f32[8,128]{1,0:T(8,128)} %bitcast.28, bf16[3,256,1024]{2,1,0:T(8,128)(2,1)} %bitcast.22), custom_call_target="tpu_custom_call" | custom-call | flops 67108864 | bytes 1048576 | tf_op jit(solution)/shard_map/pack/pallas_call | solution.py:344
  3.5 18.4 %all-to-all-start = ((f32[128,2,128]{2,1,0:T(2,128)}), f32[128,2,128]{2,1,0:T(2,128)S(1)}, u32[]{:S(2)}, u32[]{:S(2)}) async-start(f32[128,2,128]{2,1,0:T(2,128)} %bitcast.25), calls=%async_computation | async-start | bytes 262144 | tf_op jit(solution)/shard_map/all_to_all | solution.py:460
  21.9 0.0 copy-done.2
  21.9 0.4 reduce
  22.3 0.2 reshape.41
  22.5 0.1 copy.19.target_ref
  22.6 11.5 %all-to-all-done = f32[128,2,128]{2,1,0:T(2,128)S(1)} async-done(((f32[128,2,128]{2,1,0:T(2,128)}), f32[128,2,128]{2,1,0:T(2,128)S(1)}, u32[]{:S(2)}, u32[]{:S(2)}) %all-to-all-start) | async-done | bytes 131104 | tf_op jit(solution)/shard_map/all_to_all | solution.py:460
  34.1 3.8 %splat.1 = f32[4,32,1024]{2,1,0:T(8,128)} custom-call(f32[256,128]{1,0:T(8,128)S(1)} %bitcast.18), custom_call_target="tpu_custom_call" | custom-call | flops 536870912 | bytes 1048576 | tf_op jit(solution)/shard_map/splat/pallas_call | solution.py:344
  37.9 4.0 %all-to-all-start.1 = ((f32[4,32,1024]{2,1,0:T(8,128)}), f32[4,32,1024]{2,1,0:T(8,128)S(1)}, u32[]{:S(2)}, u32[]{:S(2)}) async-start(f32[4,32,1024]{2,1,0:T(8,128)} %splat.1), calls=%async_computation.1 | async-start | bytes 1048576 | tf_op jit(solution)/shard_map/all_to_all | solution.py:460
  42.0 5.1 %pull_map.1.map_ref = f32[3,64,128]{2,1,0:T(8,128)S(1)} custom-call(f32[256,128]{1,0:T(8,128)S(1)} %bitcast.19, bf16[32,1024]{1,0:T(8,128)(2,1)S(1)} %copy.19.target_ref), custom_call_target="tpu_custom_call" | custom-call | flops 4294967296 | bytes 1048576 | tf_op jit(solution)/shard_map/pull_map/pallas_call | solution.py:344
  47.1 0.0 copy-start
  47.1 0.0 copy-start.1
  47.1 2.8 %all-to-all-done.1.parts_ref = f32[4,32,1024]{2,1,0:T(8,128)S(1)} async-done(((f32[4,32,1024]{2,1,0:T(8,128)}), f32[4,32,1024]{2,1,0:T(8,128)S(1)}, u32[]{:S(2)}, u32[]{:S(2)}) %all-to-all-start.1) | async-done | bytes 524320 | tf_op jit(solution)/shard_map/all_to_all | solution.py:460
  49.9 5.9 %pull.1 = f32[512,128]{1,0:T(8,128)S(1)} custom-call(f32[256,128]{1,0:T(8,128)S(1)} %bitcast.20, f32[4,32,1024]{2,1,0:T(8,128)S(1)} %all-to-all-done.1.parts_ref, bf16[32,1024]{1,0:T(8,128)(2,1)S(1)} %copy.19.target_ref, f32[3,64,128]{2,1,0:T(8,128)S(1)} %pull_map.1.map_ref), custom_call_target="tpu_custom_call" | custom-call | flops 4294967296 | bytes 1048576 | tf_op jit(solution)/shard_map/pull/pallas_call | solution.py:344
  55.8 21.5 %all_to_all.25 = f32[128,4,128]{2,1,0:T(4,128)S(1)} all-to-all(f32[128,4,128]{2,1,0:T(4,128)S(1)} %bitcast.17), channel_id=1, replica_groups=mesh['y'=8,'z'=8,'core'=2,'seg'=4] {'y','z','core'}, dimensions={0} | all-to-all | bytes 524288 | tf_op jit(solution)/shard_map/all_to_all | solution.py:460
  77.3 0.0 copy-done
  77.3 0.0 copy-done.1
  77.3 2.0 %finish.1 = (f32[3,1024]{1,0:T(4,128)}, f32[32,128]{1,0:T(8,128)S(1)}, f32[1,128]{1,0:T(1,128)}) custom-call(f32[512,128]{1,0:T(8,128)S(1)} %bitcast.16, bf16[2,32,128]{2,1,0:T(8,128)(2,1)S(1)} %copy-done.1, bf16[3,256,1024]{2,1,0:T(8,128)(2,1)S(1)} %bitcast.23), custom_call_target="tpu_custom_call" | custom-call | flops 67108864 | bytes 1048576 | tf_op jit(solution)/shard_map/finish/pallas_call | solution.py:344
  79.3 11.5 %all_to_all.26 = f32[16,2,128]{2,1,0:T(2,128)S(1)} all-to-all(f32[16,2,128]{2,1,0:T(2,128)S(1)} %bitcast.21), channel_id=1, replica_groups=mesh['y'=8,'z'=8,'core'=2,'seg'=4] {'z','core'}, dimensions={0} | all-to-all | bytes 32768 | tf_op jit(solution)/shard_map/all_to_all | solution.py:460
  90.8 12.0 %all_to_all.27 = f32[32,2,128]{2,1,0:T(2,128)S(1)} all-to-all(f32[32,2,128]{2,1,0:T(2,128)S(1)} %broadcast_in_dim.2), channel_id=1, replica_groups=mesh['y'=8,'z'=8,'core'=2,'seg'=4] {'y','seg'}, dimensions={0} | all-to-all | bytes 65536 | tf_op jit(solution)/shard_map/all_to_all | solution.py:460
  102.8 0.6 reduce_sum.19
  (3 shorter events, 0.1 us)
Async XLA Ops:
  0.6 21.3 %copy-start.2 = (bf16[1,32768]{1,0:T(2,128)(2,1)S(1)}, bf16[1,32768]{1,0:T(2,128)(2,1)}, u32[]{:S(2)}) copy-start(bf16[1,32768]{1,0:T(2,128)(2,1)} %param.11) | copy-start | bytes 196612
  3.5 30.6 %all-to-all-start = ((f32[128,2,128]{2,1,0:T(2,128)}), f32[128,2,128]{2,1,0:T(2,128)S(1)}, u32[]{:S(2)}, u32[]{:S(2)}) async-start(f32[128,2,128]{2,1,0:T(2,128)} %bitcast.25), calls=%async_computation | async-start | bytes 262144 | tf_op jit(solution)/shard_map/all_to_all | solution.py:460
  37.9 11.9 %all-to-all-start.1 = ((f32[4,32,1024]{2,1,0:T(8,128)}), f32[4,32,1024]{2,1,0:T(8,128)S(1)}, u32[]{:S(2)}, u32[]{:S(2)}) async-start(f32[4,32,1024]{2,1,0:T(8,128)} %splat.1), calls=%async_computation.1 | async-start | bytes 1048576 | tf_op jit(solution)/shard_map/all_to_all | solution.py:460
  47.1 30.2 %copy-start = (bf16[256,3,1024]{2,0,1:T(8,128)(2,1)S(1)}, bf16[256,3,1024]{2,0,1:T(8,128)(2,1)}, u32[]{:S(2)}) copy-start(bf16[256,3,1024]{2,0,1:T(8,128)(2,1)} %param.9) | copy-start | bytes 4718596
  47.1 30.2 %copy-start.1 = (bf16[2,32,128]{2,1,0:T(8,128)(2,1)S(1)}, bf16[2,32,128]{2,1,0:T(8,128)(2,1)}, u32[]{:S(2)}) copy-start(bf16[2,32,128]{2,1,0:T(8,128)(2,1)} %get-tuple-element.9.refs_1_) | copy-start | bytes 49156

commit v8 on v7

--- a/solution.py
+++ b/solution.py
@@ -124,23 +124,26 @@
         pick_ref[slot] = against_rows(same, pick).astype(jnp.bfloat16)
 
 
-def finish_kernel(voxels, atoms, back_ref, pick_ref, modes_ref, forces_ref, spread_ref, score_ref, block_ref):
+def finish_kernel(voxels, atoms, back_ref, pick_ref, modes_ref, forces_ref, spread_ref, score_ref, wide_ref, block_ref):
     n_tile = pick_ref.shape[2]
-    lane = lax.broadcasted_iota(jnp.int32, (1, LANES), 1)
-    totals = jnp.sum(back_ref[pl.ds(3, n_tile, stride=4), :], axis=0, keepdims=True)
+    wide_ref[...] = back_ref[...].astype(jnp.float32)
+    last = wide_ref[pl.ds(3, n_tile, stride=4), :]
+    place = lax.broadcasted_iota(jnp.int32, (n_tile, LANES), 1) // 3
+    ratio = jnp.sum(jnp.where(place == 3, last, 0.0), axis=1, keepdims=True)
+    totals = jnp.sum(last, axis=0, keepdims=True)
     srm, srr, smm = [
-        jnp.sum(jnp.where(lane == i, totals, 0.0), axis=1, keepdims=True) for i in range(3)
+        jnp.sum(jnp.where(place[0:1] == i, totals, 0.0), axis=1, keepdims=True) for i in range(3)
     ]
     root = jnp.sqrt(srr * smm)
     score = srm / root
     score_ref[...] = jnp.broadcast_to(score, score_ref.shape)
     map_scale = voxels / root
-    model_scale = voxels * (score / srr)
+    model_scale = map_scale * (ratio - srm / srr)
     cells = forces_ref.shape[1] // LANES
     modes = jnp.zeros((1, modes_ref.shape[1]), jnp.float32)
     for component in range(3):
-        pulled = back_ref[pl.ds(component, n_tile, stride=4), :]
-        pulled = pulled * map_scale - pltpu.roll(pulled, LANES // 2, 1) * model_scale
+        pulled = wide_ref[pl.ds(component, n_tile, stride=4), :]
+        pulled = pulled * map_scale + pltpu.roll(pulled, LANES // 2, 1) * model_scale
         parts = exact_parts(pulled)
         first, second = [
             sum([jnp.dot(pick_ref[slot], part, preferred_element_type=jnp.float32) for part in parts[::-1]])
@@ -315,28 +318,36 @@
     pull_rows(True, place_ref, row_ref, sum_ref, *scratch)
 
 
-def pull_kernel(got_ref, parts_ref, target_ref, map_ref, out_ref, place_ref, row_ref, sum_ref, *scratch):
+def pull_kernel(got_ref, parts_ref, target_ref, map_ref, out_ref, place_ref, row_ref, sum_ref, stage_ref, *scratch):
     unpack_rows(got_ref, place_ref)
     density = (parts_ref[0] + parts_ref[2]) + (parts_ref[1] + parts_ref[3])
     center_x, center_z = voxel_centers()
     store_rows(row_ref, (density, density * center_x, density * center_z))
+    wide = target_ref[...].astype(jnp.float32)
+    totals = [
+        jnp.sum(jnp.sum(product, axis=0, keepdims=True), axis=1, keepdims=True)
+        for product in (density * wide, density * density, wide * wide)
+    ]
+    ratio = jnp.where(totals[1] > 0.0, totals[0] / totals[1], 0.0)
+    pairs = place_ref.shape[1]
+    lane = lax.broadcasted_iota(jnp.int32, (8, LANES), 1)
+    last = jnp.zeros((8, LANES), jnp.float32)
+    for place, value in enumerate(totals + [ratio]):
+        for i, term in enumerate(exact_parts(jnp.broadcast_to(value, (8, LANES)))):
+            last = jnp.where(lane == 3 * place + i, term.astype(jnp.float32), last)
+    stage_ref[pl.ds(3, 2 * pairs, stride=4), :] = jnp.broadcast_to(last[0:1], (2 * pairs, LANES))
     pull_rows(False, place_ref, row_ref, sum_ref, *scratch)
-    wide = target_ref[...].astype(jnp.float32)
-    pairs = place_ref.shape[1]
     left = lax.broadcasted_iota(jnp.int32, (pairs, LANES), 1) < LANES // 2
     for component in range(3):
-        first, second = map_ref[component], sum_ref[component]
-        out_ref[pl.ds(component, pairs, stride=8), :] = jnp.where(
+        second = sum_ref[component]
+        first = map_ref[component] - ratio * second
+        stage_ref[pl.ds(component, pairs, stride=8), :] = jnp.where(
             left, first, pltpu.roll(second, LANES // 2, 1)
         )
-        out_ref[pl.ds(4 + component, pairs, stride=8), :] = jnp.where(
+        stage_ref[pl.ds(4 + component, pairs, stride=8), :] = jnp.where(
             left, pltpu.roll(first, LANES // 2, 1), second
         )
-    lane = lax.broadcasted_iota(jnp.int32, (2 * pairs, LANES), 1)
-    totals = jnp.zeros((2 * pairs, LANES), jnp.float32)
-    for place, product in enumerate((density * wide, density * density, wide * wide)):
-        totals = jnp.where(lane == place, jnp.sum(product), totals)
-    out_ref[pl.ds(3, 2 * pairs, stride=4), :] = totals
+    out_ref[...] = stage_ref[...].astype(jnp.bfloat16)
 
 
 def call(kernel, name, out_shape, scratch, flops, *operands, source=pltpu.VMEM, limit=32):
@@ -383,7 +394,7 @@
             jax.ShapeDtypeStruct((2 * copies, LANES), jnp.float32),
             jax.ShapeDtypeStruct((1, LANES), jnp.float32),
         ),
-        [((3, blocks, LANES), jnp.float32)],
+        [(back.shape, jnp.float32), ((3, blocks, LANES), jnp.float32)],
         2**26,
         back,
         picks,
@@ -438,11 +449,12 @@
     return call(
         pull_kernel,
         "pull",
-        jax.ShapeDtypeStruct((8 * groups, LANES), jnp.float32),
+        jax.ShapeDtypeStruct((8 * groups, LANES), jnp.bfloat16),
         [
             ((4, groups, LANES), jnp.float32),
             ((6 * EDGE, PLANE), jnp.bfloat16),
             ((3, groups, LANES), jnp.float32),
+            ((8 * groups, LANES), jnp.float32),
         ]
         + shape_scratch(groups),
         2**32,

time: 104 us -> 101 us (0.971)
  blocking collectives: 45 us -> 42.2 us
    all_to_all x3, blocking collectives: 45 us -> 42.2 us  [exchange(): return lax.all_to_all(values, axes, split_axis=0, concat_axis=0, tiled=True)]
where the time goes in v8:
time: 101 us
  blocking collectives  42.2 us (42%)
  starting transfers between devices  22.5 us (22%)
  Pallas kernels  19.6 us (19%)
  waiting for transfers between devices  14.3 us (14%)
    all_to_all x3, blocking collectives, exchange(): return lax.all_to_all(values, axes, split_axis=0, concat_axis=0, tiled=True)  42.2 us
    all_to_all x2, starting transfers between devices, exchange(): return lax.all_to_all(values, axes, split_axis=0, concat_axis=0, tiled=True)  22.5 us
    pallas_call x5, Pallas kernels, call(): pl.pallas_call(kernel, out_shape=out_shape, in_specs=[pl.BlockSpec(memory...  19.6 us
    all_to_all x2, waiting for transfers between devices, exchange(): return lax.all_to_all(values, axes, split_axis=0, concat_axis=0, tiled=True)  14.3 us
  transfers between devices with their start and end apart: 2, of which 2 were waited for; matrix products, arithmetic and copies ran while one was open for 1% of the time, Pallas kernels for 5%

profile of v8, /device:TPU:1, one launch (start us, length us, event | category | flops | bytes accessed | tf_op | source)
XLA Modules:
  0.0 100.5 jit_solution(4516539840672138631)
XLA Ops:
  0.6 0.0 copy-start.2
  0.6 2.8 %pack.1 = (f32[256,128]{1,0:T(8,128)}, bf16[2,32,128]{2,1,0:T(8,128)(2,1)}) custom-call(s32[4,32]{1,0:T(4,128)} %bitcast.29, s32[3,4,32]{2,1,0:T(4,128)} %bitcast.27, f32[1,256]{1,0:T(1,128)} %bitcast.30, f32[3,1024]{1,0:T(4,128)} %refs_3_.1, f32[8,128]{1,0:T(8,128)} %bitcast.28, bf16[3,256,1024]{2,1,0:T(8,128)(2,1)} %bitcast.22), custom_call_target="tpu_custom_call" | custom-call | flops 67108864 | bytes 1048576 | tf_op jit(solution)/shard_map/pack/pallas_call | solution.py:355
  3.5 18.4 %all-to-all-start = ((f32[128,2,128]{2,1,0:T(2,128)}), f32[128,2,128]{2,1,0:T(2,128)S(1)}, u32[]{:S(2)}, u32[]{:S(2)}) async-start(f32[128,2,128]{2,1,0:T(2,128)} %bitcast.25), calls=%async_computation | async-start | bytes 262144 | tf_op jit(solution)/shard_map/all_to_all | solution.py:472
  21.9 0.0 copy-done.2
  21.9 0.4 reduce
  22.3 0.2 reshape.41
  22.5 0.1 copy.19.target_ref
  22.6 11.5 %all-to-all-done = f32[128,2,128]{2,1,0:T(2,128)S(1)} async-done(((f32[128,2,128]{2,1,0:T(2,128)}), f32[128,2,128]{2,1,0:T(2,128)S(1)}, u32[]{:S(2)}, u32[]{:S(2)}) %all-to-all-start) | async-done | bytes 131104 | tf_op jit(solution)/shard_map/all_to_all | solution.py:472
  34.1 3.8 %splat.1 = f32[4,32,1024]{2,1,0:T(8,128)} custom-call(f32[256,128]{1,0:T(8,128)S(1)} %bitcast.16), custom_call_target="tpu_custom_call" | custom-call | flops 536870912 | bytes 1048576 | tf_op jit(solution)/shard_map/splat/pallas_call | solution.py:355
  37.9 4.0 %all-to-all-start.1 = ((f32[4,32,1024]{2,1,0:T(8,128)}), f32[4,32,1024]{2,1,0:T(8,128)S(1)}, u32[]{:S(2)}, u32[]{:S(2)}) async-start(f32[4,32,1024]{2,1,0:T(8,128)} %splat.1), calls=%async_computation.1 | async-start | bytes 1048576 | tf_op jit(solution)/shard_map/all_to_all | solution.py:472
  42.0 5.1 %pull_map.1.map_ref = f32[3,64,128]{2,1,0:T(8,128)S(1)} custom-call(f32[256,128]{1,0:T(8,128)S(1)} %bitcast.17, bf16[32,1024]{1,0:T(8,128)(2,1)S(1)} %copy.19.target_ref), custom_call_target="tpu_custom_call" | custom-call | flops 4294967296 | bytes 1048576 | tf_op jit(solution)/shard_map/pull_map/pallas_call | solution.py:355
  47.1 0.0 copy-start
  47.1 0.0 copy-start.1
  47.1 2.8 %all-to-all-done.1.parts_ref = f32[4,32,1024]{2,1,0:T(8,128)S(1)} async-done(((f32[4,32,1024]{2,1,0:T(8,128)}), f32[4,32,1024]{2,1,0:T(8,128)S(1)}, u32[]{:S(2)}, u32[]{:S(2)}) %all-to-all-start.1) | async-done | bytes 524320 | tf_op jit(solution)/shard_map/all_to_all | solution.py:472
  49.9 5.8 %pull.1 = bf16[512,128]{1,0:T(8,128)(2,1)S(1)} custom-call(f32[256,128]{1,0:T(8,128)S(1)} %bitcast.18, f32[4,32,1024]{2,1,0:T(8,128)S(1)} %all-to-all-done.1.parts_ref, bf16[32,1024]{1,0:T(8,128)(2,1)S(1)} %copy.19.target_ref, f32[3,64,128]{2,1,0:T(8,128)S(1)} %pull_map.1.map_ref), custom_call_target="tpu_custom_call" | custom-call | flops 4294967296 | bytes 1048576 | tf_op jit(solution)/shard_map/pull/pallas_call | solution.py:355
  55.7 19.7 %all_to_all.25 = bf16[128,4,128]{2,1,0:T(4,128)(2,1)S(1)} all-to-all(bf16[128,4,128]{2,1,0:T(4,128)(2,1)S(1)} %bitcast.20), channel_id=1, replica_groups=mesh['y'=8,'z'=8,'core'=2,'seg'=4] {'y','z','core'}, dimensions={0} | all-to-all | bytes 262144 | tf_op jit(solution)/shard_map/all_to_all | solution.py:472
  75.4 0.0 copy-done
  75.4 0.0 copy-done.1
  75.4 2.0 %finish.1 = (f32[3,1024]{1,0:T(4,128)}, f32[32,128]{1,0:T(8,128)S(1)}, f32[1,128]{1,0:T(1,128)}) custom-call(bf16[512,128]{1,0:T(8,128)(2,1)S(1)} %bitcast.19, bf16[2,32,128]{2,1,0:T(8,128)(2,1)S(1)} %copy-done.1, bf16[3,256,1024]{2,1,0:T(8,128)(2,1)S(1)} %bitcast.23), custom_call_target="tpu_custom_call" | custom-call | flops 67108864 | bytes 1048576 | tf_op jit(solution)/shard_map/finish/pallas_call | solution.py:355
  77.4 10.6 %all_to_all.26 = f32[16,2,128]{2,1,0:T(2,128)S(1)} all-to-all(f32[16,2,128]{2,1,0:T(2,128)S(1)} %bitcast.21), channel_id=1, replica_groups=mesh['y'=8,'z'=8,'core'=2,'seg'=4] {'z','core'}, dimensions={0} | all-to-all | bytes 32768 | tf_op jit(solution)/shard_map/all_to_all | solution.py:472
  88.0 11.9 %all_to_all.27 = f32[32,2,128]{2,1,0:T(2,128)S(1)} all-to-all(f32[32,2,128]{2,1,0:T(2,128)S(1)} %broadcast_in_dim.2), channel_id=1, replica_groups=mesh['y'=8,'z'=8,'core'=2,'seg'=4] {'y','seg'}, dimensions={0} | all-to-all | bytes 65536 | tf_op jit(solution)/shard_map/all_to_all | solution.py:472
  99.9 0.6 reduce_sum.19
  (3 shorter events, 0.1 us)
Async XLA Ops:
  0.6 21.3 %copy-start.2 = (bf16[1,32768]{1,0:T(2,128)(2,1)S(1)}, bf16[1,32768]{1,0:T(2,128)(2,1)}, u32[]{:S(2)}) copy-start(bf16[1,32768]{1,0:T(2,128)(2,1)} %param.11) | copy-start | bytes 196612
  3.5 30.6 %all-to-all-start = ((f32[128,2,128]{2,1,0:T(2,128)}), f32[128,2,128]{2,1,0:T(2,128)S(1)}, u32[]{:S(2)}, u32[]{:S(2)}) async-start(f32[128,2,128]{2,1,0:T(2,128)} %bitcast.25), calls=%async_computation | async-start | bytes 262144 | tf_op jit(solution)/shard_map/all_to_all | solution.py:472
  37.9 11.9 %all-to-all-start.1 = ((f32[4,32,1024]{2,1,0:T(8,128)}), f32[4,32,1024]{2,1,0:T(8,128)S(1)}, u32[]{:S(2)}, u32[]{:S(2)}) async-start(f32[4,32,1024]{2,1,0:T(8,128)} %splat.1), calls=%async_computation.1 | async-start | bytes 1048576 | tf_op jit(solution)/shard_map/all_to_all | solution.py:472
  47.1 28.3 %copy-start = (bf16[256,3,1024]{2,0,1:T(8,128)(2,1)S(1)}, bf16[256,3,1024]{2,0,1:T(8,128)(2,1)}, u32[]{:S(2)}) copy-start(bf16[256,3,1024]{2,0,1:T(8,128)(2,1)} %param.9) | copy-start | bytes 4718596
  47.1 28.3 %copy-start.1 = (bf16[2,32,128]{2,1,0:T(8,128)(2,1)S(1)}, bf16[2,32,128]{2,1,0:T(8,128)(2,1)}, u32[]{:S(2)}) copy-start(bf16[2,32,128]{2,1,0:T(8,128)(2,1)} %get-tuple-element.9.refs_1_) | copy-start | bytes 49156

commit v9 on v8

--- a/solution.py
+++ b/solution.py
@@ -18,7 +18,12 @@
 STEP = 4
 HIGHS = EDGE // STEP
 MIDDLE = EDGE / 2
-FAR = 40.0
+
+SPAN = 40.0
+PLACE_STEPS = 32000.0 / SPAN
+MASS_STEPS = 8000.0
+DENSITY_STEPS = 16000.0
+POWER_ROWS = 16
 
 inverse_var = 1.0 / 2.25
 rate = 0.5 * inverse_var / math.log(2.0)
@@ -43,6 +48,14 @@
     rest = values - high.astype(jnp.float32)
     middle = rest.astype(jnp.bfloat16)
     return high, middle, (rest - middle.astype(jnp.float32)).astype(jnp.bfloat16)
+
+
+def whole_steps(values):
+    return jnp.floor(values + 0.5).astype(jnp.int32).astype(jnp.int16)
+
+
+def from_steps(steps):
+    return steps.astype(jnp.int32).astype(jnp.float32)
 
 
 def against_rows(left, right):
@@ -65,8 +78,8 @@
 
 
 def pack_kernel(*refs):
-    sources, (send_ref, pick_ref), (cell_ref, block_ref) = refs[:6], refs[6:8], refs[8:10]
-    local, sems = refs[10:16], refs[16]
+    sources, (send_ref, pick_ref), (cell_ref, block_ref, wide_ref) = refs[:6], refs[6:8], refs[8:11]
+    local, sems = refs[11:17], refs[17]
     copies = [
         pltpu.make_async_copy(source, place, sems.at[i])
         for i, (source, place) in enumerate(zip(sources, local))
@@ -120,8 +133,13 @@
     for slot in range(2):
         pick = picks[slot].astype(jnp.bfloat16)
         high, middle, low = [jnp.dot(pick, part, preferred_element_type=jnp.float32) for part in parts]
-        send_ref[pl.ds(slot, n_tile, stride=2), :] = ((high + middle) + low) + shifts[slot]
+        rows = ((high + middle) + low) + shifts[slot]
+        steps = jnp.clip(rows - MIDDLE, -SPAN, SPAN) * PLACE_STEPS
+        wide_ref[pl.ds(slot, n_tile, stride=2), :] = jnp.where(
+            quarter_of(rows.shape) < 3, steps, rows * MASS_STEPS
+        )
         pick_ref[slot] = against_rows(same, pick).astype(jnp.bfloat16)
+    send_ref[...] = whole_steps(wide_ref[...])
 
 
 def finish_kernel(voxels, atoms, back_ref, pick_ref, modes_ref, forces_ref, spread_ref, score_ref, wide_ref, block_ref):
@@ -163,11 +181,13 @@
         )
 
 
-def unpack_rows(got_ref, place_ref):
+def unpack_rows(got_ref, wide_ref, place_ref):
+    wide_ref[...] = from_steps(got_ref[...])
     groups = got_ref.shape[0] // 4
-    rows = [got_ref[pl.ds(i, groups, stride=4), :] for i in range(4)]
-    for component in range(4):
-        place_ref[component] = regroup(rows, component)
+    rows = [wide_ref[pl.ds(i, groups, stride=4), :] for i in range(4)]
+    for component in range(3):
+        place_ref[component] = regroup(rows, component) * (1.0 / PLACE_STEPS) + MIDDLE
+    place_ref[3] = regroup(rows, 3) * (1.0 / MASS_STEPS)
 
 
 def chunk_row(place_ref, component, chunk, size):
@@ -194,10 +214,10 @@
     )
 
 
-def splat_kernel(got_ref, out_ref, place_ref, line_ref, even_ref, odd_ref, even_weight_ref, odd_weight_ref, sum_ref):
+def splat_kernel(got_ref, out_ref, wide_ref, place_ref, line_ref, even_ref, odd_ref, even_weight_ref, odd_weight_ref, sum_ref):
     size = even_ref.shape[1]
     planes, weights = (even_ref, odd_ref), (even_weight_ref, odd_weight_ref)
-    unpack_rows(got_ref, place_ref)
+    unpack_rows(got_ref, wide_ref, place_ref)
     sum_ref[...] = jnp.zeros_like(sum_ref)
     lows = [low + 0.5 - STEP / 2 for low in range(STEP)]
 
@@ -212,7 +232,7 @@
             block = line * jnp.concatenate([along_x, along_x], axis=0)
             planes[slot][pl.ds(z * HIGHS, 2 * HIGHS), :] = block.astype(jnp.bfloat16)
         along_y = masses * factors(place_y, centers_of(size))[0]
-        near = jnp.clip(place_x, -FAR, FAR)
+        near = jnp.clip(place_x, -SPAN, SPAN)
         for low in range(STEP):
             fine = jnp.exp2((2.0 * rate * lows[low]) * near)
             weights[slot][pl.ds(low * EDGE, EDGE), :] = (along_y * fine).astype(jnp.bfloat16)
@@ -227,11 +247,32 @@
     total = sum_ref[...].T
     high = (lax.broadcasted_iota(jnp.int32, (EDGE, EDGE * HIGHS), 1) % HIGHS).astype(jnp.float32)
     coarse = STEP * high + (STEP / 2 - MIDDLE)
+    blocks = []
     for low in range(STEP):
         scale = jnp.exp2(-rate * (2.0 * lows[low] * coarse + lows[low] ** 2))
         block = total[low * EDGE : (low + 1) * EDGE] * scale
-        for copy in range(out_ref.shape[0]):
-            out_ref[copy, :, pl.ds(low * EDGE * HIGHS, EDGE * HIGHS)] = block
+        blocks += [block[:, i : i + LANES] for i in range(0, block.shape[1], LANES)]
+    largest = blocks[0]
+    for block in blocks[1:]:
+        largest = jnp.maximum(largest, block)
+    largest = jnp.max(jnp.max(largest, axis=0, keepdims=True), axis=1, keepdims=True)
+    power = jnp.floor(jnp.log(jnp.clip(largest, 1e-30, 1e30)) * (1.0 / math.log(2.0)))
+    steps = DENSITY_STEPS * jnp.exp2(-power)
+    rows = [whole_steps(block * steps) for block in blocks]
+    rows.append(whole_steps(jnp.broadcast_to(power, (POWER_ROWS, LANES))))
+    for copy in range(out_ref.shape[0]):
+        place = 0
+        for block in rows:
+            out_ref[copy, pl.ds(place, block.shape[0]), :] = block
+            place += block.shape[0]
+
+
+def density_of(parts_ref, part):
+    count = parts_ref.shape[1] - POWER_ROWS
+    power = from_steps(parts_ref[part, pl.ds(count, POWER_ROWS), :])[0:1]
+    step = jnp.exp2(power) * (1.0 / DENSITY_STEPS)
+    blocks = [from_steps(parts_ref[part, pl.ds(i, EDGE), :]) * step for i in range(0, count, EDGE)]
+    return jnp.concatenate(blocks, axis=1)
 
 
 def build_shape(place_ref, line_ref, plane_ref, weight_ref, chunk, size):
@@ -310,17 +351,18 @@
     pipeline(place_ref.shape[1] * LANES // size, build, use)
 
 
-def map_kernel(got_ref, target_ref, sum_ref, place_ref, row_ref, *scratch):
-    unpack_rows(got_ref, place_ref)
+def map_kernel(got_ref, target_ref, sum_ref, wide_ref, place_ref, row_ref, *scratch):
+    unpack_rows(got_ref, wide_ref, place_ref)
     wide = target_ref[...].astype(jnp.float32)
     center_x, center_z = voxel_centers()
     store_rows(row_ref, (target_ref[...], wide * center_x, wide * center_z))
     pull_rows(True, place_ref, row_ref, sum_ref, *scratch)
 
 
-def pull_kernel(got_ref, parts_ref, target_ref, map_ref, out_ref, place_ref, row_ref, sum_ref, stage_ref, *scratch):
-    unpack_rows(got_ref, place_ref)
-    density = (parts_ref[0] + parts_ref[2]) + (parts_ref[1] + parts_ref[3])
+def pull_kernel(got_ref, parts_ref, target_ref, map_ref, out_ref, wide_ref, place_ref, row_ref, sum_ref, stage_ref, *scratch):
+    unpack_rows(got_ref, wide_ref, place_ref)
+    parts = [density_of(parts_ref, i) for i in range(4)]
+    density = (parts[0] + parts[2]) + (parts[1] + parts[3])
     center_x, center_z = voxel_centers()
     store_rows(row_ref, (density, density * center_x, density * center_z))
     wide = target_ref[...].astype(jnp.float32)
@@ -371,10 +413,14 @@
         pack_kernel,
         "pack",
         (
-            jax.ShapeDtypeStruct((2 * n_tile, LANES), jnp.float32),
+            jax.ShapeDtypeStruct((2 * n_tile, LANES), jnp.int16),
             jax.ShapeDtypeStruct((2, blocks, n_tile), jnp.bfloat16),
         ),
-        [((4, weights.shape[0], LANES), jnp.float32), ((blocks, LANES), jnp.float32)]
+        [
+            ((4, weights.shape[0], LANES), jnp.float32),
+            ((blocks, LANES), jnp.float32),
+            ((2 * n_tile, LANES), jnp.float32),
+        ]
         + [(operand.shape, operand.dtype) for operand in operands]
         + [pltpu.SemaphoreType.DMA((len(operands),))],
         2**26,
@@ -410,9 +456,9 @@
     return call(
         splat_kernel,
         "splat",
-        jax.ShapeDtypeStruct((copies, EDGE, PLANE), jnp.float32),
+        jax.ShapeDtypeStruct((copies, EDGE * PLANE // LANES + POWER_ROWS, LANES), jnp.int16),
         [
-            ((4, groups, LANES), jnp.float32),
+            ((4 * groups, LANES), jnp.float32), ((4, groups, LANES), jnp.float32),
             ((2, EDGE, size), jnp.float32),
             plane,
             plane,
@@ -437,7 +483,7 @@
         map_kernel,
         "pull_map",
         jax.ShapeDtypeStruct((3, groups, LANES), jnp.float32),
-        [((4, groups, LANES), jnp.float32), ((5 * EDGE, PLANE), jnp.bfloat16)] + shape_scratch(groups),
+        [((4 * groups, LANES), jnp.float32), ((4, groups, LANES), jnp.float32), ((5 * EDGE, PLANE), jnp.bfloat16)] + shape_scratch(groups),
         2**32,
         got,
         target,
@@ -451,7 +497,7 @@
         "pull",
         jax.ShapeDtypeStruct((8 * groups, LANES), jnp.bfloat16),
         [
-            ((4, groups, LANES), jnp.float32),
+            ((4 * groups, LANES), jnp.float32), ((4, groups, LANES), jnp.float32),
             ((6 * EDGE, PLANE), jnp.bfloat16),
             ((3, groups, LANES), jnp.float32),
             ((8 * groups, LANES), jnp.float32),

time: 101 us -> 98.4 us (0.974)
  waiting for transfers between devices: 14.3 us -> 11.4 us
    all_to_all x2, waiting for transfers between devices: 14.3 us -> 11.4 us  [exchange(): return lax.all_to_all(values, axes, split_axis=0, concat_axis=0, tiled=True)]
where the time goes in v9:
time: 98.4 us; the launch traced here: 98 us
  blocking collectives  42.3 us (43%)
  starting transfers between devices  22.4 us (23%)
  Pallas kernels  19.9 us (20%)
  waiting for transfers between devices  11.4 us (12%)
  other arithmetic  1 us (1%)
    all_to_all x3, blocking collectives, exchange(): return lax.all_to_all(values, axes, split_axis=0, concat_axis=0, tiled=True)  42.3 us
    all_to_all x2, starting transfers between devices, exchange(): return lax.all_to_all(values, axes, split_axis=0, concat_axis=0, tiled=True)  22.4 us
    pallas_call x5, Pallas kernels, call(): pl.pallas_call(kernel, out_shape=out_shape, in_specs=[pl.BlockSpec(memory...  19.9 us
    all_to_all x2, waiting for transfers between devices, exchange(): return lax.all_to_all(values, axes, split_axis=0, concat_axis=0, tiled=True)  11.4 us
  transfers between devices with their start and end apart: 2, of which 2 were waited for; matrix products, arithmetic and copies ran while one was open for 1% of the time, Pallas kernels for 5%

profile of v9, /device:TPU:1, one launch (start us, length us, event | category | flops | bytes accessed | tf_op | source)
XLA Modules:
  0.0 98.0 jit_solution(6762084165671784476)
XLA Ops:
  0.6 0.0 copy-start.2
  0.6 2.8 %pack.1 = (s16[256,128]{1,0:T(8,128)(2,1)}, bf16[2,32,128]{2,1,0:T(8,128)(2,1)}) custom-call(s32[4,32]{1,0:T(4,128)} %bitcast.29, s32[3,4,32]{2,1,0:T(4,128)} %bitcast.27, f32[1,256]{1,0:T(1,128)} %bitcast.30, f32[3,1024]{1,0:T(4,128)} %refs_3_.1, f32[8,128]{1,0:T(8,128)} %bitcast.28, bf16[3,256,1024]{2,1,0:T(8,128)(2,1)} %bitcast.22), custom_call_target="tpu_custom_call" | custom-call | flops 67108864 | bytes 1048576 | tf_op jit(solution)/shard_map/pack/pallas_call | solution.py:397
  3.5 18.4 %all-to-all-start = ((s16[128,2,128]{2,1,0:T(2,128)(2,1)}), s16[128,2,128]{2,1,0:T(2,128)(2,1)S(1)}, u32[]{:S(2)}, u32[]{:S(2)}) async-start(s16[128,2,128]{2,1,0:T(2,128)(2,1)} %bitcast.25), calls=%async_computation | async-start | bytes 131072 | tf_op jit(solution)/shard_map/all_to_all | solution.py:518
  21.9 0.0 copy-done.2
  21.9 0.4 reduce
  22.3 0.2 reshape.41
  22.5 0.1 copy.19.target_ref
  22.6 10.8 %all-to-all-done = s16[128,2,128]{2,1,0:T(2,128)(2,1)S(1)} async-done(((s16[128,2,128]{2,1,0:T(2,128)(2,1)}), s16[128,2,128]{2,1,0:T(2,128)(2,1)S(1)}, u32[]{:S(2)}, u32[]{:S(2)}) %all-to-all-start) | async-done | bytes 65568 | tf_op jit(solution)/shard_map/all_to_all | solution.py:518
  33.5 3.9 %splat.1 = s16[4,272,128]{2,1,0:T(8,128)(2,1)} custom-call(s16[256,128]{1,0:T(8,128)(2,1)S(1)} %bitcast.18), custom_call_target="tpu_custom_call" | custom-call | flops 536870912 | bytes 1048576 | tf_op jit(solution)/shard_map/splat/pallas_call | solution.py:397
  37.4 4.0 %all-to-all-start.1 = ((s16[4,272,128]{2,1,0:T(8,128)(2,1)}), s16[4,272,128]{2,1,0:T(8,128)(2,1)S(1)}, u32[]{:S(2)}, u32[]{:S(2)}) async-start(s16[4,272,128]{2,1,0:T(8,128)(2,1)} %splat.1), calls=%async_computation.1 | async-start | bytes 557056 | tf_op jit(solution)/shard_map/all_to_all | solution.py:518
  41.4 5.2 %pull_map.1.map_ref = f32[3,64,128]{2,1,0:T(8,128)S(1)} custom-call(s16[256,128]{1,0:T(8,128)(2,1)S(1)} %bitcast.19, bf16[32,1024]{1,0:T(8,128)(2,1)S(1)} %copy.19.target_ref), custom_call_target="tpu_custom_call" | custom-call | flops 4294967296 | bytes 1048576 | tf_op jit(solution)/shard_map/pull_map/pallas_call | solution.py:397
  46.6 0.0 copy-start
  46.6 0.0 copy-start.1
  46.6 0.6 all-to-all-done.1.parts_ref
  47.2 5.9 %pull.1 = bf16[512,128]{1,0:T(8,128)(2,1)S(1)} custom-call(s16[256,128]{1,0:T(8,128)(2,1)S(1)} %bitcast.20, s16[4,272,128]{2,1,0:T(8,128)(2,1)S(1)} %all-to-all-done.1.parts_ref, bf16[32,1024]{1,0:T(8,128)(2,1)S(1)} %copy.19.target_ref, f32[3,64,128]{2,1,0:T(8,128)S(1)} %pull_map.1.map_ref), custom_call_target="tpu_custom_call" | custom-call | flops 4294967296 | bytes 1048576 | tf_op jit(solution)/shard_map/pull/pallas_call | solution.py:397
  53.1 19.1 %all_to_all.25 = bf16[128,4,128]{2,1,0:T(4,128)(2,1)S(1)} all-to-all(bf16[128,4,128]{2,1,0:T(4,128)(2,1)S(1)} %bitcast.17), channel_id=1, replica_groups=mesh['y'=8,'z'=8,'core'=2,'seg'=4] {'y','z','core'}, dimensions={0} | all-to-all | bytes 262144 | tf_op jit(solution)/shard_map/all_to_all | solution.py:518
  72.3 0.0 copy-done
  72.3 0.0 copy-done.1
  72.3 2.0 %finish.1 = (f32[3,1024]{1,0:T(4,128)}, f32[32,128]{1,0:T(8,128)S(1)}, f32[1,128]{1,0:T(1,128)}) custom-call(bf16[512,128]{1,0:T(8,128)(2,1)S(1)} %bitcast.16, bf16[2,32,128]{2,1,0:T(8,128)(2,1)S(1)} %copy-done.1, bf16[3,256,1024]{2,1,0:T(8,128)(2,1)S(1)} %bitcast.23), custom_call_target="tpu_custom_call" | custom-call | flops 67108864 | bytes 1048576 | tf_op jit(solution)/shard_map/finish/pallas_call | solution.py:397
  74.3 10.6 %all_to_all.26 = f32[16,2,128]{2,1,0:T(2,128)S(1)} all-to-all(f32[16,2,128]{2,1,0:T(2,128)S(1)} %bitcast.21), channel_id=1, replica_groups=mesh['y'=8,'z'=8,'core'=2,'seg'=4] {'z','core'}, dimensions={0} | all-to-all | bytes 32768 | tf_op jit(solution)/shard_map/all_to_all | solution.py:518
  84.9 12.6 %all_to_all.27 = f32[32,2,128]{2,1,0:T(2,128)S(1)} all-to-all(f32[32,2,128]{2,1,0:T(2,128)S(1)} %broadcast_in_dim.2), channel_id=1, replica_groups=mesh['y'=8,'z'=8,'core'=2,'seg'=4] {'y','seg'}, dimensions={0} | all-to-all | bytes 65536 | tf_op jit(solution)/shard_map/all_to_all | solution.py:518
  97.4 0.6 reduce_sum.19
  (3 shorter events, 0.1 us)
Async XLA Ops:
  0.6 21.3 %copy-start.2 = (bf16[1,32768]{1,0:T(2,128)(2,1)S(1)}, bf16[1,32768]{1,0:T(2,128)(2,1)}, u32[]{:S(2)}) copy-start(bf16[1,32768]{1,0:T(2,128)(2,1)} %param.11) | copy-start | bytes 196612
  3.5 30.0 %all-to-all-start = ((s16[128,2,128]{2,1,0:T(2,128)(2,1)}), s16[128,2,128]{2,1,0:T(2,128)(2,1)S(1)}, u32[]{:S(2)}, u32[]{:S(2)}) async-start(s16[128,2,128]{2,1,0:T(2,128)(2,1)} %bitcast.25), calls=%async_computation | async-start | bytes 131072 | tf_op jit(solution)/shard_map/all_to_all | solution.py:518
  37.4 9.8 %all-to-all-start.1 = ((s16[4,272,128]{2,1,0:T(8,128)(2,1)}), s16[4,272,128]{2,1,0:T(8,128)(2,1)S(1)}, u32[]{:S(2)}, u32[]{:S(2)}) async-start(s16[4,272,128]{2,1,0:T(8,128)(2,1)} %splat.1), calls=%async_computation.1 | async-start | bytes 557056 | tf_op jit(solution)/shard_map/all_to_all | solution.py:518
  46.6 25.7 %copy-start = (bf16[256,3,1024]{2,0,1:T(8,128)(2,1)S(1)}, bf16[256,3,1024]{2,0,1:T(8,128)(2,1)}, u32[]{:S(2)}) copy-start(bf16[256,3,1024]{2,0,1:T(8,128)(2,1)} %param.9) | copy-start | bytes 4718596
  46.6 25.7 %copy-start.1 = (bf16[2,32,128]{2,1,0:T(8,128)(2,1)S(1)}, bf16[2,32,128]{2,1,0:T(8,128)(2,1)}, u32[]{:S(2)}) copy-start(bf16[2,32,128]{2,1,0:T(8,128)(2,1)} %get-tuple-element.9.refs_1_) | copy-start | bytes 49156

commit v10 on v9

--- a/solution.py
+++ b/solution.py
@@ -214,18 +214,28 @@
     )
 
 
+LOWS = [low + 0.5 - STEP / 2 for low in range(STEP)]
+
+
+def coarse_of(high):
+    return STEP * high.astype(jnp.float32) + (STEP / 2 - MIDDLE)
+
+
+def own_factor(low, width):
+    coarse = coarse_of(lax.broadcasted_iota(jnp.int32, (EDGE, width), 1) % HIGHS)
+    return jnp.exp2(-rate * (2.0 * LOWS[low] * coarse + LOWS[low] ** 2))
+
+
 def splat_kernel(got_ref, out_ref, wide_ref, place_ref, line_ref, even_ref, odd_ref, even_weight_ref, odd_weight_ref, sum_ref):
     size = even_ref.shape[1]
     planes, weights = (even_ref, odd_ref), (even_weight_ref, odd_weight_ref)
     unpack_rows(got_ref, wide_ref, place_ref)
     sum_ref[...] = jnp.zeros_like(sum_ref)
-    lows = [low + 0.5 - STEP / 2 for low in range(STEP)]
 
     def build(slot, chunk):
         place_x, place_y, place_z, masses = [chunk_row(place_ref, i, chunk, size) for i in range(4)]
         place_x = place_x - MIDDLE
-        coarse = STEP * row_number(HIGHS, size).astype(jnp.float32) + (STEP / 2 - MIDDLE)
-        along_x = factors(place_x, coarse)[0]
+        along_x = factors(place_x, coarse_of(row_number(HIGHS, size)))[0]
         line_ref[slot] = factors(place_z, centers_of(size))[0]
         for z in range(0, EDGE, 2):
             line = pair_of_lines(line_ref.at[slot], z, size)
@@ -234,7 +244,7 @@
         along_y = masses * factors(place_y, centers_of(size))[0]
         near = jnp.clip(place_x, -SPAN, SPAN)
         for low in range(STEP):
-            fine = jnp.exp2((2.0 * rate * lows[low]) * near)
+            fine = jnp.exp2((2.0 * rate * LOWS[low]) * near)
             weights[slot][pl.ds(low * EDGE, EDGE), :] = (along_y * fine).astype(jnp.bfloat16)
 
     def use(slot, chunk):
@@ -245,12 +255,9 @@
 
     pipeline(place_ref.shape[1] * LANES // size, build, use)
     total = sum_ref[...].T
-    high = (lax.broadcasted_iota(jnp.int32, (EDGE, EDGE * HIGHS), 1) % HIGHS).astype(jnp.float32)
-    coarse = STEP * high + (STEP / 2 - MIDDLE)
     blocks = []
     for low in range(STEP):
-        scale = jnp.exp2(-rate * (2.0 * lows[low] * coarse + lows[low] ** 2))
-        block = total[low * EDGE : (low + 1) * EDGE] * scale
+        block = total[low * EDGE : (low + 1) * EDGE] * own_factor(low, EDGE * HIGHS)
         blocks += [block[:, i : i + LANES] for i in range(0, block.shape[1], LANES)]
     largest = blocks[0]
     for block in blocks[1:]:
@@ -275,102 +282,82 @@
     return jnp.concatenate(blocks, axis=1)
 
 
-def build_shape(place_ref, line_ref, plane_ref, weight_ref, chunk, size):
-    place_x, place_y, place_z, masses = [chunk_row(place_ref, i, chunk, size) for i in range(4)]
-    row = row_number(EDGE, size)
-    centers = (STEP * (row % HIGHS) + row // HIGHS).astype(jnp.float32) + 0.5
-    along_x = factors(place_x, centers)[0]
-    doubled = []
+def field_rows(row_ref, field):
+    width = EDGE * HIGHS
     for low in range(STEP):
-        block = along_x[low * HIGHS : (low + 1) * HIGHS]
-        doubled.append(jnp.concatenate([block, block], axis=0).astype(jnp.bfloat16))
-    line_ref[...] = factors(place_z, centers_of(size))[0].astype(jnp.bfloat16).astype(jnp.float32)
-    for z in range(0, EDGE, 2):
-        line = pair_of_lines(line_ref, z, size).astype(jnp.bfloat16)
+        rows = field[:, low * width : (low + 1) * width] * own_factor(low, width)
+        row_ref[low * EDGE : (low + 1) * EDGE] = rows.astype(jnp.bfloat16)
+
+
+def pull_rows(place_ref, row_ref, sum_ref, line_ref, even_ref, odd_ref, weight_ref, fine_ref):
+    planes = (even_ref, odd_ref)
+    size = even_ref.shape[2]
+    width = min(WIDTH, size)
+
+    def build(slot, chunk):
+        place_x, place_y, place_z, masses = [chunk_row(place_ref, i, chunk, size) for i in range(4)]
+        place_x = place_x - MIDDLE
+        distance = coarse_of(row_number(HIGHS, size)) - place_x
+        along_x = jnp.exp2(-rate * (distance * distance))
+        near = jnp.clip(place_x, -SPAN, SPAN)
         for low in range(STEP):
-            plane_ref[pl.ds(low * EDGE * HIGHS + z * HIGHS, 2 * HIGHS), :] = line * doubled[low]
-    profile_y, slope_y = factors(place_y, centers_of(size))
-    weight_ref[0] = (masses * profile_y).astype(jnp.bfloat16).astype(jnp.float32)
-    weight_ref[1] = (masses * slope_y).astype(jnp.bfloat16).astype(jnp.float32)
-
-
-def voxel_centers():
-    voxel = lax.broadcasted_iota(jnp.int32, (EDGE, PLANE), 1)
-    low, z, high = voxel // (EDGE * HIGHS), voxel // HIGHS % EDGE, voxel % HIGHS
-    return [part.astype(jnp.float32) + (0.5 - MIDDLE) for part in (STEP * high + low, z)]
-
-
-def store_rows(row_ref, arrays):
-    place = 0
-    for values in arrays:
-        terms = (values,) if values.dtype == jnp.bfloat16 else exact_parts(values)[:2]
-        for term in terms:
-            row_ref[place : place + EDGE] = term
-            place += EDGE
-
-
-def take_forces(sum_ref, chunk, sums, weights, places):
-    plain, by_x, by_z = sums
-    along_y, slope_y = weights
-    whole, force_y, moment_x, moment_z = [
-        jnp.sum(values * weight, axis=0, keepdims=True)
-        for values, weight in ((plain, along_y), (plain, slope_y), (by_x, along_y), (by_z, along_y))
-    ]
-    force_x = inverse_var * (moment_x - (places[0] - MIDDLE) * whole)
-    force_z = inverse_var * (moment_z - (places[1] - MIDDLE) * whole)
-    rows = whole.shape[1] // LANES
-    for component, force in enumerate((force_x, force_y, force_z)):
-        for i in range(rows):
-            sum_ref[component, pl.ds(chunk * rows + i, 1), :] = force[:, i * LANES : (i + 1) * LANES]
-
-
-def pull_rows(single, place_ref, row_ref, sum_ref, line_ref, even_ref, odd_ref, weight_ref):
-    planes = (even_ref, odd_ref)
-    size = even_ref.shape[1]
-    width = min(WIDTH, size)
-
-    def build(slot, chunk):
-        build_shape(place_ref, line_ref.at[slot], planes[slot], weight_ref.at[slot], chunk, size)
+            fine_ref[slot, pl.ds(low, 1), :] = jnp.exp2((2.0 * rate * LOWS[low]) * near)
+        for i, values in enumerate(factors(place_z, centers_of(size))):
+            line_ref[slot, i] = values.astype(jnp.bfloat16).astype(jnp.float32)
+        for i, values in enumerate(factors(place_y, centers_of(size))):
+            weight_ref[slot, i] = (masses * values).astype(jnp.bfloat16).astype(jnp.float32)
+        plain = jnp.concatenate([along_x, along_x], axis=0)
+        sloped = plain * jnp.concatenate([distance, distance], axis=0)
+        for z in range(0, EDGE, 2):
+            line = pair_of_lines(line_ref.at[slot, 0], z, size)
+            slope_line = pair_of_lines(line_ref.at[slot, 1], z, size)
+            place = pl.ds(z * HIGHS, 2 * HIGHS)
+            planes[slot][0, place, :] = (line * plain).astype(jnp.bfloat16)
+            planes[slot][1, place, :] = (line * sloped).astype(jnp.bfloat16)
+            planes[slot][2, place, :] = (slope_line * plain).astype(jnp.bfloat16)
 
     def use(slot, chunk):
         for part in range(size // width):
             atoms = pl.ds(part * width, width)
-            small = chunk * (size // width) + part
-            pulled = jnp.dot(row_ref[...], planes[slot][:, atoms], preferred_element_type=jnp.float32)
-            block = [pulled[i : i + EDGE] for i in range(0, pulled.shape[0], EDGE)]
-            plain = block[0] if single else block[0] + block[1]
-            block = block[1:] if single else block[2:]
-            take_forces(
-                sum_ref,
-                small,
-                (plain, block[0] + block[1], block[2] + block[3]),
-                [weight_ref[slot, i, :, atoms] for i in range(2)],
-                [chunk_row(place_ref, i, small, width) for i in (0, 2)],
-            )
+            pulled = [
+                jnp.dot(row_ref[...], planes[slot][i, :, atoms], preferred_element_type=jnp.float32)
+                for i in range(3)
+            ]
+            sums = [jnp.zeros((EDGE, width), jnp.float32) for _ in range(3)]
+            for low in range(STEP):
+                fine = fine_ref[slot, pl.ds(low, 1), atoms]
+                plain, by_x, by_z = [values[low * EDGE : (low + 1) * EDGE] for values in pulled]
+                sums[0] = sums[0] + (by_x + LOWS[low] * plain) * fine
+                sums[1] = sums[1] + plain * fine
+                sums[2] = sums[2] + by_z * fine
+            along_y, slope_y = [weight_ref[slot, i, :, atoms] for i in range(2)]
+            rows = width // LANES
+            for component, weight in enumerate((inverse_var * along_y, slope_y, along_y)):
+                force = jnp.sum(sums[component] * weight, axis=0, keepdims=True)
+                for i in range(rows):
+                    row = (chunk * (size // width) + part) * rows + i
+                    sum_ref[component, pl.ds(row, 1), :] = force[:, i * LANES : (i + 1) * LANES]
 
     pipeline(place_ref.shape[1] * LANES // size, build, use)
 
 
 def map_kernel(got_ref, target_ref, sum_ref, wide_ref, place_ref, row_ref, *scratch):
     unpack_rows(got_ref, wide_ref, place_ref)
-    wide = target_ref[...].astype(jnp.float32)
-    center_x, center_z = voxel_centers()
-    store_rows(row_ref, (target_ref[...], wide * center_x, wide * center_z))
-    pull_rows(True, place_ref, row_ref, sum_ref, *scratch)
+    field_rows(row_ref, target_ref[...].astype(jnp.float32))
+    pull_rows(place_ref, row_ref, sum_ref, *scratch)
 
 
 def pull_kernel(got_ref, parts_ref, target_ref, map_ref, out_ref, wide_ref, place_ref, row_ref, sum_ref, stage_ref, *scratch):
     unpack_rows(got_ref, wide_ref, place_ref)
     parts = [density_of(parts_ref, i) for i in range(4)]
     density = (parts[0] + parts[2]) + (parts[1] + parts[3])
-    center_x, center_z = voxel_centers()
-    store_rows(row_ref, (density, density * center_x, density * center_z))
     wide = target_ref[...].astype(jnp.float32)
     totals = [
         jnp.sum(jnp.sum(product, axis=0, keepdims=True), axis=1, keepdims=True)
         for product in (density * wide, density * density, wide * wide)
     ]
-    ratio = jnp.where(totals[1] > 0.0, totals[0] / totals[1], 0.0)
+    ratio = jnp.where(totals[0] > 0.0, totals[0] / jnp.maximum(totals[1], 1e-30), 1.0)
+    field_rows(row_ref, wide - ratio * density)
     pairs = place_ref.shape[1]
     lane = lax.broadcasted_iota(jnp.int32, (8, LANES), 1)
     last = jnp.zeros((8, LANES), jnp.float32)
@@ -378,11 +365,11 @@
         for i, term in enumerate(exact_parts(jnp.broadcast_to(value, (8, LANES)))):
             last = jnp.where(lane == 3 * place + i, term.astype(jnp.float32), last)
     stage_ref[pl.ds(3, 2 * pairs, stride=4), :] = jnp.broadcast_to(last[0:1], (2 * pairs, LANES))
-    pull_rows(False, place_ref, row_ref, sum_ref, *scratch)
+    pull_rows(place_ref, row_ref, sum_ref, *scratch)
     left = lax.broadcasted_iota(jnp.int32, (pairs, LANES), 1) < LANES // 2
     for component in range(3):
-        second = sum_ref[component]
-        first = map_ref[component] - ratio * second
+        first = sum_ref[component]
+        second = (map_ref[component] - first) / ratio
         stage_ref[pl.ds(component, pairs, stride=8), :] = jnp.where(
             left, first, pltpu.roll(second, LANES // 2, 1)
         )
@@ -471,10 +458,11 @@
     )
 
 
-def shape_scratch(groups):
+def pull_scratch(groups):
     size = min(CHUNK, groups * LANES // 2)
-    plane = ((PLANE, size), jnp.bfloat16)
-    return [((2, EDGE, size), jnp.float32), plane, plane, ((2, 2, EDGE, size), jnp.float32)]
+    plane = ((3, EDGE * HIGHS, size), jnp.bfloat16)
+    lines = ((2, 2, EDGE, size), jnp.float32)
+    return [lines, plane, plane, lines, ((2, STEP, size), jnp.float32)]
 
 
 def pull_map(got, target):
@@ -483,7 +471,7 @@
         map_kernel,
         "pull_map",
         jax.ShapeDtypeStruct((3, groups, LANES), jnp.float32),
-        [((4 * groups, LANES), jnp.float32), ((4, groups, LANES), jnp.float32), ((5 * EDGE, PLANE), jnp.bfloat16)] + shape_scratch(groups),
+        [((4 * groups, LANES), jnp.float32), ((4, groups, LANES), jnp.float32), ((STEP * EDGE, EDGE * HIGHS), jnp.bfloat16)] + pull_scratch(groups),
         2**32,
         got,
         target,
@@ -498,11 +486,11 @@
         jax.ShapeDtypeStruct((8 * groups, LANES), jnp.bfloat16),
         [
             ((4 * groups, LANES), jnp.float32), ((4, groups, LANES), jnp.float32),
-            ((6 * EDGE, PLANE), jnp.bfloat16),
+            ((STEP * EDGE, EDGE * HIGHS), jnp.bfloat16),
             ((3, groups, LANES), jnp.float32),
             ((8 * groups, LANES), jnp.float32),
         ]
-        + shape_scratch(groups),
+        + pull_scratch(groups),
         2**32,
         got,
         parts,

time: 98.4 us -> 98.2 us (level)
  no operation moved by 1% of the time
where the time goes in v10:
time: 98.2 us; the launch traced here: 97.9 us
  blocking collectives  42.4 us (43%)
  starting transfers between devices  22.4 us (23%)
  Pallas kernels  19.7 us (20%)
  waiting for transfers between devices  11.2 us (11%)
  other arithmetic  1 us (1%)
    all_to_all x3, blocking collectives, exchange(): return lax.all_to_all(values, axes, split_axis=0, concat_axis=0, tiled=True)  42.4 us
    all_to_all x2, starting transfers between devices, exchange(): return lax.all_to_all(values, axes, split_axis=0, concat_axis=0, tiled=True)  22.4 us
    pallas_call x5, Pallas kernels, call(): pl.pallas_call(kernel, out_shape=out_shape, in_specs=[pl.BlockSpec(memory...  19.7 us
    all_to_all x2, waiting for transfers between devices, exchange(): return lax.all_to_all(values, axes, split_axis=0, concat_axis=0, tiled=True)  11.2 us
  transfers between devices with their start and end apart: 2, of which 2 were waited for; matrix products, arithmetic and copies ran while one was open for 1% of the time, Pallas kernels for 5%

profile of v10, /device:TPU:1, one launch (start us, length us, event | category | flops | bytes accessed | tf_op | source)
XLA Modules:
  0.0 97.9 jit_solution(1112870419037884997)
XLA Ops:
  0.6 0.0 copy-start.2
  0.6 2.8 %pack.1 = (s16[256,128]{1,0:T(8,128)(2,1)}, bf16[2,32,128]{2,1,0:T(8,128)(2,1)}) custom-call(s32[4,32]{1,0:T(4,128)} %bitcast.29, s32[3,4,32]{2,1,0:T(4,128)} %bitcast.27, f32[1,256]{1,0:T(1,128)} %bitcast.30, f32[3,1024]{1,0:T(4,128)} %refs_3_.1, f32[8,128]{1,0:T(8,128)} %bitcast.28, bf16[3,256,1024]{2,1,0:T(8,128)(2,1)} %bitcast.22), custom_call_target="tpu_custom_call" | custom-call | flops 67108864 | bytes 1048576 | tf_op jit(solution)/shard_map/pack/pallas_call | solution.py:384
  3.5 18.4 %all-to-all-start = ((s16[128,2,128]{2,1,0:T(2,128)(2,1)}), s16[128,2,128]{2,1,0:T(2,128)(2,1)S(1)}, u32[]{:S(2)}, u32[]{:S(2)}) async-start(s16[128,2,128]{2,1,0:T(2,128)(2,1)} %bitcast.25), calls=%async_computation | async-start | bytes 131072 | tf_op jit(solution)/shard_map/all_to_all | solution.py:506
  21.9 0.0 copy-done.2
  21.9 0.4 reduce
  22.3 0.2 reshape.41
  22.5 0.1 copy.19.target_ref
  22.6 10.8 %all-to-all-done = s16[128,2,128]{2,1,0:T(2,128)(2,1)S(1)} async-done(((s16[128,2,128]{2,1,0:T(2,128)(2,1)}), s16[128,2,128]{2,1,0:T(2,128)(2,1)S(1)}, u32[]{:S(2)}, u32[]{:S(2)}) %all-to-all-start) | async-done | bytes 65568 | tf_op jit(solution)/shard_map/all_to_all | solution.py:506
  33.5 3.9 %splat.1 = s16[4,272,128]{2,1,0:T(8,128)(2,1)} custom-call(s16[256,128]{1,0:T(8,128)(2,1)S(1)} %bitcast.18), custom_call_target="tpu_custom_call" | custom-call | flops 536870912 | bytes 1048576 | tf_op jit(solution)/shard_map/splat/pallas_call | solution.py:384
  37.4 4.0 %all-to-all-start.1 = ((s16[4,272,128]{2,1,0:T(8,128)(2,1)}), s16[4,272,128]{2,1,0:T(8,128)(2,1)S(1)}, u32[]{:S(2)}, u32[]{:S(2)}) async-start(s16[4,272,128]{2,1,0:T(8,128)(2,1)} %splat.1), calls=%async_computation.1 | async-start | bytes 557056 | tf_op jit(solution)/shard_map/all_to_all | solution.py:506
  41.4 5.3 %pull_map.1.map_ref = f32[3,64,128]{2,1,0:T(8,128)S(1)} custom-call(s16[256,128]{1,0:T(8,128)(2,1)S(1)} %bitcast.19, bf16[32,1024]{1,0:T(8,128)(2,1)S(1)} %copy.19.target_ref), custom_call_target="tpu_custom_call" | custom-call | flops 4294967296 | bytes 1048576 | tf_op jit(solution)/shard_map/pull_map/pallas_call | solution.py:384
  46.8 0.0 copy-start
  46.8 0.0 copy-start.1
  46.8 0.4 all-to-all-done.1.parts_ref
  47.2 5.6 %pull.1 = bf16[512,128]{1,0:T(8,128)(2,1)S(1)} custom-call(s16[256,128]{1,0:T(8,128)(2,1)S(1)} %bitcast.20, s16[4,272,128]{2,1,0:T(8,128)(2,1)S(1)} %all-to-all-done.1.parts_ref, bf16[32,1024]{1,0:T(8,128)(2,1)S(1)} %copy.19.target_ref, f32[3,64,128]{2,1,0:T(8,128)S(1)} %pull_map.1.map_ref), custom_call_target="tpu_custom_call" | custom-call | flops 4294967296 | bytes 1048576 | tf_op jit(solution)/shard_map/pull/pallas_call | solution.py:384
  52.8 19.1 %all_to_all.25 = bf16[128,4,128]{2,1,0:T(4,128)(2,1)S(1)} all-to-all(bf16[128,4,128]{2,1,0:T(4,128)(2,1)S(1)} %bitcast.17), channel_id=1, replica_groups=mesh['y'=8,'z'=8,'core'=2,'seg'=4] {'y','z','core'}, dimensions={0} | all-to-all | bytes 262144 | tf_op jit(solution)/shard_map/all_to_all | solution.py:506
  71.9 0.0 copy-done
  71.9 0.0 copy-done.1
  71.9 2.0 %finish.1 = (f32[3,1024]{1,0:T(4,128)}, f32[32,128]{1,0:T(8,128)S(1)}, f32[1,128]{1,0:T(1,128)}) custom-call(bf16[512,128]{1,0:T(8,128)(2,1)S(1)} %bitcast.16, bf16[2,32,128]{2,1,0:T(8,128)(2,1)S(1)} %copy-done.1, bf16[3,256,1024]{2,1,0:T(8,128)(2,1)S(1)} %bitcast.23), custom_call_target="tpu_custom_call" | custom-call | flops 67108864 | bytes 1048576 | tf_op jit(solution)/shard_map/finish/pallas_call | solution.py:384
  73.9 10.6 %all_to_all.26 = f32[16,2,128]{2,1,0:T(2,128)S(1)} all-to-all(f32[16,2,128]{2,1,0:T(2,128)S(1)} %bitcast.21), channel_id=1, replica_groups=mesh['y'=8,'z'=8,'core'=2,'seg'=4] {'z','core'}, dimensions={0} | all-to-all | bytes 32768 | tf_op jit(solution)/shard_map/all_to_all | solution.py:506
  84.5 12.7 %all_to_all.27 = f32[32,2,128]{2,1,0:T(2,128)S(1)} all-to-all(f32[32,2,128]{2,1,0:T(2,128)S(1)} %broadcast_in_dim.2), channel_id=1, replica_groups=mesh['y'=8,'z'=8,'core'=2,'seg'=4] {'y','seg'}, dimensions={0} | all-to-all | bytes 65536 | tf_op jit(solution)/shard_map/all_to_all | solution.py:506
  97.3 0.6 reduce_sum.19
  (3 shorter events, 0.1 us)
Async XLA Ops:
  0.6 21.3 %copy-start.2 = (bf16[1,32768]{1,0:T(2,128)(2,1)S(1)}, bf16[1,32768]{1,0:T(2,128)(2,1)}, u32[]{:S(2)}) copy-start(bf16[1,32768]{1,0:T(2,128)(2,1)} %param.11) | copy-start | bytes 196612
  3.5 30.0 %all-to-all-start = ((s16[128,2,128]{2,1,0:T(2,128)(2,1)}), s16[128,2,128]{2,1,0:T(2,128)(2,1)S(1)}, u32[]{:S(2)}, u32[]{:S(2)}) async-start(s16[128,2,128]{2,1,0:T(2,128)(2,1)} %bitcast.25), calls=%async_computation | async-start | bytes 131072 | tf_op jit(solution)/shard_map/all_to_all | solution.py:506
  37.4 9.8 %all-to-all-start.1 = ((s16[4,272,128]{2,1,0:T(8,128)(2,1)}), s16[4,272,128]{2,1,0:T(8,128)(2,1)S(1)}, u32[]{:S(2)}, u32[]{:S(2)}) async-start(s16[4,272,128]{2,1,0:T(8,128)(2,1)} %splat.1), calls=%async_computation.1 | async-start | bytes 557056 | tf_op jit(solution)/shard_map/all_to_all | solution.py:506
  46.8 25.2 %copy-start = (bf16[256,3,1024]{2,0,1:T(8,128)(2,1)S(1)}, bf16[256,3,1024]{2,0,1:T(8,128)(2,1)}, u32[]{:S(2)}) copy-start(bf16[256,3,1024]{2,0,1:T(8,128)(2,1)} %param.9) | copy-start | bytes 4718596
  46.8 25.2 %copy-start.1 = (bf16[2,32,128]{2,1,0:T(8,128)(2,1)S(1)}, bf16[2,32,128]{2,1,0:T(8,128)(2,1)}, u32[]{:S(2)}) copy-start(bf16[2,32,128]{2,1,0:T(8,128)(2,1)} %get-tuple-element.9.refs_1_) | copy-start | bytes 49156

commit v11 on v10

--- a/solution.py
+++ b/solution.py
@@ -80,9 +80,10 @@
 def pack_kernel(*refs):
     sources, (send_ref, pick_ref), (cell_ref, block_ref, wide_ref) = refs[:6], refs[6:8], refs[8:11]
     local, sems = refs[11:17], refs[17]
+    pairs = list(zip(sources[:5], local[:5]))
+    pairs += [(sources[5].at[i], local[5].at[i]) for i in range(3)]
     copies = [
-        pltpu.make_async_copy(source, place, sems.at[i])
-        for i, (source, place) in enumerate(zip(sources, local))
+        pltpu.make_async_copy(source, place, sems.at[i]) for i, (source, place) in enumerate(pairs)
     ]
     for copy in copies:
         copy.start()
@@ -118,10 +119,11 @@
             shifts[slot] = shifts[slot] + against_rows(
                 mine.astype(jnp.bfloat16), offsets.astype(jnp.bfloat16)
             )
-    for copy in copies[2:]:
+    for copy in copies[2:5]:
         copy.wait()
     amps = jnp.broadcast_to(amps_ref[...], (16, amps_ref.shape[1])).astype(jnp.bfloat16)
     for component in range(3):
+        copies[5 + component].wait()
         moved = jnp.dot(amps, modes_ref[component], preferred_element_type=jnp.float32)
         places = coords_ref[pl.ds(component, 1), :] + moved[0:1]
         for cell in range(cells):
@@ -130,20 +132,23 @@
     for i in range(4):
         block_ref[pl.ds(i, cells, stride=4), :] = regroup([cell_ref[c] for c in range(4)], i)
     parts = exact_parts(block_ref[...])
+    picks = [pick.astype(jnp.bfloat16) for pick in picks]
+    both = jnp.concatenate(picks, axis=0)
+    high, middle, low = [jnp.dot(both, part, preferred_element_type=jnp.float32) for part in parts]
+    places = (high + middle) + low
     for slot in range(2):
-        pick = picks[slot].astype(jnp.bfloat16)
-        high, middle, low = [jnp.dot(pick, part, preferred_element_type=jnp.float32) for part in parts]
-        rows = ((high + middle) + low) + shifts[slot]
+        rows = places[slot * n_tile : (slot + 1) * n_tile] + shifts[slot]
         steps = jnp.clip(rows - MIDDLE, -SPAN, SPAN) * PLACE_STEPS
         wide_ref[pl.ds(slot, n_tile, stride=2), :] = jnp.where(
             quarter_of(rows.shape) < 3, steps, rows * MASS_STEPS
         )
-        pick_ref[slot] = against_rows(same, pick).astype(jnp.bfloat16)
+        pick_ref[slot] = against_rows(same, picks[slot]).astype(jnp.bfloat16)
     send_ref[...] = whole_steps(wide_ref[...])
 
 
 def finish_kernel(voxels, atoms, back_ref, pick_ref, modes_ref, forces_ref, spread_ref, score_ref, wide_ref, block_ref):
-    n_tile = pick_ref.shape[2]
+    blocks, n_tile = pick_ref.shape[1:]
+    picks = pick_ref[...].reshape(2 * blocks, n_tile)
     wide_ref[...] = back_ref[...].astype(jnp.float32)
     last = wide_ref[pl.ds(3, n_tile, stride=4), :]
     place = lax.broadcasted_iota(jnp.int32, (n_tile, LANES), 1) // 3
@@ -162,12 +167,10 @@
     for component in range(3):
         pulled = wide_ref[pl.ds(component, n_tile, stride=4), :]
         pulled = pulled * map_scale + pltpu.roll(pulled, LANES // 2, 1) * model_scale
-        parts = exact_parts(pulled)
-        first, second = [
-            sum([jnp.dot(pick_ref[slot], part, preferred_element_type=jnp.float32) for part in parts[::-1]])
-            for slot in range(2)
-        ]
-        block_ref[component] = first + pltpu.roll(second, LANES - ATOM_BLOCK, 1)
+        high, low, _ = exact_parts(pulled)
+        sums = jnp.dot(picks, low, preferred_element_type=jnp.float32)
+        sums = sums + jnp.dot(picks, high, preferred_element_type=jnp.float32)
+        block_ref[component] = sums[:blocks] + pltpu.roll(sums[blocks:], LANES - ATOM_BLOCK, 1)
         rows = regroup([block_ref[component, pl.ds(i, cells, stride=4), :] for i in range(4)], 0)
         for cell in range(cells):
             forces_ref[pl.ds(component, 1), cell * LANES : (cell + 1) * LANES] = rows[cell : cell + 1]
@@ -306,15 +309,18 @@
             line_ref[slot, i] = values.astype(jnp.bfloat16).astype(jnp.float32)
         for i, values in enumerate(factors(place_y, centers_of(size))):
             weight_ref[slot, i] = (masses * values).astype(jnp.bfloat16).astype(jnp.float32)
-        plain = jnp.concatenate([along_x, along_x], axis=0)
-        sloped = plain * jnp.concatenate([distance, distance], axis=0)
+        plain, sloped = [
+            jnp.concatenate([values, values], axis=0).astype(jnp.bfloat16)
+            for values in (along_x, distance * along_x)
+        ]
         for z in range(0, EDGE, 2):
-            line = pair_of_lines(line_ref.at[slot, 0], z, size)
-            slope_line = pair_of_lines(line_ref.at[slot, 1], z, size)
+            line, slope_line = [
+                pair_of_lines(line_ref.at[slot, i], z, size).astype(jnp.bfloat16) for i in range(2)
+            ]
             place = pl.ds(z * HIGHS, 2 * HIGHS)
-            planes[slot][0, place, :] = (line * plain).astype(jnp.bfloat16)
-            planes[slot][1, place, :] = (line * sloped).astype(jnp.bfloat16)
-            planes[slot][2, place, :] = (slope_line * plain).astype(jnp.bfloat16)
+            planes[slot][0, place, :] = line * plain
+            planes[slot][1, place, :] = line * sloped
+            planes[slot][2, place, :] = slope_line * plain
 
     def use(slot, chunk):
         for part in range(size // width):
@@ -409,7 +415,7 @@
             ((2 * n_tile, LANES), jnp.float32),
         ]
         + [(operand.shape, operand.dtype) for operand in operands]
-        + [pltpu.SemaphoreType.DMA((len(operands),))],
+        + [pltpu.SemaphoreType.DMA((len(operands) + 2,))],
         2**26,
         *operands,
         source=pltpu.HBM,

time: 98.2 us -> 97.2 us (0.990)
  Pallas kernels: 19.7 us -> 18.7 us
    pallas_call x5, Pallas kernels: 19.7 us -> 18.7 us  [call(): pl.pallas_call(kernel, out_shape=out_shape, in_specs=[pl.BlockSpec(memory...]
where the time goes in v11:
time: 97.2 us; the launch traced here: 96.9 us
  blocking collectives  41.9 us (43%)
  starting transfers between devices  22.4 us (23%)
  Pallas kernels  18.7 us (19%)
  waiting for transfers between devices  11.7 us (12%)
  other arithmetic  1 us (1%)
    all_to_all x3, blocking collectives, exchange(): return lax.all_to_all(values, axes, split_axis=0, concat_axis=0, tiled=True)  41.9 us
    all_to_all x2, starting transfers between devices, exchange(): return lax.all_to_all(values, axes, split_axis=0, concat_axis=0, tiled=True)  22.4 us
    pallas_call x5, Pallas kernels, call(): pl.pallas_call(kernel, out_shape=out_shape, in_specs=[pl.BlockSpec(memory...  18.7 us
    all_to_all x2, waiting for transfers between devices, exchange(): return lax.all_to_all(values, axes, split_axis=0, concat_axis=0, tiled=True)  11.7 us
  transfers between devices with their start and end apart: 2, of which 2 were waited for; matrix products, arithmetic and copies ran while one was open for 1% of the time, Pallas kernels for 5%

profile of v11, /device:TPU:1, one launch (start us, length us, event | category | flops | bytes accessed | tf_op | source)
XLA Modules:
  0.0 96.9 jit_solution(8675580272746300944)
XLA Ops:
  0.6 0.0 copy-start.2
  0.6 3.0 %pack.1 = (s16[256,128]{1,0:T(8,128)(2,1)}, bf16[2,32,128]{2,1,0:T(8,128)(2,1)}) custom-call(s32[4,32]{1,0:T(4,128)} %bitcast.29, s32[3,4,32]{2,1,0:T(4,128)} %bitcast.27, f32[1,256]{1,0:T(1,128)} %bitcast.30, f32[3,1024]{1,0:T(4,128)} %refs_3_.1, f32[8,128]{1,0:T(8,128)} %bitcast.28, bf16[3,256,1024]{2,1,0:T(8,128)(2,1)} %bitcast.22), custom_call_target="tpu_custom_call" | custom-call | flops 67108864 | bytes 1048576 | tf_op jit(solution)/shard_map/pack/pallas_call | solution.py:390
  3.6 18.4 %all-to-all-start = ((s16[128,2,128]{2,1,0:T(2,128)(2,1)}), s16[128,2,128]{2,1,0:T(2,128)(2,1)S(1)}, u32[]{:S(2)}, u32[]{:S(2)}) async-start(s16[128,2,128]{2,1,0:T(2,128)(2,1)} %bitcast.25), calls=%async_computation | async-start | bytes 131072 | tf_op jit(solution)/shard_map/all_to_all | solution.py:512
  22.1 0.0 copy-done.2
  22.1 0.4 reduce
  22.4 0.2 reshape.41
  22.7 0.1 copy.19.target_ref
  22.8 10.8 %all-to-all-done = s16[128,2,128]{2,1,0:T(2,128)(2,1)S(1)} async-done(((s16[128,2,128]{2,1,0:T(2,128)(2,1)}), s16[128,2,128]{2,1,0:T(2,128)(2,1)S(1)}, u32[]{:S(2)}, u32[]{:S(2)}) %all-to-all-start) | async-done | bytes 65568 | tf_op jit(solution)/shard_map/all_to_all | solution.py:512
  33.6 3.9 %splat.1 = s16[4,272,128]{2,1,0:T(8,128)(2,1)} custom-call(s16[256,128]{1,0:T(8,128)(2,1)S(1)} %bitcast.18), custom_call_target="tpu_custom_call" | custom-call | flops 536870912 | bytes 1048576 | tf_op jit(solution)/shard_map/splat/pallas_call | solution.py:390
  37.5 4.0 %all-to-all-start.1 = ((s16[4,272,128]{2,1,0:T(8,128)(2,1)}), s16[4,272,128]{2,1,0:T(8,128)(2,1)S(1)}, u32[]{:S(2)}, u32[]{:S(2)}) async-start(s16[4,272,128]{2,1,0:T(8,128)(2,1)} %splat.1), calls=%async_computation.1 | async-start | bytes 557056 | tf_op jit(solution)/shard_map/all_to_all | solution.py:512
  41.5 4.8 %pull_map.1.map_ref = f32[3,64,128]{2,1,0:T(8,128)S(1)} custom-call(s16[256,128]{1,0:T(8,128)(2,1)S(1)} %bitcast.19, bf16[32,1024]{1,0:T(8,128)(2,1)S(1)} %copy.19.target_ref), custom_call_target="tpu_custom_call" | custom-call | flops 4294967296 | bytes 1048576 | tf_op jit(solution)/shard_map/pull_map/pallas_call | solution.py:390
  46.4 0.0 copy-start
  46.4 0.0 copy-start.1
  46.4 0.9 all-to-all-done.1.parts_ref
  47.3 5.1 %pull.1 = bf16[512,128]{1,0:T(8,128)(2,1)S(1)} custom-call(s16[256,128]{1,0:T(8,128)(2,1)S(1)} %bitcast.20, s16[4,272,128]{2,1,0:T(8,128)(2,1)S(1)} %all-to-all-done.1.parts_ref, bf16[32,1024]{1,0:T(8,128)(2,1)S(1)} %copy.19.target_ref, f32[3,64,128]{2,1,0:T(8,128)S(1)} %pull_map.1.map_ref), custom_call_target="tpu_custom_call" | custom-call | flops 4294967296 | bytes 1048576 | tf_op jit(solution)/shard_map/pull/pallas_call | solution.py:390
  52.4 19.2 %all_to_all.25 = bf16[128,4,128]{2,1,0:T(4,128)(2,1)S(1)} all-to-all(bf16[128,4,128]{2,1,0:T(4,128)(2,1)S(1)} %bitcast.17), channel_id=1, replica_groups=mesh['y'=8,'z'=8,'core'=2,'seg'=4] {'y','z','core'}, dimensions={0} | all-to-all | bytes 262144 | tf_op jit(solution)/shard_map/all_to_all | solution.py:512
  71.6 0.0 copy-done
  71.6 0.0 copy-done.1
  71.6 1.9 %finish.1 = (f32[3,1024]{1,0:T(4,128)}, f32[32,128]{1,0:T(8,128)S(1)}, f32[1,128]{1,0:T(1,128)}) custom-call(bf16[512,128]{1,0:T(8,128)(2,1)S(1)} %bitcast.16, bf16[2,32,128]{2,1,0:T(8,128)(2,1)S(1)} %copy-done.1, bf16[3,256,1024]{2,1,0:T(8,128)(2,1)S(1)} %bitcast.23), custom_call_target="tpu_custom_call" | custom-call | flops 67108864 | bytes 1048576 | tf_op jit(solution)/shard_map/finish/pallas_call | solution.py:390
  73.5 10.6 %all_to_all.26 = f32[16,2,128]{2,1,0:T(2,128)S(1)} all-to-all(f32[16,2,128]{2,1,0:T(2,128)S(1)} %bitcast.21), channel_id=1, replica_groups=mesh['y'=8,'z'=8,'core'=2,'seg'=4] {'z','core'}, dimensions={0} | all-to-all | bytes 32768 | tf_op jit(solution)/shard_map/all_to_all | solution.py:512
  84.1 12.2 %all_to_all.27 = f32[32,2,128]{2,1,0:T(2,128)S(1)} all-to-all(f32[32,2,128]{2,1,0:T(2,128)S(1)} %broadcast_in_dim.2), channel_id=1, replica_groups=mesh['y'=8,'z'=8,'core'=2,'seg'=4] {'y','seg'}, dimensions={0} | all-to-all | bytes 65536 | tf_op jit(solution)/shard_map/all_to_all | solution.py:512
  96.3 0.6 reduce_sum.19
  (3 shorter events, 0.1 us)
Async XLA Ops:
  0.6 21.4 %copy-start.2 = (bf16[1,32768]{1,0:T(2,128)(2,1)S(1)}, bf16[1,32768]{1,0:T(2,128)(2,1)}, u32[]{:S(2)}) copy-start(bf16[1,32768]{1,0:T(2,128)(2,1)} %param.11) | copy-start | bytes 196612
  3.6 30.0 %all-to-all-start = ((s16[128,2,128]{2,1,0:T(2,128)(2,1)}), s16[128,2,128]{2,1,0:T(2,128)(2,1)S(1)}, u32[]{:S(2)}, u32[]{:S(2)}) async-start(s16[128,2,128]{2,1,0:T(2,128)(2,1)} %bitcast.25), calls=%async_computation | async-start | bytes 131072 | tf_op jit(solution)/shard_map/all_to_all | solution.py:512
  37.5 9.8 %all-to-all-start.1 = ((s16[4,272,128]{2,1,0:T(8,128)(2,1)}), s16[4,272,128]{2,1,0:T(8,128)(2,1)S(1)}, u32[]{:S(2)}, u32[]{:S(2)}) async-start(s16[4,272,128]{2,1,0:T(8,128)(2,1)} %splat.1), calls=%async_computation.1 | async-start | bytes 557056 | tf_op jit(solution)/shard_map/all_to_all | solution.py:512
  46.4 25.2 %copy-start = (bf16[256,3,1024]{2,0,1:T(8,128)(2,1)S(1)}, bf16[256,3,1024]{2,0,1:T(8,128)(2,1)}, u32[]{:S(2)}) copy-start(bf16[256,3,1024]{2,0,1:T(8,128)(2,1)} %param.9) | copy-start | bytes 4718596
  46.4 25.2 %copy-start.1 = (bf16[2,32,128]{2,1,0:T(8,128)(2,1)S(1)}, bf16[2,32,128]{2,1,0:T(8,128)(2,1)}, u32[]{:S(2)}) copy-start(bf16[2,32,128]{2,1,0:T(8,128)(2,1)} %get-tuple-element.9.refs_1_) | copy-start | bytes 49156

commit v12 on v10

--- a/solution.py
+++ b/solution.py
@@ -130,20 +130,23 @@
     for i in range(4):
         block_ref[pl.ds(i, cells, stride=4), :] = regroup([cell_ref[c] for c in range(4)], i)
     parts = exact_parts(block_ref[...])
+    picks = [pick.astype(jnp.bfloat16) for pick in picks]
+    both = jnp.concatenate(picks, axis=0)
+    high, middle, low = [jnp.dot(both, part, preferred_element_type=jnp.float32) for part in parts]
+    places = (high + middle) + low
     for slot in range(2):
-        pick = picks[slot].astype(jnp.bfloat16)
-        high, middle, low = [jnp.dot(pick, part, preferred_element_type=jnp.float32) for part in parts]
-        rows = ((high + middle) + low) + shifts[slot]
+        rows = places[slot * n_tile : (slot + 1) * n_tile] + shifts[slot]
         steps = jnp.clip(rows - MIDDLE, -SPAN, SPAN) * PLACE_STEPS
         wide_ref[pl.ds(slot, n_tile, stride=2), :] = jnp.where(
             quarter_of(rows.shape) < 3, steps, rows * MASS_STEPS
         )
-        pick_ref[slot] = against_rows(same, pick).astype(jnp.bfloat16)
+        pick_ref[slot] = against_rows(same, picks[slot]).astype(jnp.bfloat16)
     send_ref[...] = whole_steps(wide_ref[...])
 
 
 def finish_kernel(voxels, atoms, back_ref, pick_ref, modes_ref, forces_ref, spread_ref, score_ref, wide_ref, block_ref):
-    n_tile = pick_ref.shape[2]
+    blocks, n_tile = pick_ref.shape[1:]
+    picks = pick_ref[...].reshape(2 * blocks, n_tile)
     wide_ref[...] = back_ref[...].astype(jnp.float32)
     last = wide_ref[pl.ds(3, n_tile, stride=4), :]
     place = lax.broadcasted_iota(jnp.int32, (n_tile, LANES), 1) // 3
@@ -162,12 +165,10 @@
     for component in range(3):
         pulled = wide_ref[pl.ds(component, n_tile, stride=4), :]
         pulled = pulled * map_scale + pltpu.roll(pulled, LANES // 2, 1) * model_scale
-        parts = exact_parts(pulled)
-        first, second = [
-            sum([jnp.dot(pick_ref[slot], part, preferred_element_type=jnp.float32) for part in parts[::-1]])
-            for slot in range(2)
-        ]
-        block_ref[component] = first + pltpu.roll(second, LANES - ATOM_BLOCK, 1)
+        high, low, _ = exact_parts(pulled)
+        sums = jnp.dot(picks, low, preferred_element_type=jnp.float32)
+        sums = sums + jnp.dot(picks, high, preferred_element_type=jnp.float32)
+        block_ref[component] = sums[:blocks] + pltpu.roll(sums[blocks:], LANES - ATOM_BLOCK, 1)
         rows = regroup([block_ref[component, pl.ds(i, cells, stride=4), :] for i in range(4)], 0)
         for cell in range(cells):
             forces_ref[pl.ds(component, 1), cell * LANES : (cell + 1) * LANES] = rows[cell : cell + 1]
@@ -323,13 +324,14 @@
                 jnp.dot(row_ref[...], planes[slot][i, :, atoms], preferred_element_type=jnp.float32)
                 for i in range(3)
             ]
-            sums = [jnp.zeros((EDGE, width), jnp.float32) for _ in range(3)]
-            for low in range(STEP):
-                fine = fine_ref[slot, pl.ds(low, 1), atoms]
-                plain, by_x, by_z = [values[low * EDGE : (low + 1) * EDGE] for values in pulled]
-                sums[0] = sums[0] + (by_x + LOWS[low] * plain) * fine
-                sums[1] = sums[1] + plain * fine
-                sums[2] = sums[2] + by_z * fine
+            fine = [fine_ref[slot, pl.ds(low, 1), atoms] for low in range(STEP)]
+            plain, by_x, by_z = [
+                [values[low * EDGE : (low + 1) * EDGE] * fine[low] for low in range(STEP)]
+                for values in pulled
+            ]
+            by_low = 1.5 * (plain[3] - plain[0]) + 0.5 * (plain[2] - plain[1])
+            sums = [(values[0] + values[1]) + (values[2] + values[3]) for values in (by_x, plain, by_z)]
+            sums[0] = sums[0] + by_low
             along_y, slope_y = [weight_ref[slot, i, :, atoms] for i in range(2)]
             rows = width // LANES
             for component, weight in enumerate((inverse_var * along_y, slope_y, along_y)):
@@ -400,7 +402,7 @@
         pack_kernel,
         "pack",
         (
-            jax.ShapeDtypeStruct((2 * n_tile, LANES), jnp.int16),
+            pltpu.VMEM((2 * n_tile, LANES), jnp.int16),
             jax.ShapeDtypeStruct((2, blocks, n_tile), jnp.bfloat16),
         ),
         [
@@ -413,7 +415,7 @@
         2**26,
         *operands,
         source=pltpu.HBM,
-        limit=60,
+        limit=56,
     )
 
 
@@ -443,7 +445,7 @@
     return call(
         splat_kernel,
         "splat",
-        jax.ShapeDtypeStruct((copies, EDGE * PLANE // LANES + POWER_ROWS, LANES), jnp.int16),
+        pltpu.VMEM((copies, EDGE * PLANE // LANES + POWER_ROWS, LANES), jnp.int16),
         [
             ((4 * groups, LANES), jnp.float32), ((4, groups, LANES), jnp.float32),
             ((2, EDGE, size), jnp.float32),

time: 98.2 us -> 98.1 us (level)
  no operation moved by 1% of the time
where the time goes in v12:
time: 98.1 us; the launch traced here: 97.7 us
  blocking collectives  42.4 us (43%)
  starting transfers between devices  22.4 us (23%)
  Pallas kernels  19.5 us (20%)
  waiting for transfers between devices  11.3 us (12%)
  other arithmetic  1 us (1%)
    all_to_all x3, blocking collectives, exchange(): return lax.all_to_all(values, axes, split_axis=0, concat_axis=0, tiled=True)  42.4 us
    all_to_all x2, starting transfers between devices, exchange(): return lax.all_to_all(values, axes, split_axis=0, concat_axis=0, tiled=True)  22.4 us
    pallas_call x5, Pallas kernels, call(): pl.pallas_call(kernel, out_shape=out_shape, in_specs=[pl.BlockSpec(memory...  19.5 us
    all_to_all x2, waiting for transfers between devices, exchange(): return lax.all_to_all(values, axes, split_axis=0, concat_axis=0, tiled=True)  11.3 us
  transfers between devices with their start and end apart: 2, of which 2 were waited for; matrix products, arithmetic and copies ran while one was open for 1% of the time, Pallas kernels for 5%

profile of v12, /device:TPU:1, one launch (start us, length us, event | category | flops | bytes accessed | tf_op | source)
XLA Modules:
  0.0 97.7 jit_solution(11324041947417115158)
XLA Ops:
  0.6 0.0 copy-start.2
  0.6 2.8 %pack.1 = (s16[256,128]{1,0:T(8,128)(2,1)}, bf16[2,32,128]{2,1,0:T(8,128)(2,1)}) custom-call(s32[4,32]{1,0:T(4,128)} %bitcast.28, s32[3,4,32]{2,1,0:T(4,128)} %bitcast.26, f32[1,256]{1,0:T(1,128)} %bitcast.29, f32[3,1024]{1,0:T(4,128)} %refs_3_.1, f32[8,128]{1,0:T(8,128)} %bitcast.27, bf16[3,256,1024]{2,1,0:T(8,128)(2,1)} %bitcast.22), custom_call_target="tpu_custom_call" | custom-call | flops 67108864 | bytes 1048576 | tf_op jit(solution)/shard_map/pack/pallas_call | solution.py:386
  3.5 18.4 %all-to-all-start = ((s16[128,2,128]{2,1,0:T(2,128)(2,1)}), s16[128,2,128]{2,1,0:T(2,128)(2,1)S(1)}, u32[]{:S(2)}, u32[]{:S(2)}) async-start(s16[128,2,128]{2,1,0:T(2,128)(2,1)} %bitcast.5), calls=%async_computation | async-start | bytes 131072 | tf_op jit(solution)/shard_map/all_to_all | solution.py:508
  21.9 0.0 copy-done.2
  21.9 0.4 reduce
  22.3 0.2 reshape.41
  22.5 0.1 copy.19.target_ref
  22.6 10.8 %all-to-all-done = s16[128,2,128]{2,1,0:T(2,128)(2,1)S(1)} async-done(((s16[128,2,128]{2,1,0:T(2,128)(2,1)}), s16[128,2,128]{2,1,0:T(2,128)(2,1)S(1)}, u32[]{:S(2)}, u32[]{:S(2)}) %all-to-all-start) | async-done | bytes 65568 | tf_op jit(solution)/shard_map/all_to_all | solution.py:508
  33.5 3.9 %splat.1 = s16[4,272,128]{2,1,0:T(8,128)(2,1)} custom-call(s16[256,128]{1,0:T(8,128)(2,1)S(1)} %bitcast.18), custom_call_target="tpu_custom_call" | custom-call | flops 536870912 | bytes 1048576 | tf_op jit(solution)/shard_map/splat/pallas_call | solution.py:386
  37.4 4.0 %all-to-all-start.1 = ((s16[4,272,128]{2,1,0:T(8,128)(2,1)}), s16[4,272,128]{2,1,0:T(8,128)(2,1)S(1)}, u32[]{:S(2)}, u32[]{:S(2)}) async-start(s16[4,272,128]{2,1,0:T(8,128)(2,1)} %splat.1), calls=%async_computation.1 | async-start | bytes 557056 | tf_op jit(solution)/shard_map/all_to_all | solution.py:508
  41.4 5.3 %pull_map.1.map_ref = f32[3,64,128]{2,1,0:T(8,128)S(1)} custom-call(s16[256,128]{1,0:T(8,128)(2,1)S(1)} %bitcast.19, bf16[32,1024]{1,0:T(8,128)(2,1)S(1)} %copy.19.target_ref), custom_call_target="tpu_custom_call" | custom-call | flops 4294967296 | bytes 1048576 | tf_op jit(solution)/shard_map/pull_map/pallas_call | solution.py:386
  46.7 0.0 copy-start
  46.7 0.0 copy-start.1
  46.8 0.4 all-to-all-done.1.parts_ref
  47.2 5.6 %pull.1 = bf16[512,128]{1,0:T(8,128)(2,1)S(1)} custom-call(s16[256,128]{1,0:T(8,128)(2,1)S(1)} %bitcast.20, s16[4,272,128]{2,1,0:T(8,128)(2,1)S(1)} %all-to-all-done.1.parts_ref, bf16[32,1024]{1,0:T(8,128)(2,1)S(1)} %copy.19.target_ref, f32[3,64,128]{2,1,0:T(8,128)S(1)} %pull_map.1.map_ref), custom_call_target="tpu_custom_call" | custom-call | flops 4294967296 | bytes 1048576 | tf_op jit(solution)/shard_map/pull/pallas_call | solution.py:386
  52.8 19.1 %all_to_all.25 = bf16[128,4,128]{2,1,0:T(4,128)(2,1)S(1)} all-to-all(bf16[128,4,128]{2,1,0:T(4,128)(2,1)S(1)} %bitcast.17), channel_id=1, replica_groups=mesh['y'=8,'z'=8,'core'=2,'seg'=4] {'y','z','core'}, dimensions={0} | all-to-all | bytes 262144 | tf_op jit(solution)/shard_map/all_to_all | solution.py:508
  71.9 0.0 copy-done
  71.9 0.0 copy-done.1
  71.9 1.9 %finish.1 = (f32[3,1024]{1,0:T(4,128)}, f32[32,128]{1,0:T(8,128)S(1)}, f32[1,128]{1,0:T(1,128)}) custom-call(bf16[512,128]{1,0:T(8,128)(2,1)S(1)} %bitcast.16, bf16[2,32,128]{2,1,0:T(8,128)(2,1)S(1)} %copy-done.1, bf16[3,256,1024]{2,1,0:T(8,128)(2,1)S(1)} %bitcast.23), custom_call_target="tpu_custom_call" | custom-call | flops 67108864 | bytes 1048576 | tf_op jit(solution)/shard_map/finish/pallas_call | solution.py:386
  73.8 10.6 %all_to_all.26 = f32[16,2,128]{2,1,0:T(2,128)S(1)} all-to-all(f32[16,2,128]{2,1,0:T(2,128)S(1)} %bitcast.21), channel_id=1, replica_groups=mesh['y'=8,'z'=8,'core'=2,'seg'=4] {'z','core'}, dimensions={0} | all-to-all | bytes 32768 | tf_op jit(solution)/shard_map/all_to_all | solution.py:508
  84.4 12.7 %all_to_all.27 = f32[32,2,128]{2,1,0:T(2,128)S(1)} all-to-all(f32[32,2,128]{2,1,0:T(2,128)S(1)} %broadcast_in_dim.2), channel_id=1, replica_groups=mesh['y'=8,'z'=8,'core'=2,'seg'=4] {'y','seg'}, dimensions={0} | all-to-all | bytes 65536 | tf_op jit(solution)/shard_map/all_to_all | solution.py:508
  97.1 0.6 reduce_sum.19
  (3 shorter events, 0.1 us)
Async XLA Ops:
  0.6 21.3 %copy-start.2 = (bf16[1,32768]{1,0:T(2,128)(2,1)S(1)}, bf16[1,32768]{1,0:T(2,128)(2,1)}, u32[]{:S(2)}) copy-start(bf16[1,32768]{1,0:T(2,128)(2,1)} %param.11) | copy-start | bytes 196612
  3.5 30.0 %all-to-all-start = ((s16[128,2,128]{2,1,0:T(2,128)(2,1)}), s16[128,2,128]{2,1,0:T(2,128)(2,1)S(1)}, u32[]{:S(2)}, u32[]{:S(2)}) async-start(s16[128,2,128]{2,1,0:T(2,128)(2,1)} %bitcast.5), calls=%async_computation | async-start | bytes 131072 | tf_op jit(solution)/shard_map/all_to_all | solution.py:508
  37.4 9.8 %all-to-all-start.1 = ((s16[4,272,128]{2,1,0:T(8,128)(2,1)}), s16[4,272,128]{2,1,0:T(8,128)(2,1)S(1)}, u32[]{:S(2)}, u32[]{:S(2)}) async-start(s16[4,272,128]{2,1,0:T(8,128)(2,1)} %splat.1), calls=%async_computation.1 | async-start | bytes 557056 | tf_op jit(solution)/shard_map/all_to_all | solution.py:508
  46.7 25.2 %copy-start = (bf16[256,3,1024]{2,0,1:T(8,128)(2,1)S(1)}, bf16[256,3,1024]{2,0,1:T(8,128)(2,1)}, u32[]{:S(2)}) copy-start(bf16[256,3,1024]{2,0,1:T(8,128)(2,1)} %param.9) | copy-start | bytes 4718596
  46.7 25.2 %copy-start.1 = (bf16[2,32,128]{2,1,0:T(8,128)(2,1)S(1)}, bf16[2,32,128]{2,1,0:T(8,128)(2,1)}, u32[]{:S(2)}) copy-start(bf16[2,32,128]{2,1,0:T(8,128)(2,1)} %get-tuple-element.9.refs_1_) | copy-start | bytes 49156

commit v13 on v12

--- a/solution.py
+++ b/solution.py
@@ -201,12 +201,16 @@
 def pipeline(chunks, build, use):
     build(0, 0)
 
-    @pl.loop(0, chunks // 2)
+    @pl.loop(0, chunks // 2 - 1)
     def _(step):
         build(1, 2 * step + 1)
         use(0, 2 * step)
-        build(0, jnp.minimum(2 * step + 2, chunks - 2))
+        build(0, 2 * step + 2)
         use(1, 2 * step + 1)
+
+    build(1, chunks - 1)
+    use(0, chunks - 2)
+    use(1, chunks - 1)
 
 
 def pair_of_lines(line_ref, z, size):
@@ -290,7 +294,7 @@
         row_ref[low * EDGE : (low + 1) * EDGE] = rows.astype(jnp.bfloat16)
 
 
-def pull_rows(place_ref, row_ref, sum_ref, line_ref, even_ref, odd_ref, weight_ref, fine_ref):
+def pull_rows(keep, shape_ref, place_ref, row_ref, sum_ref, line_ref, even_ref, odd_ref, fine_ref):
     planes = (even_ref, odd_ref)
     size = even_ref.shape[2]
     width = min(WIDTH, size)
@@ -301,12 +305,15 @@
         distance = coarse_of(row_number(HIGHS, size)) - place_x
         along_x = jnp.exp2(-rate * (distance * distance))
         near = jnp.clip(place_x, -SPAN, SPAN)
-        for low in range(STEP):
-            fine_ref[slot, pl.ds(low, 1), :] = jnp.exp2((2.0 * rate * LOWS[low]) * near)
-        for i, values in enumerate(factors(place_z, centers_of(size))):
-            line_ref[slot, i] = values.astype(jnp.bfloat16).astype(jnp.float32)
-        for i, values in enumerate(factors(place_y, centers_of(size))):
-            weight_ref[slot, i] = (masses * values).astype(jnp.bfloat16).astype(jnp.float32)
+        lows = row_number(STEP, size).astype(jnp.float32) + LOWS[0]
+        fine_ref[slot] = jnp.exp2((2.0 * rate) * lows * near)
+        if keep:
+            for i, values in enumerate(factors(place_z, centers_of(size))):
+                shape_ref[chunk, i] = values.astype(jnp.bfloat16)
+            for i, values in enumerate(factors(place_y, centers_of(size))):
+                shape_ref[chunk, 2 + i] = (masses * values).astype(jnp.bfloat16)
+        for i in range(2):
+            line_ref[slot, i] = shape_ref[chunk, i].astype(jnp.float32)
         plain = jnp.concatenate([along_x, along_x], axis=0)
         sloped = plain * jnp.concatenate([distance, distance], axis=0)
         for z in range(0, EDGE, 2):
@@ -332,7 +339,7 @@
             by_low = 1.5 * (plain[3] - plain[0]) + 0.5 * (plain[2] - plain[1])
             sums = [(values[0] + values[1]) + (values[2] + values[3]) for values in (by_x, plain, by_z)]
             sums[0] = sums[0] + by_low
-            along_y, slope_y = [weight_ref[slot, i, :, atoms] for i in range(2)]
+            along_y, slope_y = [shape_ref[chunk, 2 + i, :, atoms].astype(jnp.float32) for i in range(2)]
             rows = width // LANES
             for component, weight in enumerate((inverse_var * along_y, slope_y, along_y)):
                 force = jnp.sum(sums[component] * weight, axis=0, keepdims=True)
@@ -343,14 +350,13 @@
     pipeline(place_ref.shape[1] * LANES // size, build, use)
 
 
-def map_kernel(got_ref, target_ref, sum_ref, wide_ref, place_ref, row_ref, *scratch):
+def map_kernel(got_ref, target_ref, sum_ref, place_ref, shape_ref, wide_ref, row_ref, *scratch):
     unpack_rows(got_ref, wide_ref, place_ref)
     field_rows(row_ref, target_ref[...].astype(jnp.float32))
-    pull_rows(place_ref, row_ref, sum_ref, *scratch)
-
-
-def pull_kernel(got_ref, parts_ref, target_ref, map_ref, out_ref, wide_ref, place_ref, row_ref, sum_ref, stage_ref, *scratch):
-    unpack_rows(got_ref, wide_ref, place_ref)
+    pull_rows(True, shape_ref, place_ref, row_ref, sum_ref, *scratch)
+
+
+def pull_kernel(parts_ref, target_ref, map_ref, place_ref, shape_ref, out_ref, row_ref, sum_ref, stage_ref, *scratch):
     parts = [density_of(parts_ref, i) for i in range(4)]
     density = (parts[0] + parts[2]) + (parts[1] + parts[3])
     wide = target_ref[...].astype(jnp.float32)
@@ -367,7 +373,7 @@
         for i, term in enumerate(exact_parts(jnp.broadcast_to(value, (8, LANES)))):
             last = jnp.where(lane == 3 * place + i, term.astype(jnp.float32), last)
     stage_ref[pl.ds(3, 2 * pairs, stride=4), :] = jnp.broadcast_to(last[0:1], (2 * pairs, LANES))
-    pull_rows(place_ref, row_ref, sum_ref, *scratch)
+    pull_rows(False, shape_ref, place_ref, row_ref, sum_ref, *scratch)
     left = lax.broadcasted_iota(jnp.int32, (pairs, LANES), 1) < LANES // 2
     for component in range(3):
         first = sum_ref[component]
@@ -463,41 +469,44 @@
 def pull_scratch(groups):
     size = min(CHUNK, groups * LANES // 2)
     plane = ((3, EDGE * HIGHS, size), jnp.bfloat16)
-    lines = ((2, 2, EDGE, size), jnp.float32)
-    return [lines, plane, plane, lines, ((2, STEP, size), jnp.float32)]
+    return [((2, 2, EDGE, size), jnp.float32), plane, plane, ((2, STEP, size), jnp.float32)]
 
 
 def pull_map(got, target):
     groups = got.shape[0] // 4
+    size = min(CHUNK, groups * LANES // 2)
     return call(
         map_kernel,
         "pull_map",
-        jax.ShapeDtypeStruct((3, groups, LANES), jnp.float32),
-        [((4 * groups, LANES), jnp.float32), ((4, groups, LANES), jnp.float32), ((STEP * EDGE, EDGE * HIGHS), jnp.bfloat16)] + pull_scratch(groups),
+        (
+            pltpu.VMEM((3, groups, LANES), jnp.float32),
+            pltpu.VMEM((4, groups, LANES), jnp.float32),
+            pltpu.VMEM((groups * LANES // size, 4, EDGE, size), jnp.bfloat16),
+        ),
+        [((4 * groups, LANES), jnp.float32), ((STEP * EDGE, EDGE * HIGHS), jnp.bfloat16)]
+        + pull_scratch(groups),
         2**32,
         got,
         target,
     )
 
 
-def pull(got, parts, target, from_map):
-    groups = got.shape[0] // 4
+def pull(parts, target, from_map):
+    groups = from_map[0].shape[1]
     return call(
         pull_kernel,
         "pull",
         jax.ShapeDtypeStruct((8 * groups, LANES), jnp.bfloat16),
         [
-            ((4 * groups, LANES), jnp.float32), ((4, groups, LANES), jnp.float32),
             ((STEP * EDGE, EDGE * HIGHS), jnp.bfloat16),
             ((3, groups, LANES), jnp.float32),
             ((8 * groups, LANES), jnp.float32),
         ]
         + pull_scratch(groups),
         2**32,
-        got,
         parts,
         target,
-        from_map,
+        *from_map,
     )
 
 
@@ -526,7 +535,7 @@
     target = density_map.reshape(EDGE, HIGHS, STEP, EDGE)
     target = jnp.transpose(target, (3, 2, 0, 1)).reshape(EDGE, PLANE)
     parts = exchange(splat(got, n_seg), "seg")
-    pulled = pull(got, parts, target, pull_map(got, target))
+    pulled = pull(parts, target, pull_map(got, target))
     back = exchange(pulled.reshape(n_tile, 4, LANES), TILE_AXES).reshape(4 * n_tile, LANES)
     near, far = ("z", "core"), ("y", "seg")
     forces, spread, score = finish(

time: 98.1 us -> 96.7 us (0.986)
  Pallas kernels: 19.5 us -> 18.3 us
    pallas_call x5, Pallas kernels: 19.5 us -> 18.3 us  [call(): pl.pallas_call(kernel, out_shape=out_shape, in_specs=[pl.BlockSpec(memory...]
where the time goes in v13:
time: 96.7 us; the launch traced here: 96.4 us
  blocking collectives  42.1 us (44%)
  starting transfers between devices  22.5 us (23%)
  Pallas kernels  18.3 us (19%)
  waiting for transfers between devices  11.5 us (12%)
  other arithmetic  1 us (1%)
    all_to_all x3, blocking collectives, exchange(): return lax.all_to_all(values, axes, split_axis=0, concat_axis=0, tiled=True)  42.1 us
    all_to_all x2, starting transfers between devices, exchange(): return lax.all_to_all(values, axes, split_axis=0, concat_axis=0, tiled=True)  22.5 us
    pallas_call x5, Pallas kernels, call(): pl.pallas_call(kernel, out_shape=out_shape, in_specs=[pl.BlockSpec(memory...  18.3 us
    all_to_all x2, waiting for transfers between devices, exchange(): return lax.all_to_all(values, axes, split_axis=0, concat_axis=0, tiled=True)  11.5 us
  transfers between devices with their start and end apart: 2, of which 2 were waited for; matrix products, arithmetic and copies ran while one was open for 1% of the time, Pallas kernels for 5%

profile of v13, /device:TPU:1, one launch (start us, length us, event | category | flops | bytes accessed | tf_op | source)
XLA Modules:
  0.0 96.4 jit_solution(9030857158639880114)
XLA Ops:
  0.6 0.0 copy-start.2
  0.6 2.8 %pack.1 = (s16[256,128]{1,0:T(8,128)(2,1)}, bf16[2,32,128]{2,1,0:T(8,128)(2,1)}) custom-call(s32[4,32]{1,0:T(4,128)} %bitcast.27, s32[3,4,32]{2,1,0:T(4,128)} %bitcast.25, f32[1,256]{1,0:T(1,128)} %bitcast.28, f32[3,1024]{1,0:T(4,128)} %refs_3_.1, f32[8,128]{1,0:T(8,128)} %bitcast.26, bf16[3,256,1024]{2,1,0:T(8,128)(2,1)} %bitcast.21), custom_call_target="tpu_custom_call" | custom-call | flops 67108864 | bytes 1048576 | tf_op jit(solution)/shard_map/pack/pallas_call | solution.py:392
  3.5 18.4 %all-to-all-start = ((s16[128,2,128]{2,1,0:T(2,128)(2,1)}), s16[128,2,128]{2,1,0:T(2,128)(2,1)S(1)}, u32[]{:S(2)}, u32[]{:S(2)}) async-start(s16[128,2,128]{2,1,0:T(2,128)(2,1)} %bitcast.5), calls=%async_computation | async-start | bytes 131072 | tf_op jit(solution)/shard_map/all_to_all | solution.py:517
  21.9 0.0 copy-done.2
  21.9 0.4 reduce
  22.3 0.2 reshape.41
  22.5 0.1 copy.19.target_ref
  22.6 10.8 %all-to-all-done = s16[128,2,128]{2,1,0:T(2,128)(2,1)S(1)} async-done(((s16[128,2,128]{2,1,0:T(2,128)(2,1)}), s16[128,2,128]{2,1,0:T(2,128)(2,1)S(1)}, u32[]{:S(2)}, u32[]{:S(2)}) %all-to-all-start) | async-done | bytes 65568 | tf_op jit(solution)/shard_map/all_to_all | solution.py:517
  33.4 4.0 %splat.1 = s16[4,272,128]{2,1,0:T(8,128)(2,1)} custom-call(s16[256,128]{1,0:T(8,128)(2,1)S(1)} %bitcast.18), custom_call_target="tpu_custom_call" | custom-call | flops 536870912 | bytes 1048576 | tf_op jit(solution)/shard_map/splat/pallas_call | solution.py:392
  37.4 4.0 %all-to-all-start.1 = ((s16[4,272,128]{2,1,0:T(8,128)(2,1)}), s16[4,272,128]{2,1,0:T(8,128)(2,1)S(1)}, u32[]{:S(2)}, u32[]{:S(2)}) async-start(s16[4,272,128]{2,1,0:T(8,128)(2,1)} %splat.1), calls=%async_computation.1 | async-start | bytes 557056 | tf_op jit(solution)/shard_map/all_to_all | solution.py:517
  41.4 5.1 %pull_map.1 = (f32[3,64,128]{2,1,0:T(8,128)S(1)}, f32[4,64,128]{2,1,0:T(8,128)S(1)}, bf16[16,4,32,512]{3,2,1,0:T(8,128)(2,1)S(1)}) custom-call(s16[256,128]{1,0:T(8,128)(2,1)S(1)} %bitcast.19, bf16[32,1024]{1,0:T(8,128)(2,1)S(1)} %copy.19.target_ref), custom_call_target="tpu_custom_call" | custom-call | flops 4294967296 | bytes 1048576 | tf_op jit(solution)/shard_map/pull_map/pallas_call | solution.py:392
  46.5 0.7 all-to-all-done.1.parts_ref
  47.2 0.0 copy-start
  47.2 0.0 copy-start.1
  47.2 4.5 %pull.1 = bf16[512,128]{1,0:T(8,128)(2,1)S(1)} custom-call(s16[4,272,128]{2,1,0:T(8,128)(2,1)S(1)} %all-to-all-done.1.parts_ref, bf16[32,1024]{1,0:T(8,128)(2,1)S(1)} %copy.19.target_ref, f32[3,64,128]{2,1,0:T(8,128)S(1)} %get-tuple-element.12.map_ref, f32[4,64,128]{2,1,0:T(8,128)S(1)} %get-tuple-element.13.place_ref, ...), custom_call_target="tpu_custom_call" | custom-call | flops 4294967296 | bytes 1048576 | tf_op jit(solution)/shard_map/pull/pallas_call | solution.py:392
  51.7 19.1 %all_to_all.25 = bf16[128,4,128]{2,1,0:T(4,128)(2,1)S(1)} all-to-all(bf16[128,4,128]{2,1,0:T(4,128)(2,1)S(1)} %bitcast.17), channel_id=1, replica_groups=mesh['y'=8,'z'=8,'core'=2,'seg'=4] {'y','z','core'}, dimensions={0} | all-to-all | bytes 262144 | tf_op jit(solution)/shard_map/all_to_all | solution.py:517
  70.9 0.0 copy-done
  70.9 0.0 copy-done.1
  70.9 1.9 %finish.1 = (f32[3,1024]{1,0:T(4,128)}, f32[32,128]{1,0:T(8,128)S(1)}, f32[1,128]{1,0:T(1,128)}) custom-call(bf16[512,128]{1,0:T(8,128)(2,1)S(1)} %bitcast.16, bf16[2,32,128]{2,1,0:T(8,128)(2,1)S(1)} %copy-done.1, bf16[3,256,1024]{2,1,0:T(8,128)(2,1)S(1)} %bitcast.22), custom_call_target="tpu_custom_call" | custom-call | flops 67108864 | bytes 1048576 | tf_op jit(solution)/shard_map/finish/pallas_call | solution.py:392
  72.8 10.6 %all_to_all.26 = f32[16,2,128]{2,1,0:T(2,128)S(1)} all-to-all(f32[16,2,128]{2,1,0:T(2,128)S(1)} %bitcast.20), channel_id=1, replica_groups=mesh['y'=8,'z'=8,'core'=2,'seg'=4] {'z','core'}, dimensions={0} | all-to-all | bytes 32768 | tf_op jit(solution)/shard_map/all_to_all | solution.py:517
  83.4 12.4 %all_to_all.27 = f32[32,2,128]{2,1,0:T(2,128)S(1)} all-to-all(f32[32,2,128]{2,1,0:T(2,128)S(1)} %broadcast_in_dim.2), channel_id=1, replica_groups=mesh['y'=8,'z'=8,'core'=2,'seg'=4] {'y','seg'}, dimensions={0} | all-to-all | bytes 65536 | tf_op jit(solution)/shard_map/all_to_all | solution.py:517
  95.8 0.6 reduce_sum.19
  (3 shorter events, 0.1 us)
Async XLA Ops:
  0.6 21.3 %copy-start.2 = (bf16[1,32768]{1,0:T(2,128)(2,1)S(1)}, bf16[1,32768]{1,0:T(2,128)(2,1)}, u32[]{:S(2)}) copy-start(bf16[1,32768]{1,0:T(2,128)(2,1)} %param.11) | copy-start | bytes 196612
  3.5 29.9 %all-to-all-start = ((s16[128,2,128]{2,1,0:T(2,128)(2,1)}), s16[128,2,128]{2,1,0:T(2,128)(2,1)S(1)}, u32[]{:S(2)}, u32[]{:S(2)}) async-start(s16[128,2,128]{2,1,0:T(2,128)(2,1)} %bitcast.5), calls=%async_computation | async-start | bytes 131072 | tf_op jit(solution)/shard_map/all_to_all | solution.py:517
  37.4 9.8 %all-to-all-start.1 = ((s16[4,272,128]{2,1,0:T(8,128)(2,1)}), s16[4,272,128]{2,1,0:T(8,128)(2,1)S(1)}, u32[]{:S(2)}, u32[]{:S(2)}) async-start(s16[4,272,128]{2,1,0:T(8,128)(2,1)} %splat.1), calls=%async_computation.1 | async-start | bytes 557056 | tf_op jit(solution)/shard_map/all_to_all | solution.py:517
  47.2 23.6 %copy-start = (bf16[256,3,1024]{2,0,1:T(8,128)(2,1)S(1)}, bf16[256,3,1024]{2,0,1:T(8,128)(2,1)}, u32[]{:S(2)}) copy-start(bf16[256,3,1024]{2,0,1:T(8,128)(2,1)} %param.9) | copy-start | bytes 4718596
  47.2 23.6 %copy-start.1 = (bf16[2,32,128]{2,1,0:T(8,128)(2,1)S(1)}, bf16[2,32,128]{2,1,0:T(8,128)(2,1)}, u32[]{:S(2)}) copy-start(bf16[2,32,128]{2,1,0:T(8,128)(2,1)} %get-tuple-element.15.refs_1_) | copy-start | bytes 49156

commit v14 on v13

--- a/solution.py
+++ b/solution.py
@@ -198,19 +198,20 @@
     )
 
 
-def pipeline(chunks, build, use):
+def pipeline(chunks, build, use, last_apart=True):
     build(0, 0)
 
-    @pl.loop(0, chunks // 2 - 1)
+    @pl.loop(0, chunks // 2 - last_apart)
     def _(step):
         build(1, 2 * step + 1)
         use(0, 2 * step)
-        build(0, 2 * step + 2)
+        build(0, 2 * step + 2 if last_apart else jnp.minimum(2 * step + 2, chunks - 2))
         use(1, 2 * step + 1)
 
-    build(1, chunks - 1)
-    use(0, chunks - 2)
-    use(1, chunks - 1)
+    if last_apart:
+        build(1, chunks - 1)
+        use(0, chunks - 2)
+        use(1, chunks - 1)
 
 
 def pair_of_lines(line_ref, z, size):
@@ -231,7 +232,7 @@
     return jnp.exp2(-rate * (2.0 * LOWS[low] * coarse + LOWS[low] ** 2))
 
 
-def splat_kernel(got_ref, out_ref, wide_ref, place_ref, line_ref, even_ref, odd_ref, even_weight_ref, odd_weight_ref, sum_ref):
+def splat_kernel(got_ref, out_ref, wide_ref, place_ref, line_ref, even_ref, odd_ref, even_weight_ref, odd_weight_ref, fine_ref, sum_ref):
     size = even_ref.shape[1]
     planes, weights = (even_ref, odd_ref), (even_weight_ref, odd_weight_ref)
     unpack_rows(got_ref, wide_ref, place_ref)
@@ -241,16 +242,19 @@
         place_x, place_y, place_z, masses = [chunk_row(place_ref, i, chunk, size) for i in range(4)]
         place_x = place_x - MIDDLE
         along_x = factors(place_x, coarse_of(row_number(HIGHS, size)))[0]
-        line_ref[slot] = factors(place_z, centers_of(size))[0]
+        doubled = jnp.concatenate([along_x, along_x], axis=0).astype(jnp.bfloat16)
+        along_z = factors(place_z, centers_of(size))[0]
+        line_ref[slot] = along_z.astype(jnp.bfloat16).astype(jnp.float32)
         for z in range(0, EDGE, 2):
-            line = pair_of_lines(line_ref.at[slot], z, size)
-            block = line * jnp.concatenate([along_x, along_x], axis=0)
-            planes[slot][pl.ds(z * HIGHS, 2 * HIGHS), :] = block.astype(jnp.bfloat16)
-        along_y = masses * factors(place_y, centers_of(size))[0]
+            line = pair_of_lines(line_ref.at[slot], z, size).astype(jnp.bfloat16)
+            planes[slot][pl.ds(z * HIGHS, 2 * HIGHS), :] = line * doubled
+        along_y = (masses * factors(place_y, centers_of(size))[0]).astype(jnp.bfloat16)
         near = jnp.clip(place_x, -SPAN, SPAN)
+        lows = row_number(STEP, size).astype(jnp.float32) + LOWS[0]
+        fine_ref[slot] = jnp.exp2((2.0 * rate) * lows * near)
         for low in range(STEP):
-            fine = jnp.exp2((2.0 * rate * LOWS[low]) * near)
-            weights[slot][pl.ds(low * EDGE, EDGE), :] = (along_y * fine).astype(jnp.bfloat16)
+            fine = jnp.broadcast_to(fine_ref[slot, pl.ds(low, 1), :], (EDGE, size))
+            weights[slot][pl.ds(low * EDGE, EDGE), :] = along_y * fine.astype(jnp.bfloat16)
 
     def use(slot, chunk):
         width = min(WIDTH, size)
@@ -258,7 +262,7 @@
             atoms = pl.ds(part * width, width)
             sum_ref[...] += against_rows(planes[slot][:, atoms], weights[slot][:, atoms])
 
-    pipeline(place_ref.shape[1] * LANES // size, build, use)
+    pipeline(place_ref.shape[1] * LANES // size, build, use, last_apart=False)
     total = sum_ref[...].T
     blocks = []
     for low in range(STEP):
@@ -459,6 +463,7 @@
             plane,
             weight,
             weight,
+            ((2, STEP, size), jnp.float32),
             ((EDGE * HIGHS, EDGE * STEP), jnp.float32),
         ],
         2**29,

time: 96.7 us -> 96.7 us (level)
  no operation moved by 1% of the time
where the time goes in v14:
time: 96.7 us; the launch traced here: 96.3 us
  blocking collectives  42.1 us (44%)
  starting transfers between devices  22.4 us (23%)
  Pallas kernels  18.3 us (19%)
  waiting for transfers between devices  11.5 us (12%)
  other arithmetic  1 us (1%)
    all_to_all x3, blocking collectives, exchange(): return lax.all_to_all(values, axes, split_axis=0, concat_axis=0, tiled=True)  42.1 us
    all_to_all x2, starting transfers between devices, exchange(): return lax.all_to_all(values, axes, split_axis=0, concat_axis=0, tiled=True)  22.4 us
    pallas_call x5, Pallas kernels, call(): pl.pallas_call(kernel, out_shape=out_shape, in_specs=[pl.BlockSpec(memory...  18.3 us
    all_to_all x2, waiting for transfers between devices, exchange(): return lax.all_to_all(values, axes, split_axis=0, concat_axis=0, tiled=True)  11.5 us
  transfers between devices with their start and end apart: 2, of which 2 were waited for; matrix products, arithmetic and copies ran while one was open for 1% of the time, Pallas kernels for 5%

profile of v14, /device:TPU:1, one launch (start us, length us, event | category | flops | bytes accessed | tf_op | source)
XLA Modules:
  0.0 96.3 jit_solution(5006468406565788454)
XLA Ops:
  0.6 0.0 copy-start.2
  0.6 2.8 %pack.1 = (s16[256,128]{1,0:T(8,128)(2,1)}, bf16[2,32,128]{2,1,0:T(8,128)(2,1)}) custom-call(s32[4,32]{1,0:T(4,128)} %bitcast.27, s32[3,4,32]{2,1,0:T(4,128)} %bitcast.25, f32[1,256]{1,0:T(1,128)} %bitcast.28, f32[3,1024]{1,0:T(4,128)} %refs_3_.1, f32[8,128]{1,0:T(8,128)} %bitcast.26, bf16[3,256,1024]{2,1,0:T(8,128)(2,1)} %bitcast.21), custom_call_target="tpu_custom_call" | custom-call | flops 67108864 | bytes 1048576 | tf_op jit(solution)/shard_map/pack/pallas_call | solution.py:396
  3.5 18.4 %all-to-all-start = ((s16[128,2,128]{2,1,0:T(2,128)(2,1)}), s16[128,2,128]{2,1,0:T(2,128)(2,1)S(1)}, u32[]{:S(2)}, u32[]{:S(2)}) async-start(s16[128,2,128]{2,1,0:T(2,128)(2,1)} %bitcast.5), calls=%async_computation | async-start | bytes 131072 | tf_op jit(solution)/shard_map/all_to_all | solution.py:522
  21.9 0.0 copy-done.2
  21.9 0.4 reduce
  22.3 0.2 reshape.41
  22.5 0.1 copy.19.target_ref
  22.6 10.8 %all-to-all-done = s16[128,2,128]{2,1,0:T(2,128)(2,1)S(1)} async-done(((s16[128,2,128]{2,1,0:T(2,128)(2,1)}), s16[128,2,128]{2,1,0:T(2,128)(2,1)S(1)}, u32[]{:S(2)}, u32[]{:S(2)}) %all-to-all-start) | async-done | bytes 65568 | tf_op jit(solution)/shard_map/all_to_all | solution.py:522
  33.4 4.0 %splat.1 = s16[4,272,128]{2,1,0:T(8,128)(2,1)} custom-call(s16[256,128]{1,0:T(8,128)(2,1)S(1)} %bitcast.18), custom_call_target="tpu_custom_call" | custom-call | flops 536870912 | bytes 1048576 | tf_op jit(solution)/shard_map/splat/pallas_call | solution.py:396
  37.4 4.0 %all-to-all-start.1 = ((s16[4,272,128]{2,1,0:T(8,128)(2,1)}), s16[4,272,128]{2,1,0:T(8,128)(2,1)S(1)}, u32[]{:S(2)}, u32[]{:S(2)}) async-start(s16[4,272,128]{2,1,0:T(8,128)(2,1)} %splat.1), calls=%async_computation.1 | async-start | bytes 557056 | tf_op jit(solution)/shard_map/all_to_all | solution.py:522
  41.4 5.1 %pull_map.1 = (f32[3,64,128]{2,1,0:T(8,128)S(1)}, f32[4,64,128]{2,1,0:T(8,128)S(1)}, bf16[16,4,32,512]{3,2,1,0:T(8,128)(2,1)S(1)}) custom-call(s16[256,128]{1,0:T(8,128)(2,1)S(1)} %bitcast.19, bf16[32,1024]{1,0:T(8,128)(2,1)S(1)} %copy.19.target_ref), custom_call_target="tpu_custom_call" | custom-call | flops 4294967296 | bytes 1048576 | tf_op jit(solution)/shard_map/pull_map/pallas_call | solution.py:396
  46.5 0.7 all-to-all-done.1.parts_ref
  47.2 0.0 copy-start
  47.2 0.0 copy-start.1
  47.2 4.5 %pull.1 = bf16[512,128]{1,0:T(8,128)(2,1)S(1)} custom-call(s16[4,272,128]{2,1,0:T(8,128)(2,1)S(1)} %all-to-all-done.1.parts_ref, bf16[32,1024]{1,0:T(8,128)(2,1)S(1)} %copy.19.target_ref, f32[3,64,128]{2,1,0:T(8,128)S(1)} %get-tuple-element.12.map_ref, f32[4,64,128]{2,1,0:T(8,128)S(1)} %get-tuple-element.13.place_ref, ...), custom_call_target="tpu_custom_call" | custom-call | flops 4294967296 | bytes 1048576 | tf_op jit(solution)/shard_map/pull/pallas_call | solution.py:396
  51.7 19.1 %all_to_all.25 = bf16[128,4,128]{2,1,0:T(4,128)(2,1)S(1)} all-to-all(bf16[128,4,128]{2,1,0:T(4,128)(2,1)S(1)} %bitcast.17), channel_id=1, replica_groups=mesh['y'=8,'z'=8,'core'=2,'seg'=4] {'y','z','core'}, dimensions={0} | all-to-all | bytes 262144 | tf_op jit(solution)/shard_map/all_to_all | solution.py:522
  70.8 0.0 copy-done
  70.8 0.0 copy-done.1
  70.8 1.9 %finish.1 = (f32[3,1024]{1,0:T(4,128)}, f32[32,128]{1,0:T(8,128)S(1)}, f32[1,128]{1,0:T(1,128)}) custom-call(bf16[512,128]{1,0:T(8,128)(2,1)S(1)} %bitcast.16, bf16[2,32,128]{2,1,0:T(8,128)(2,1)S(1)} %copy-done.1, bf16[3,256,1024]{2,1,0:T(8,128)(2,1)S(1)} %bitcast.22), custom_call_target="tpu_custom_call" | custom-call | flops 67108864 | bytes 1048576 | tf_op jit(solution)/shard_map/finish/pallas_call | solution.py:396
  72.7 10.6 %all_to_all.26 = f32[16,2,128]{2,1,0:T(2,128)S(1)} all-to-all(f32[16,2,128]{2,1,0:T(2,128)S(1)} %bitcast.20), channel_id=1, replica_groups=mesh['y'=8,'z'=8,'core'=2,'seg'=4] {'z','core'}, dimensions={0} | all-to-all | bytes 32768 | tf_op jit(solution)/shard_map/all_to_all | solution.py:522
  83.3 12.4 %all_to_all.27 = f32[32,2,128]{2,1,0:T(2,128)S(1)} all-to-all(f32[32,2,128]{2,1,0:T(2,128)S(1)} %broadcast_in_dim.2), channel_id=1, replica_groups=mesh['y'=8,'z'=8,'core'=2,'seg'=4] {'y','seg'}, dimensions={0} | all-to-all | bytes 65536 | tf_op jit(solution)/shard_map/all_to_all | solution.py:522
  95.7 0.6 reduce_sum.19
  (3 shorter events, 0.1 us)
Async XLA Ops:
  0.6 21.3 %copy-start.2 = (bf16[1,32768]{1,0:T(2,128)(2,1)S(1)}, bf16[1,32768]{1,0:T(2,128)(2,1)}, u32[]{:S(2)}) copy-start(bf16[1,32768]{1,0:T(2,128)(2,1)} %param.11) | copy-start | bytes 196612
  3.5 29.9 %all-to-all-start = ((s16[128,2,128]{2,1,0:T(2,128)(2,1)}), s16[128,2,128]{2,1,0:T(2,128)(2,1)S(1)}, u32[]{:S(2)}, u32[]{:S(2)}) async-start(s16[128,2,128]{2,1,0:T(2,128)(2,1)} %bitcast.5), calls=%async_computation | async-start | bytes 131072 | tf_op jit(solution)/shard_map/all_to_all | solution.py:522
  37.4 9.8 %all-to-all-start.1 = ((s16[4,272,128]{2,1,0:T(8,128)(2,1)}), s16[4,272,128]{2,1,0:T(8,128)(2,1)S(1)}, u32[]{:S(2)}, u32[]{:S(2)}) async-start(s16[4,272,128]{2,1,0:T(8,128)(2,1)} %splat.1), calls=%async_computation.1 | async-start | bytes 557056 | tf_op jit(solution)/shard_map/all_to_all | solution.py:522
  47.2 23.6 %copy-start = (bf16[256,3,1024]{2,0,1:T(8,128)(2,1)S(1)}, bf16[256,3,1024]{2,0,1:T(8,128)(2,1)}, u32[]{:S(2)}) copy-start(bf16[256,3,1024]{2,0,1:T(8,128)(2,1)} %param.9) | copy-start | bytes 4718596
  47.2 23.6 %copy-start.1 = (bf16[2,32,128]{2,1,0:T(8,128)(2,1)S(1)}, bf16[2,32,128]{2,1,0:T(8,128)(2,1)}, u32[]{:S(2)}) copy-start(bf16[2,32,128]{2,1,0:T(8,128)(2,1)} %get-tuple-element.15.refs_1_) | copy-start | bytes 49156

commit v15 on v14

--- a/solution.py
+++ b/solution.py
@@ -260,10 +260,10 @@
         width = min(WIDTH, size)
         for part in range(size // width):
             atoms = pl.ds(part * width, width)
-            sum_ref[...] += against_rows(planes[slot][:, atoms], weights[slot][:, atoms])
+            sum_ref[part] += against_rows(planes[slot][:, atoms], weights[slot][:, atoms])
 
     pipeline(place_ref.shape[1] * LANES // size, build, use, last_apart=False)
-    total = sum_ref[...].T
+    total = jnp.sum(sum_ref[...], axis=0).T
     blocks = []
     for low in range(STEP):
         block = total[low * EDGE : (low + 1) * EDGE] * own_factor(low, EDGE * HIGHS)
@@ -464,7 +464,7 @@
             weight,
             weight,
             ((2, STEP, size), jnp.float32),
-            ((EDGE * HIGHS, EDGE * STEP), jnp.float32),
+            ((size // min(WIDTH, size), EDGE * HIGHS, EDGE * STEP), jnp.float32),
         ],
         2**29,
         got,

time: 96.7 us -> 96.5 us (level)
  no operation moved by 1% of the time
where the time goes in v15:
time: 96.5 us; the launch traced here: 96.1 us
  blocking collectives  42.1 us (44%)
  starting transfers between devices  22.4 us (23%)
  Pallas kernels  18 us (19%)
  waiting for transfers between devices  11.5 us (12%)
  other arithmetic  1 us (1%)
    all_to_all x3, blocking collectives, exchange(): return lax.all_to_all(values, axes, split_axis=0, concat_axis=0, tiled=True)  42.1 us
    all_to_all x2, starting transfers between devices, exchange(): return lax.all_to_all(values, axes, split_axis=0, concat_axis=0, tiled=True)  22.4 us
    pallas_call x5, Pallas kernels, call(): pl.pallas_call(kernel, out_shape=out_shape, in_specs=[pl.BlockSpec(memory...  18 us
    all_to_all x2, waiting for transfers between devices, exchange(): return lax.all_to_all(values, axes, split_axis=0, concat_axis=0, tiled=True)  11.5 us
  transfers between devices with their start and end apart: 2, of which 2 were waited for; matrix products, arithmetic and copies ran while one was open for 1% of the time, Pallas kernels for 5%

profile of v15, /device:TPU:1, one launch (start us, length us, event | category | flops | bytes accessed | tf_op | source)
XLA Modules:
  0.0 96.1 jit_solution(12459761898934777799)
XLA Ops:
  0.6 0.0 copy-start.2
  0.6 2.8 %pack.1 = (s16[256,128]{1,0:T(8,128)(2,1)}, bf16[2,32,128]{2,1,0:T(8,128)(2,1)}) custom-call(s32[4,32]{1,0:T(4,128)} %bitcast.27, s32[3,4,32]{2,1,0:T(4,128)} %bitcast.25, f32[1,256]{1,0:T(1,128)} %bitcast.28, f32[3,1024]{1,0:T(4,128)} %refs_3_.1, f32[8,128]{1,0:T(8,128)} %bitcast.26, bf16[3,256,1024]{2,1,0:T(8,128)(2,1)} %bitcast.21), custom_call_target="tpu_custom_call" | custom-call | flops 67108864 | bytes 1048576 | tf_op jit(solution)/shard_map/pack/pallas_call | solution.py:396
  3.5 18.4 %all-to-all-start = ((s16[128,2,128]{2,1,0:T(2,128)(2,1)}), s16[128,2,128]{2,1,0:T(2,128)(2,1)S(1)}, u32[]{:S(2)}, u32[]{:S(2)}) async-start(s16[128,2,128]{2,1,0:T(2,128)(2,1)} %bitcast.5), calls=%async_computation | async-start | bytes 131072 | tf_op jit(solution)/shard_map/all_to_all | solution.py:522
  21.9 0.0 copy-done.2
  21.9 0.4 reduce
  22.3 0.2 reshape.41
  22.5 0.1 copy.19.target_ref
  22.6 10.8 %all-to-all-done = s16[128,2,128]{2,1,0:T(2,128)(2,1)S(1)} async-done(((s16[128,2,128]{2,1,0:T(2,128)(2,1)}), s16[128,2,128]{2,1,0:T(2,128)(2,1)S(1)}, u32[]{:S(2)}, u32[]{:S(2)}) %all-to-all-start) | async-done | bytes 65568 | tf_op jit(solution)/shard_map/all_to_all | solution.py:522
  33.4 3.7 %splat.1 = s16[4,272,128]{2,1,0:T(8,128)(2,1)} custom-call(s16[256,128]{1,0:T(8,128)(2,1)S(1)} %bitcast.18), custom_call_target="tpu_custom_call" | custom-call | flops 536870912 | bytes 1048576 | tf_op jit(solution)/shard_map/splat/pallas_call | solution.py:396
  37.2 4.0 %all-to-all-start.1 = ((s16[4,272,128]{2,1,0:T(8,128)(2,1)}), s16[4,272,128]{2,1,0:T(8,128)(2,1)S(1)}, u32[]{:S(2)}, u32[]{:S(2)}) async-start(s16[4,272,128]{2,1,0:T(8,128)(2,1)} %splat.1), calls=%async_computation.1 | async-start | bytes 557056 | tf_op jit(solution)/shard_map/all_to_all | solution.py:522
  41.2 5.1 %pull_map.1 = (f32[3,64,128]{2,1,0:T(8,128)S(1)}, f32[4,64,128]{2,1,0:T(8,128)S(1)}, bf16[16,4,32,512]{3,2,1,0:T(8,128)(2,1)S(1)}) custom-call(s16[256,128]{1,0:T(8,128)(2,1)S(1)} %bitcast.19, bf16[32,1024]{1,0:T(8,128)(2,1)S(1)} %copy.19.target_ref), custom_call_target="tpu_custom_call" | custom-call | flops 4294967296 | bytes 1048576 | tf_op jit(solution)/shard_map/pull_map/pallas_call | solution.py:396
  46.2 0.7 all-to-all-done.1.parts_ref
  47.0 0.0 copy-start
  47.0 0.0 copy-start.1
  47.0 4.5 %pull.1 = bf16[512,128]{1,0:T(8,128)(2,1)S(1)} custom-call(s16[4,272,128]{2,1,0:T(8,128)(2,1)S(1)} %all-to-all-done.1.parts_ref, bf16[32,1024]{1,0:T(8,128)(2,1)S(1)} %copy.19.target_ref, f32[3,64,128]{2,1,0:T(8,128)S(1)} %get-tuple-element.12.map_ref, f32[4,64,128]{2,1,0:T(8,128)S(1)} %get-tuple-element.13.place_ref, ...), custom_call_target="tpu_custom_call" | custom-call | flops 4294967296 | bytes 1048576 | tf_op jit(solution)/shard_map/pull/pallas_call | solution.py:396
  51.5 19.1 %all_to_all.25 = bf16[128,4,128]{2,1,0:T(4,128)(2,1)S(1)} all-to-all(bf16[128,4,128]{2,1,0:T(4,128)(2,1)S(1)} %bitcast.17), channel_id=1, replica_groups=mesh['y'=8,'z'=8,'core'=2,'seg'=4] {'y','z','core'}, dimensions={0} | all-to-all | bytes 262144 | tf_op jit(solution)/shard_map/all_to_all | solution.py:522
  70.6 0.0 copy-done
  70.6 0.0 copy-done.1
  70.6 1.9 %finish.1 = (f32[3,1024]{1,0:T(4,128)}, f32[32,128]{1,0:T(8,128)S(1)}, f32[1,128]{1,0:T(1,128)}) custom-call(bf16[512,128]{1,0:T(8,128)(2,1)S(1)} %bitcast.16, bf16[2,32,128]{2,1,0:T(8,128)(2,1)S(1)} %copy-done.1, bf16[3,256,1024]{2,1,0:T(8,128)(2,1)S(1)} %bitcast.22), custom_call_target="tpu_custom_call" | custom-call | flops 67108864 | bytes 1048576 | tf_op jit(solution)/shard_map/finish/pallas_call | solution.py:396
  72.5 10.6 %all_to_all.26 = f32[16,2,128]{2,1,0:T(2,128)S(1)} all-to-all(f32[16,2,128]{2,1,0:T(2,128)S(1)} %bitcast.20), channel_id=1, replica_groups=mesh['y'=8,'z'=8,'core'=2,'seg'=4] {'z','core'}, dimensions={0} | all-to-all | bytes 32768 | tf_op jit(solution)/shard_map/all_to_all | solution.py:522
  83.1 12.4 %all_to_all.27 = f32[32,2,128]{2,1,0:T(2,128)S(1)} all-to-all(f32[32,2,128]{2,1,0:T(2,128)S(1)} %broadcast_in_dim.2), channel_id=1, replica_groups=mesh['y'=8,'z'=8,'core'=2,'seg'=4] {'y','seg'}, dimensions={0} | all-to-all | bytes 65536 | tf_op jit(solution)/shard_map/all_to_all | solution.py:522
  95.5 0.6 reduce_sum.19
  (3 shorter events, 0.1 us)
Async XLA Ops:
  0.6 21.3 %copy-start.2 = (bf16[1,32768]{1,0:T(2,128)(2,1)S(1)}, bf16[1,32768]{1,0:T(2,128)(2,1)}, u32[]{:S(2)}) copy-start(bf16[1,32768]{1,0:T(2,128)(2,1)} %param.11) | copy-start | bytes 196612
  3.5 29.9 %all-to-all-start = ((s16[128,2,128]{2,1,0:T(2,128)(2,1)}), s16[128,2,128]{2,1,0:T(2,128)(2,1)S(1)}, u32[]{:S(2)}, u32[]{:S(2)}) async-start(s16[128,2,128]{2,1,0:T(2,128)(2,1)} %bitcast.5), calls=%async_computation | async-start | bytes 131072 | tf_op jit(solution)/shard_map/all_to_all | solution.py:522
  37.2 9.8 %all-to-all-start.1 = ((s16[4,272,128]{2,1,0:T(8,128)(2,1)}), s16[4,272,128]{2,1,0:T(8,128)(2,1)S(1)}, u32[]{:S(2)}, u32[]{:S(2)}) async-start(s16[4,272,128]{2,1,0:T(8,128)(2,1)} %splat.1), calls=%async_computation.1 | async-start | bytes 557056 | tf_op jit(solution)/shard_map/all_to_all | solution.py:522
  47.0 23.6 %copy-start = (bf16[256,3,1024]{2,0,1:T(8,128)(2,1)S(1)}, bf16[256,3,1024]{2,0,1:T(8,128)(2,1)}, u32[]{:S(2)}) copy-start(bf16[256,3,1024]{2,0,1:T(8,128)(2,1)} %param.9) | copy-start | bytes 4718596
  47.0 23.6 %copy-start.1 = (bf16[2,32,128]{2,1,0:T(8,128)(2,1)S(1)}, bf16[2,32,128]{2,1,0:T(8,128)(2,1)}, u32[]{:S(2)}) copy-start(bf16[2,32,128]{2,1,0:T(8,128)(2,1)} %get-tuple-element.15.refs_1_) | copy-start | bytes 49156
